TPU v7x, 128 devices: a whole 4x4x4 slice. The times are simulated.
128 devices in a mesh: expert: 32 (over y, x, core), blk: 4 (over z).
Axes of the slice: x: 4, y: 4, z: 4, core: 2. Of those that a mesh axis runs over, the one named last changes fastest.
Arguments:
- tokens: bfloat16 [8192, 7168], P(('expert', 'blk')), may hold values from -6 to 6
- route_ids: int32 [8192, 8], P(('expert', 'blk')), may hold values from 0 to 31, all different within a row; in each aligned block of 64 rows (0 to 63, 64 to 127, ...) at most 20 rows name the same one
- route_gates: float32 [8192, 8], P(('expert', 'blk')), may hold values from 0.2 to 1
- gate_weight: bfloat16 [32, 1024, 7168], P('expert', 'blk'), may hold values from -0.0625 to 0.0625
- up_weight: bfloat16 [32, 1024, 7168], P('expert', 'blk'), may hold values from -0.0625 to 0.0625
- down_weight: bfloat16 [32, 1024, 7168], P('expert', 'blk'), may hold values from -0.1875 to 0.1875
Outputs:
- mixed: bfloat16 [8192, 7168], P(('expert', 'blk'))
Inputs may be any that keep to these rules, and one draw needn't show every extreme that they name: `route_ids`: each row names 8 different experts. Within the 64 rows of one device no expert is named by more than 20 rows, a bound that some block reaches.
All inputs are finite; a program needn't handle non-finite values.
Results may differ from a plain program's by a relative error of at most 0.011.
Values may be sent and summed in bfloat16 or wider, within the bound.
No kernel may reach another device: no remote copies, remote signals or barrier semaphores. Data moves between devices by JAX's collectives and lax.ppermute only.
A program may use at most 256 MiB of HBM per device.

v0:
```python
import functools

import jax
import jax.numpy as jnp
from jax import lax
from jax.experimental import pallas as pl
from jax.experimental.pallas import tpu as pltpu
from jax.sharding import Mesh, PartitionSpec as P

EXP = ("y", "x", "c")
COL = ("c", "zh", "zl")
ALL = ("y", "x", "c", "zh", "zl")


def swaps(*pairs):
    return [way for a, b in pairs for way in ((a, b), (b, a))]


PAIR = swaps((0, 3), (1, 2))
NEXT = swaps((0, 1), (6, 7), (4, 3), (5, 2))
FAR = swaps((5, 3), (4, 2))
SIBLING = swaps((0, 4), (1, 5), (2, 6), (3, 7))
FROM_HOME = [(0, 4), (1, 5), (6, 2), (7, 3)]
TO_HOME = [(b, a) for a, b in FROM_HOME]
STEPS = (1792, 2688, 2688)
QUARTER = 256
MAIN = 512
REST = 128
TILE = 896
DEEP = 1792


def along(value, pairs):
    return lax.ppermute(value, COL, pairs)


def after(value, *earlier):
    return lax.optimization_barrier((value, *earlier))[0]


def spread(own, before):
    near_before, far_before = before
    near = along(after(own, *near_before), NEXT)
    far = along(after(own, *far_before), FAR)
    panels = (own, along(own, FROM_HOME), near, along(near, SIBLING), along(far, TO_HOME), far)
    return panels, ((near,), (far,))


def pick_block(flag, wanted, block):
    return jnp.where(flag[0] == wanted, block, 0)


def hidden_kernel(flag, *refs, quarters):
    main, rest = refs[:2]
    panels, out, gate_sum, up_sum = refs[2:-3], refs[-3], refs[-2], refs[-1]
    part = pl.program_id(0)

    @pl.when(part == 0)
    def _():
        gate_sum[...] = jnp.zeros_like(gate_sum)
        up_sum[...] = jnp.zeros_like(up_sum)

    def add(total, place, weights):
        for rows, first, number in ((main, 0, MAIN), (rest, MAIN, REST)):
            total[pl.ds(first, number), pl.ds(place * QUARTER, QUARTER)] += lax.dot_general(
                rows[...], weights, (((1,), (1,)), ((), ())), preferred_element_type=jnp.float32
            )

    at = 0
    for place, kind in enumerate(quarters):
        if kind == 1:
            gate, upper = panels[at][...], panels[at + 1][...]
        else:
            home = flag[0] == 1
            gate = jnp.where(home, panels[at][...], panels[at + 2][...])
            upper = jnp.where(home, panels[at + 1][...], panels[at + 3][...])
        add(gate_sum, place, gate)
        add(up_sum, place, upper)
        at += 2 * kind

    @pl.when(part == pl.num_programs(0) - 1)
    def _():
        gate = gate_sum[...]
        out[...] = (gate / (1.0 + jnp.exp(-gate)) * up_sum[...]).astype(out.dtype)


def hidden_units(flag, main, rest, quarters):
    width = main.shape[1]
    count = len(quarters)
    kinds = tuple(len(quarter) for quarter in quarters)
    specs = [
        pl.BlockSpec((MAIN, DEEP), lambda i, f: (0, i)),
        pl.BlockSpec((REST, DEEP), lambda i, f: (0, i)),
    ]
    operands = [main, rest]
    for quarter in quarters:
        for place, (gate, upper) in enumerate(quarter):
            if len(quarter) == 1:
                spec = pl.BlockSpec((QUARTER, DEEP), lambda i, f: (0, i))
            else:
                spec = pl.BlockSpec(
                    (QUARTER, DEEP), lambda i, f, w=1 - place: (0, pick_block(f, w, i))
                )
            specs += [spec, spec]
            operands += [gate, upper]
    rows = MAIN + REST
    return pl.pallas_call(
        functools.partial(hidden_kernel, quarters=kinds),
        grid_spec=pltpu.PrefetchScalarGridSpec(
            num_scalar_prefetch=1,
            grid=(width // DEEP,),
            in_specs=specs,
            out_specs=pl.BlockSpec((rows, count * QUARTER), lambda i, f: (0, 0)),
            scratch_shapes=[pltpu.VMEM((rows, count * QUARTER), jnp.float32)] * 2,
        ),
        out_shape=jax.ShapeDtypeStruct((rows, count * QUARTER), jnp.bfloat16),
        compiler_params=pltpu.CompilerParams(vmem_limit_bytes=48 * 2**20),
        cost_estimate=pl.CostEstimate(
            flops=4 * rows * width * count * QUARTER,
            bytes_accessed=2 * width * (rows + 2 * count * QUARTER),
            transcendentals=rows * count * QUARTER,
        ),
    )(flag, *operands)


def down_kernel(flag, first, last, own, copied, near, across, brought, far, out_main, out_rest):
    home = flag[0] == 1
    panels = (
        (first[:, :QUARTER], jnp.where(home, own[...], copied[...])),
        (first[:, QUARTER : 2 * QUARTER], near[...]),
        (first[:, 2 * QUARTER :], across[...]),
        (last[...], jnp.where(home, brought[...], far[...])),
    )
    total = None
    for hidden, weights in panels:
        term = jnp.dot(hidden, weights, preferred_element_type=jnp.float32)
        total = term if total is None else total + term
    total = total.astype(out_main.dtype)
    out_main[...] = total[:MAIN]
    out_rest[...] = total[MAIN:]


def down_rows(flag, first, last, panels):
    step = panels[0].shape[1]
    rows = MAIN + REST

    def panel(wanted=None):
        if wanted is None:
            return pl.BlockSpec((QUARTER, TILE), lambda i, f: (0, i))
        return pl.BlockSpec((QUARTER, TILE), lambda i, f: (0, pick_block(f, wanted, i)))

    return pl.pallas_call(
        down_kernel,
        grid_spec=pltpu.PrefetchScalarGridSpec(
            num_scalar_prefetch=1,
            grid=(step // TILE,),
            in_specs=[
                pl.BlockSpec(first.shape, lambda i, f: (0, 0)),
                pl.BlockSpec(last.shape, lambda i, f: (0, 0)),
                panel(1),
                panel(0),
                panel(),
                panel(),
                panel(1),
                panel(0),
            ],
            out_specs=[
                pl.BlockSpec((MAIN, TILE), lambda i, f: (0, i)),
                pl.BlockSpec((REST, TILE), lambda i, f: (0, i)),
            ],
        ),
        out_shape=[
            jax.ShapeDtypeStruct((MAIN, step), jnp.bfloat16),
            jax.ShapeDtypeStruct((REST, step), jnp.bfloat16),
        ],
        compiler_params=pltpu.CompilerParams(vmem_limit_bytes=32 * 2**20),
        cost_estimate=pl.CostEstimate(
            flops=8 * rows * QUARTER * step,
            bytes_accessed=2 * (4 * QUARTER * step + rows * (4 * QUARTER + step)),
            transcendentals=0,
        ),
    )(flag, first, last, *panels)


def pair_exchange(value):
    return lax.ppermute(value, ("zh", "zl"), PAIR)


def body(tokens, route_ids, route_gates, gate_weight, up_weight, down_weight):
    tok_rows, width = tokens.shape
    chips = lax.axis_size("y") * lax.axis_size("x")
    side = lax.axis_index("zh")
    flag = (lax.axis_index("c") == side).astype(jnp.int32).reshape(1)

    routes = jnp.concatenate([route_ids.astype(jnp.float32), route_gates], axis=1)
    routes = jnp.concatenate([routes, pair_exchange(routes)], axis=0)
    both = jnp.concatenate([tokens, pair_exchange(tokens)], axis=0)

    gates, order = spread(gate_weight[0], ((), ()))
    uppers, order = spread(up_weight[0], order)
    downs, at = [], 0
    for step in STEPS:
        panels, order = spread(down_weight[0][:, at : at + step], order)
        downs.append(panels)
        at += step

    top = route_ids.shape[1]
    hosted = (2 * jnp.arange(chips, dtype=jnp.int32) + side).astype(jnp.float32)
    match = (routes[:, :top, None] == hosted[None, None, :]).astype(jnp.float32)
    named = jnp.sum(match, axis=1)
    weight = jnp.sum(routes[:, top:, None] * match, axis=1)
    count = 2 * tok_rows
    place = jnp.arange(count)
    earlier = (place[:, None] > place[None, :]).astype(jnp.bfloat16)
    rank = jnp.dot(earlier, named.astype(jnp.bfloat16), preferred_element_type=jnp.float32)
    on_slot = (rank[:, :, None] == jnp.arange(40, dtype=jnp.float32)) & (named[:, :, None] > 0)
    pick = jnp.transpose(on_slot, (1, 2, 0)).astype(jnp.bfloat16)
    mix = jnp.where(on_slot, weight[:, :, None], 0.0)

    def rows_of(part):
        flat = part.reshape(-1, count)
        return jnp.dot(flat, both, preferred_element_type=jnp.float32).astype(jnp.bfloat16)

    def halves(part):
        part = part.reshape(count, -1)
        high = lax.reduce_precision(part, 8, 7)
        return jnp.concatenate([high, part - high], axis=0).astype(jnp.bfloat16)

    mix_main, mix_rest = halves(mix[:, :, :32]), halves(mix[:, :, 32:])

    def exchange(main, rest):
        columns = main.shape[-1]
        got = lax.all_to_all(main.reshape(2 * chips, 16, columns), EXP, 0, 0, tiled=True)
        got_rest = lax.all_to_all(rest.reshape(chips, 8, columns), ("y", "x"), 0, 0, tiled=True)
        return got.reshape(-1, columns), got_rest.reshape(-1, columns)

    main, rest = exchange(rows_of(pick[:, :32]), rows_of(pick[:, 32:]))
    pairs = list(zip(gates, uppers, strict=True))
    first = hidden_units(flag, main, rest, [pairs[:2], pairs[2:3], pairs[3:4]])
    last = hidden_units(flag, main, rest, [pairs[4:]])
    outs = []
    for panels in downs:
        back, back_rest = exchange(*down_rows(flag, first, last, panels))
        sums = jnp.dot(mix_main, back, preferred_element_type=jnp.float32) + jnp.dot(
            mix_rest, back_rest, preferred_element_type=jnp.float32
        )
        sums = sums[:count] + sums[count:]
        share = pair_exchange(sums[tok_rows:].astype(jnp.bfloat16))
        outs.append((sums[:tok_rows] + share.astype(jnp.float32)).astype(jnp.bfloat16))
    return jnp.concatenate(outs, axis=1)


def solution(mesh):
    fine = Mesh(mesh.devices.reshape(4, 4, 2, 2, 2), ALL)
    rows = P(ALL, None)
    panels = P(EXP, ("zh", "zl"), None)
    return jax.shard_map(
        body,
        mesh=fine,
        in_specs=(rows, rows, rows, panels, panels, panels),
        out_specs=rows,
        check_vma=False,
    )
```

profile of v0, /device:TPU:0, one launch (start us, length us, event | category | flops | bytes accessed | tf_op | source)
XLA Modules:
  0.0 477.9 jit_solution(17643169877089401476)
XLA Ops:
  0.0 2.0 collective-permute-start.4
  2.0 2.5 collective-permute-start.8
  5.9 3.7 collective-permute-start
  10.9 83.6 %collective-permute-done = f32[64,16]{0,1:T(8,128)S(1)} collective-permute-done((f32[64,16]{0,1:T(8,128)S(1)}, f32[64,16]{0,1:T(8,128)S(1)}, u32[]{:S(2)}, u32[]{:S(2)}) %collective-permute-start) | collective-permute-done | bytes 4128 | tf_op jit(solution)/shard_map/ppermute | solution.py:186
  94.9 9.4 %collective-permute-done.1 = bf16[64,7168]{1,0:T(8,128)(2,1)S(1)} collective-permute-done((bf16[64,7168]{1,0:T(8,128)(2,1)}, bf16[64,7168]{1,0:T(8,128)(2,1)S(1)}, u32[]{:S(2)}, u32[]{:S(2)}) %collective-permute-start.1) | collective-permute-done | bytes 917536 | tf_op jit(solution)/shard_map/ppermute | solution.py:186
  105.7 1.9 fusion
  107.6 7.0 %all-to-all-start.1 = ((bf16[16,8,7168]{2,1,0:T(8,128)(2,1)}), bf16[16,8,7168]{2,1,0:T(8,128)(2,1)S(1)}, u32[]{:S(2)}, u32[]{:S(2)}) async-start(bf16[16,8,7168]{2,1,0:T(8,128)(2,1)} %fusion), calls=%async_computation.1 | async-start | bytes 3670016 | tf_op jit(solution)/shard_map/all_to_all | solution.py:234
  114.6 2.5 collective-permute-start.10
  117.1 6.5 %convolution_convert_fusion = bf16[512,7168]{1,0:T(8,128)(2,1)} fusion(pred[512,128]{1,0:T(32,128)(4,1)S(1)} %bitcast.56, bf16[128,7168]{1,0:T(8,128)(2,1)} %copy-done.13), kind=kOutput, calls=%fused_computation | convolution fusion | flops 943194112 | bytes 9240576 | tf_op jit(solution)/shard_map/dot_general | solution.py:222
  123.7 17.8 %all-to-all-done.1 = bf16[16,8,7168]{2,1,0:T(8,128)(2,1)S(1)} async-done(((bf16[16,8,7168]{2,1,0:T(8,128)(2,1)}), bf16[16,8,7168]{2,1,0:T(8,128)(2,1)S(1)}, u32[]{:S(2)}, u32[]{:S(2)}) %all-to-all-start.1) | async-done | bytes 1835040 | tf_op jit(solution)/shard_map/all_to_all | solution.py:234
  141.4 4.9 %all-to-all-start = ((bf16[32,16,7168]{2,1,0:T(8,128)(2,1)}), bf16[32,16,7168]{2,1,0:T(8,128)(2,1)}, u32[]{:S(2)}, u32[]{:S(2)}) async-start(bf16[32,16,7168]{2,1,0:T(8,128)(2,1)} %bitcast.52), calls=%async_computation | async-start | bytes 14680064 | tf_op jit(solution)/shard_map/all_to_all | solution.py:233
  146.4 2.2 collective-permute-start.3
  153.8 43.1 %collective-permute-done.5.refs_7_ = bf16[256,7168]{1,0:T(8,128)(2,1)} collective-permute-done((bf16[256,7168]{1,0:T(8,128)(2,1)}, bf16[256,7168]{1,0:T(8,128)(2,1)}, u32[]{:S(2)}, u32[]{:S(2)}) %collective-permute-start.5) | collective-permute-done | bytes 3670048 | tf_op jit(solution)/shard_map/ppermute | solution.py:34
  200.6 9.8 %collective-permute-start.2 = (bf16[256,7168]{1,0:T(8,128)(2,1)}, bf16[256,7168]{1,0:T(8,128)(2,1)}, u32[]{:S(2)}, u32[]{:S(2)}) collective-permute-start(bf16[256,7168]{1,0:T(8,128)(2,1)} %bitcast.60), channel_id=1, source_target_pairs={{0,4},{1,5},{6,2},{7,3},{8,12},{9,13},{14,10},{15,11},{16,20},{17,... | collective-permute-start | bytes 11010056 | tf_op jit(solution)/shard_map/ppermute | solution.py:34
  210.4 2.0 collective-permute-done.13.near
  212.4 12.6 %collective-permute-start.6 = (bf16[256,7168]{1,0:T(8,128)(2,1)}, bf16[256,7168]{1,0:T(8,128)(2,1)}, u32[]{:S(2)}, u32[]{:S(2)}) collective-permute-start(bf16[256,7168]{1,0:T(8,128)(2,1)} %collective-permute-done.4.refs_6_), channel_id=1, source_target_pairs={{0,4},{4,0},{1,5},{5,1},{2,6},{6,2},{3,7},{7,3},{8,12},{12,8},{9,1... | collective-permute-start | bytes 11010056 | tf_op jit(solution)/shard_map/ppermute | solution.py:34
  226.9 3.0 fusion.25
  233.5 5.2 %all-to-all-done = bf16[32,16,7168]{2,1,0:T(8,128)(2,1)} async-done(((bf16[32,16,7168]{2,1,0:T(8,128)(2,1)}), bf16[32,16,7168]{2,1,0:T(8,128)(2,1)}, u32[]{:S(2)}, u32[]{:S(2)}) %all-to-all-start) | async-done | bytes 7340064 | tf_op jit(solution)/shard_map/all_to_all | solution.py:233
  238.7 2.0 copy-done.1
  240.7 9.7 %shard_map.65.last = bf16[640,256]{1,0:T(8,128)(2,1)S(1)} custom-call(s32[1]{0:T(128)} %bitcast.1.flag, bf16[512,7168]{1,0:T(8,128)(2,1)} %bitcast.6.refs_0_, bf16[128,7168]{1,0:T(8,128)(2,1)S(1)} %bitcast.49, bf16[256,7168]{1,0:T(8,128)(2,1)S(1)} %copy-done.1, bf16[256,7168]{1,0:T(8,128)(2,1)} %collective-permute-done.11.refs_3_, ...), custom_call_target="tpu_custom_call" | custom-call | flops 4697620480 | bytes 16515072 | tf_op jit(solution)/shard_map/pallas_call | solution.py:107
  250.5 2.5 collective-permute-start.18
  253.1 9.0 %collective-permute-done.19.near = bf16[256,2688]{1,0:T(8,128)(2,1)} collective-permute-done((bf16[256,2688]{1,0:T(8,128)(2,1)}, bf16[256,2688]{1,0:T(8,128)(2,1)}, u32[]{:S(2)}, u32[]{:S(2)}) %collective-permute-start.19) | collective-permute-done | bytes 1376288 | tf_op jit(solution)/shard_map/ppermute | solution.py:34
  263.4 3.8 collective-permute-start.20
  268.7 23.1 %shard_map.64.first = bf16[640,768]{1,0:T(8,128)(2,1)S(1)} custom-call(s32[1]{0:T(128)} %bitcast.1.flag, bf16[512,7168]{1,0:T(8,128)(2,1)} %bitcast.6.refs_0_, bf16[128,7168]{1,0:T(8,128)(2,1)S(1)} %bitcast.50, bf16[256,7168]{1,0:T(8,128)(2,1)} %bitcast.61, bf16[256,7168]{1,0:T(8,128)(2,1)} %bitcast.65, bf16[256,7168]{1,0:T(8,128)(2,1)} %collective-permute-done.2.refs_4_, ...), custom_call_target="tpu_custom_call" | custom-call | flops 14092861440 | bytes 31195136 | tf_op jit(solution)/shard_map/pallas_call | solution.py:107
  291.8 4.5 shard_map.66
  296.4 6.8 %all-to-all-start.3 = ((bf16[16,8,1792]{2,1,0:T(8,128)(2,1)}), bf16[16,8,1792]{2,1,0:T(8,128)(2,1)}, u32[]{:S(2)}, u32[]{:S(2)}) async-start(bf16[16,8,1792]{2,1,0:T(8,128)(2,1)} %bitcast.16), calls=%async_computation.3 | async-start | bytes 917504 | tf_op jit(solution)/shard_map/all_to_all | solution.py:234
  304.4 7.5 %shard_map.67 = (bf16[512,2688]{1,0:T(8,128)(2,1)}, bf16[128,2688]{1,0:T(8,128)(2,1)S(1)}) custom-call(s32[1]{0:T(128)} %bitcast.1.flag, bf16[640,768]{1,0:T(8,128)(2,1)S(1)} %copy-done.11, bf16[640,256]{1,0:T(8,128)(2,1)S(1)} %shard_map.65.last, bf16[256,2688]{1,0:T(8,128)(2,1)} %get-tuple-element.26.own, bf16[256,2688]{1,0:T(8,128)(2,1)} %collective-permute-done.18.copied, ...), custom_call_target="tpu_custom_call" | custom-call | flops 3523215360 | bytes 10256384 | tf_op jit(solution)/shard_map/pallas_call | solution.py:152
  311.9 2.8 all-to-all-done.3
  314.7 18.8 %all_to_all.40 = bf16[16,8,2688]{2,1,0:T(8,128)(2,1)} all-to-all(bf16[16,8,2688]{2,1,0:T(8,128)(2,1)S(1)} %bitcast.51), channel_id=1, replica_groups=mesh['y'=4,'x'=4,'c'=2,'zh'=2,'zl'=2] {'y','x'}, dimensions={0} | all-to-all | bytes 1376256 | tf_op jit(solution)/shard_map/all_to_all | solution.py:234
  333.5 4.7 all-to-all-start.2
  340.1 25.1 %all-to-all-done.2 = bf16[32,16,1792]{2,1,0:T(8,128)(2,1)} async-done(((bf16[32,16,1792]{2,1,0:T(8,128)(2,1)}), bf16[32,16,1792]{2,1,0:T(8,128)(2,1)}, u32[]{:S(2)}, u32[]{:S(2)}) %all-to-all-start.2) | async-done | bytes 1835040 | tf_op jit(solution)/shard_map/all_to_all | solution.py:233
  365.1 4.9 %all-to-all-start.4 = ((bf16[32,16,2688]{2,1,0:T(8,128)(2,1)}), bf16[32,16,2688]{2,1,0:T(8,128)(2,1)}, u32[]{:S(2)}, u32[]{:S(2)}) async-start(bf16[32,16,2688]{2,1,0:T(8,128)(2,1)} %bitcast.18), calls=%async_computation.4 | async-start | bytes 5505024 | tf_op jit(solution)/shard_map/all_to_all | solution.py:233
  370.1 2.1 collective-permute-start.24
  374.8 2.0 collective-permute-done.26.across
  378.8 7.0 %shard_map.68 = (bf16[512,2688]{1,0:T(8,128)(2,1)}, bf16[128,2688]{1,0:T(8,128)(2,1)}) custom-call(s32[1]{0:T(128)} %bitcast.1.flag, bf16[640,768]{1,0:T(8,128)(2,1)S(1)} %copy-done.12, bf16[640,256]{1,0:T(8,128)(2,1)S(1)} %shard_map.65.last, bf16[256,2688]{1,0:T(8,128)(2,1)S(1)} %get-tuple-element.30.own, ...), custom_call_target="tpu_custom_call" | custom-call | flops 3523215360 | bytes 10256384 | tf_op jit(solution)/shard_map/pallas_call | solution.py:152
  385.8 21.8 %all-to-all-done.4 = bf16[32,16,2688]{2,1,0:T(8,128)(2,1)} async-done(((bf16[32,16,2688]{2,1,0:T(8,128)(2,1)}), bf16[32,16,2688]{2,1,0:T(8,128)(2,1)}, u32[]{:S(2)}, u32[]{:S(2)}) %all-to-all-start.4) | async-done | bytes 2752544 | tf_op jit(solution)/shard_map/all_to_all | solution.py:233
  407.6 4.1 all-to-all-start.6
  412.5 2.2 fusion.13
  416.5 8.9 %collective-permute-done.17 = bf16[64,1792]{1,0:T(8,128)(2,1)S(1)} collective-permute-done((bf16[64,1792]{1,0:T(8,128)(2,1)S(1)}, bf16[64,1792]{1,0:T(8,128)(2,1)S(1)}, u32[]{:S(2)}, u32[]{:S(2)}) %collective-permute-start.17) | collective-permute-done | bytes 229408 | tf_op jit(solution)/shard_map/ppermute | solution.py:186
  426.2 2.8 fusion.12
  429.0 2.1 convolution_add_fusion.1
  431.0 18.1 %all-to-all-done.6 = bf16[32,16,2688]{2,1,0:T(8,128)(2,1)S(1)} async-done(((bf16[32,16,2688]{2,1,0:T(8,128)(2,1)}), bf16[32,16,2688]{2,1,0:T(8,128)(2,1)S(1)}, u32[]{:S(2)}, u32[]{:S(2)}) %all-to-all-start.6) | async-done | bytes 2752544 | tf_op jit(solution)/shard_map/all_to_all | solution.py:233
  449.1 3.6 all-to-all-start.7
  452.7 1.9 slice_add_fusion.1
  456.5 2.5 fusion.11
  459.0 6.1 %all-to-all-done.7 = bf16[16,8,2688]{2,1,0:T(8,128)(2,1)S(1)} async-done(((bf16[16,8,2688]{2,1,0:T(8,128)(2,1)}), bf16[16,8,2688]{2,1,0:T(8,128)(2,1)S(1)}, u32[]{:S(2)}, u32[]{:S(2)}) %all-to-all-start.7) | async-done | bytes 688160 | tf_op jit(solution)/shard_map/all_to_all | solution.py:234
  465.1 2.3 convolution_add_fusion
  469.9 6.9 %collective-permute-done.29 = bf16[64,2688]{1,0:T(8,128)(2,1)S(1)} collective-permute-done((bf16[64,2688]{1,0:T(8,128)(2,1)S(1)}, bf16[64,2688]{1,0:T(8,128)(2,1)S(1)}, u32[]{:S(2)}, u32[]{:S(2)}) %collective-permute-start.29) | collective-permute-done | bytes 344096 | tf_op jit(solution)/shard_map/ppermute | solution.py:186
  (123 shorter events, 37.8 us)
Async XLA Ops:
  0.0 94.5 %copy-start.25 = (f32[64,8]{0,1:T(8,128)S(1)}, f32[64,8]{0,1:T(8,128)}, u32[]{:S(2)}) copy-start(f32[64,8]{0,1:T(8,128)} %param.8) | copy-start | bytes 6148
  0.0 117.1 %collective-permute-start.4 = (bf16[256,7168]{1,0:T(8,128)(2,1)}, bf16[256,7168]{1,0:T(8,128)(2,1)}, u32[]{:S(2)}, u32[]{:S(2)}) collective-permute-start(bf16[256,7168]{1,0:T(8,128)(2,1)} %bitcast.58), channel_id=1, source_target_pairs={{0,1},{1,0},{6,7},{7,6},{4,3},{3,4},{5,2},{2,5},{8,9},{9,8},{14,15... | collective-permute-start | bytes 11010056 | tf_op jit(solution)/shard_map/ppermute | solution.py:34
  2.0 112.6 %collective-permute-start.8 = (bf16[256,7168]{1,0:T(8,128)(2,1)}, bf16[256,7168]{1,0:T(8,128)(2,1)}, u32[]{:S(2)}, u32[]{:S(2)}) collective-permute-start(bf16[256,7168]{1,0:T(8,128)(2,1)} %bitcast.59), channel_id=1, source_target_pairs={{5,3},{3,5},{4,2},{2,4},{13,11},{11,13},{12,10},{10,12},{21,19},{1... | collective-permute-start | bytes 11010056 | tf_op jit(solution)/shard_map/ppermute | solution.py:34
  5.9 88.6 %collective-permute-start = (f32[64,16]{0,1:T(8,128)S(1)}, f32[64,16]{0,1:T(8,128)S(1)}, u32[]{:S(2)}, u32[]{:S(2)}) collective-permute-start(f32[64,16]{0,1:T(8,128)S(1)} %pad_maximum_fusion.9), channel_id=1, source_target_pairs={{0,3},{3,0},{1,2},{2,1},{4,7},{7,4},{5,6},{6,5},{8,11},{11,8},{9,1... | collective-permute-start | bytes 12296 | tf_op jit(solution)/shard_map/ppermute | solution.py:186
  9.6 94.8 %collective-permute-start.1 = (bf16[64,7168]{1,0:T(8,128)(2,1)}, bf16[64,7168]{1,0:T(8,128)(2,1)S(1)}, u32[]{:S(2)}, u32[]{:S(2)}) collective-permute-start(bf16[64,7168]{1,0:T(8,128)(2,1)} %param.6), channel_id=1, source_target_pairs={{0,3},{3,0},{1,2},{2,1},{4,7},{7,4},{5,6},{6,5},{8,11},{11,8},{9,1... | collective-permute-start | bytes 2752520 | tf_op jit(solution)/shard_map/ppermute | solution.py:186
  94.9 12.7 %copy-start.23 = (f32[128,16]{0,1:T(8,128)}, f32[128,16]{0,1:T(8,128)S(1)}, u32[]{:S(2)}) copy-start(f32[128,16]{0,1:T(8,128)S(1)} %fusion.17) | copy-start | bytes 24580
  107.6 33.9 %all-to-all-start.1 = ((bf16[16,8,7168]{2,1,0:T(8,128)(2,1)}), bf16[16,8,7168]{2,1,0:T(8,128)(2,1)S(1)}, u32[]{:S(2)}, u32[]{:S(2)}) async-start(bf16[16,8,7168]{2,1,0:T(8,128)(2,1)} %fusion), calls=%async_computation.1 | async-start | bytes 3670016 | tf_op jit(solution)/shard_map/all_to_all | solution.py:234
  114.6 37.9 %collective-permute-start.10 = (bf16[256,7168]{1,0:T(8,128)(2,1)}, bf16[256,7168]{1,0:T(8,128)(2,1)}, u32[]{:S(2)}, u32[]{:S(2)}) collective-permute-start(bf16[256,7168]{1,0:T(8,128)(2,1)} %bitcast.62), channel_id=1, source_target_pairs={{5,3},{3,5},{4,2},{2,4},{13,11},{11,13},{12,10},{10,12},{21,19},{1... | collective-permute-start | bytes 11010056 | tf_op jit(solution)/shard_map/ppermute | solution.py:34
  117.1 79.9 %collective-permute-start.5 = (bf16[256,7168]{1,0:T(8,128)(2,1)}, bf16[256,7168]{1,0:T(8,128)(2,1)}, u32[]{:S(2)}, u32[]{:S(2)}) collective-permute-start(bf16[256,7168]{1,0:T(8,128)(2,1)} %bitcast.63), channel_id=1, source_target_pairs={{0,1},{1,0},{6,7},{7,6},{4,3},{3,4},{5,2},{2,5},{8,9},{9,8},{14,15... | collective-permute-start | bytes 11010056 | tf_op jit(solution)/shard_map/ppermute | solution.py:34
  141.4 97.2 %all-to-all-start = ((bf16[32,16,7168]{2,1,0:T(8,128)(2,1)}), bf16[32,16,7168]{2,1,0:T(8,128)(2,1)}, u32[]{:S(2)}, u32[]{:S(2)}) async-start(bf16[32,16,7168]{2,1,0:T(8,128)(2,1)} %bitcast.52), calls=%async_computation | async-start | bytes 14680064 | tf_op jit(solution)/shard_map/all_to_all | solution.py:233
  146.4 54.2 %collective-permute-start.3 = (bf16[256,7168]{1,0:T(8,128)(2,1)}, bf16[256,7168]{1,0:T(8,128)(2,1)S(1)}, u32[]{:S(2)}, u32[]{:S(2)}) collective-permute-start(bf16[256,7168]{1,0:T(8,128)(2,1)} %bitcast.64), channel_id=1, source_target_pairs={{0,4},{1,5},{6,2},{7,3},{8,12},{9,13},{14,10},{15,11},{16,20},{17,... | collective-permute-start | bytes 11010056 | tf_op jit(solution)/shard_map/ppermute | solution.py:34
  149.9 48.1 %collective-permute-start.12 = (bf16[256,1792]{1,0:T(8,128)(2,1)S(1)}, bf16[256,1792]{1,0:T(8,128)(2,1)S(1)}, u32[]{:S(2)}, u32[]{:S(2)}) collective-permute-start(bf16[256,1792]{1,0:T(8,128)(2,1)S(1)} %slice.92.own), channel_id=1, source_target_pairs={{0,4},{1,5},{6,2},{7,3},{8,12},{9,13},{14,10},{15,11},{16,20},{17,... | collective-permute-start | bytes 2752520 | tf_op jit(solution)/shard_map/ppermute | solution.py:34
  151.2 78.7 %collective-permute-start.9 = (bf16[256,7168]{1,0:T(8,128)(2,1)}, bf16[256,7168]{1,0:T(8,128)(2,1)S(1)}, u32[]{:S(2)}, u32[]{:S(2)}) collective-permute-start(bf16[256,7168]{1,0:T(8,128)(2,1)} %collective-permute-done.8.refs_4_), channel_id=1, source_target_pairs={{4,0},{5,1},{2,6},{3,7},{12,8},{13,9},{10,14},{11,15},{20,16},{21,... | collective-permute-start | bytes 11010056 | tf_op jit(solution)/shard_map/ppermute | solution.py:34
  152.5 79.2 %collective-permute-start.11 = (bf16[256,7168]{1,0:T(8,128)(2,1)}, bf16[256,7168]{1,0:T(8,128)(2,1)}, u32[]{:S(2)}, u32[]{:S(2)}) collective-permute-start(bf16[256,7168]{1,0:T(8,128)(2,1)} %collective-permute-done.10.refs_5_), channel_id=1, source_target_pairs={{4,0},{5,1},{2,6},{3,7},{12,8},{13,9},{10,14},{11,15},{20,16},{21,... | collective-permute-start | bytes 11010056 | tf_op jit(solution)/shard_map/ppermute | solution.py:34
  197.0 15.4 %collective-permute-start.13 = (bf16[256,1792]{1,0:T(8,128)(2,1)S(1)}, bf16[256,1792]{1,0:T(8,128)(2,1)S(1)}, u32[]{:S(2)}, u32[]{:S(2)}) collective-permute-start(bf16[256,1792]{1,0:T(8,128)(2,1)S(1)} %slice.92.own), channel_id=1, source_target_pairs={{0,1},{1,0},{6,7},{7,6},{4,3},{3,4},{5,2},{2,5},{8,9},{9,8},{14,15... | collective-permute-start | bytes 2752520 | tf_op jit(solution)/shard_map/ppermute | solution.py:34
  199.0 26.1 %collective-permute-start.15 = (bf16[256,1792]{1,0:T(8,128)(2,1)S(1)}, bf16[256,1792]{1,0:T(8,128)(2,1)S(1)}, u32[]{:S(2)}, u32[]{:S(2)}) collective-permute-start(bf16[256,1792]{1,0:T(8,128)(2,1)S(1)} %slice.92.own), channel_id=1, source_target_pairs={{5,3},{3,5},{4,2},{2,4},{13,11},{11,13},{12,10},{10,12},{21,19},{1... | collective-permute-start | bytes 2752520 | tf_op jit(solution)/shard_map/ppermute | solution.py:34
  200.6 24.4 %copy-start.26 = (bf16[256,7168]{1,0:T(8,128)(2,1)}, bf16[256,7168]{1,0:T(8,128)(2,1)S(1)}, u32[]{:S(2)}) copy-start(bf16[256,7168]{1,0:T(8,128)(2,1)S(1)} %collective-permute-done.3.refs_5_) | copy-start | bytes 11010052
  200.6 49.9 %collective-permute-start.2 = (bf16[256,7168]{1,0:T(8,128)(2,1)}, bf16[256,7168]{1,0:T(8,128)(2,1)}, u32[]{:S(2)}, u32[]{:S(2)}) collective-permute-start(bf16[256,7168]{1,0:T(8,128)(2,1)} %bitcast.60), channel_id=1, source_target_pairs={{0,4},{1,5},{6,2},{7,3},{8,12},{9,13},{14,10},{15,11},{16,20},{17,... | collective-permute-start | bytes 11010056 | tf_op jit(solution)/shard_map/ppermute | solution.py:34
  212.4 12.7 %copy-start.6 = (bf16[256,1792]{1,0:T(8,128)(2,1)}, bf16[256,1792]{1,0:T(8,128)(2,1)S(1)}, u32[]{:S(2)}) copy-start(bf16[256,1792]{1,0:T(8,128)(2,1)S(1)} %collective-permute-done.13.near) | copy-start | bytes 2752516
  212.4 40.6 %collective-permute-start.6 = (bf16[256,7168]{1,0:T(8,128)(2,1)}, bf16[256,7168]{1,0:T(8,128)(2,1)}, u32[]{:S(2)}, u32[]{:S(2)}) collective-permute-start(bf16[256,7168]{1,0:T(8,128)(2,1)} %collective-permute-done.4.refs_6_), channel_id=1, source_target_pairs={{0,4},{4,0},{1,5},{5,1},{2,6},{6,2},{3,7},{7,3},{8,12},{12,8},{9,1... | collective-permute-start | bytes 11010056 | tf_op jit(solution)/shard_map/ppermute | solution.py:34
  226.0 41.2 %collective-permute-start.7 = (bf16[256,7168]{1,0:T(8,128)(2,1)}, bf16[256,7168]{1,0:T(8,128)(2,1)}, u32[]{:S(2)}, u32[]{:S(2)}) collective-permute-start(bf16[256,7168]{1,0:T(8,128)(2,1)} %collective-permute-done.5.refs_7_), channel_id=1, source_target_pairs={{0,4},{4,0},{1,5},{5,1},{2,6},{6,2},{3,7},{7,3},{8,12},{12,8},{9,1... | collective-permute-start | bytes 11010056 | tf_op jit(solution)/shard_map/ppermute | solution.py:34
  231.8 30.3 %collective-permute-start.19 = (bf16[256,2688]{1,0:T(8,128)(2,1)}, bf16[256,2688]{1,0:T(8,128)(2,1)}, u32[]{:S(2)}, u32[]{:S(2)}) collective-permute-start(bf16[256,2688]{1,0:T(8,128)(2,1)} %get-tuple-element.26.own), channel_id=1, source_target_pairs={{0,1},{1,0},{6,7},{7,6},{4,3},{3,4},{5,2},{2,5},{8,9},{9,8},{14,15... | collective-permute-start | bytes 4128776 | tf_op jit(solution)/shard_map/ppermute | solution.py:34
  231.8 31.6 %collective-permute-start.21 = (bf16[256,2688]{1,0:T(8,128)(2,1)}, bf16[256,2688]{1,0:T(8,128)(2,1)}, u32[]{:S(2)}, u32[]{:S(2)}) collective-permute-start(bf16[256,2688]{1,0:T(8,128)(2,1)} %get-tuple-element.26.own), channel_id=1, source_target_pairs={{5,3},{3,5},{4,2},{2,4},{13,11},{11,13},{12,10},{10,12},{21,19},{1... | collective-permute-start | bytes 4128776 | tf_op jit(solution)/shard_map/ppermute | solution.py:34
  240.7 12.3 %copy-start.7 = (bf16[256,1792]{1,0:T(8,128)(2,1)S(1)}, bf16[256,1792]{1,0:T(8,128)(2,1)}, u32[]{:S(2)}) copy-start(bf16[256,1792]{1,0:T(8,128)(2,1)} %copy-done.6) | copy-start | bytes 2752516
  240.7 21.4 %copy-start.9 = (bf16[256,1792]{1,0:T(8,128)(2,1)S(1)}, bf16[256,1792]{1,0:T(8,128)(2,1)}, u32[]{:S(2)}) copy-start(bf16[256,1792]{1,0:T(8,128)(2,1)} %copy-done.8) | copy-start | bytes 2752516
  250.5 41.3 %copy-start.3 = (bf16[256,1792]{1,0:T(8,128)(2,1)S(1)}, bf16[256,1792]{1,0:T(8,128)(2,1)}, u32[]{:S(2)}) copy-start(bf16[256,1792]{1,0:T(8,128)(2,1)} %copy-done.2) | copy-start | bytes 2752516
  250.5 41.3 %copy-start.5 = (bf16[256,1792]{1,0:T(8,128)(2,1)S(1)}, bf16[256,1792]{1,0:T(8,128)(2,1)}, u32[]{:S(2)}) copy-start(bf16[256,1792]{1,0:T(8,128)(2,1)} %copy-done.4) | copy-start | bytes 2752516
  250.5 52.7 %collective-permute-start.18 = (bf16[256,2688]{1,0:T(8,128)(2,1)}, bf16[256,2688]{1,0:T(8,128)(2,1)}, u32[]{:S(2)}, u32[]{:S(2)}) collective-permute-start(bf16[256,2688]{1,0:T(8,128)(2,1)} %get-tuple-element.26.own), channel_id=1, source_target_pairs={{0,4},{1,5},{6,2},{7,3},{8,12},{9,13},{14,10},{15,11},{16,20},{17,... | collective-permute-start | bytes 4128776 | tf_op jit(solution)/shard_map/ppermute | solution.py:34
  253.0 38.7 %collective-permute-start.14 = (bf16[256,1792]{1,0:T(8,128)(2,1)S(1)}, bf16[256,1792]{1,0:T(8,128)(2,1)S(1)}, u32[]{:S(2)}, u32[]{:S(2)}) collective-permute-start(bf16[256,1792]{1,0:T(8,128)(2,1)S(1)} %copy-done.7), channel_id=1, source_target_pairs={{0,4},{4,0},{1,5},{5,1},{2,6},{6,2},{3,7},{7,3},{8,12},{12,8},{9,1... | collective-permute-start | bytes 2752520 | tf_op jit(solution)/shard_map/ppermute | solution.py:34
  262.1 29.7 %collective-permute-start.16 = (bf16[256,1792]{1,0:T(8,128)(2,1)S(1)}, bf16[256,1792]{1,0:T(8,128)(2,1)S(1)}, u32[]{:S(2)}, u32[]{:S(2)}) collective-permute-start(bf16[256,1792]{1,0:T(8,128)(2,1)S(1)} %copy-done.9), channel_id=1, source_target_pairs={{4,0},{5,1},{2,6},{3,7},{12,8},{13,9},{10,14},{11,15},{20,16},{21,... | collective-permute-start | bytes 2752520 | tf_op jit(solution)/shard_map/ppermute | solution.py:34
  263.4 39.8 %collective-permute-start.20 = (bf16[256,2688]{1,0:T(8,128)(2,1)}, bf16[256,2688]{1,0:T(8,128)(2,1)}, u32[]{:S(2)}, u32[]{:S(2)}) collective-permute-start(bf16[256,2688]{1,0:T(8,128)(2,1)} %collective-permute-done.19.near), channel_id=1, source_target_pairs={{0,4},{4,0},{1,5},{5,1},{2,6},{6,2},{3,7},{7,3},{8,12},{12,8},{9,1... | collective-permute-start | bytes 4128776 | tf_op jit(solution)/shard_map/ppermute | solution.py:34
  267.2 36.0 %collective-permute-start.22 = (bf16[256,2688]{1,0:T(8,128)(2,1)}, bf16[256,2688]{1,0:T(8,128)(2,1)}, u32[]{:S(2)}, u32[]{:S(2)}) collective-permute-start(bf16[256,2688]{1,0:T(8,128)(2,1)} %collective-permute-done.21.far), channel_id=1, source_target_pairs={{4,0},{5,1},{2,6},{3,7},{12,8},{13,9},{10,14},{11,15},{20,16},{21,... | collective-permute-start | bytes 4128776 | tf_op jit(solution)/shard_map/ppermute | solution.py:34
  296.4 18.3 %all-to-all-start.3 = ((bf16[16,8,1792]{2,1,0:T(8,128)(2,1)}), bf16[16,8,1792]{2,1,0:T(8,128)(2,1)}, u32[]{:S(2)}, u32[]{:S(2)}) async-start(bf16[16,8,1792]{2,1,0:T(8,128)(2,1)} %bitcast.16), calls=%async_computation.3 | async-start | bytes 917504 | tf_op jit(solution)/shard_map/all_to_all | solution.py:234
  333.5 31.6 %all-to-all-start.2 = ((bf16[32,16,1792]{2,1,0:T(8,128)(2,1)}), bf16[32,16,1792]{2,1,0:T(8,128)(2,1)}, u32[]{:S(2)}, u32[]{:S(2)}) async-start(bf16[32,16,1792]{2,1,0:T(8,128)(2,1)} %bitcast.13), calls=%async_computation.2 | async-start | bytes 3670016 | tf_op jit(solution)/shard_map/all_to_all | solution.py:233
  338.2 34.0 %collective-permute-start.25 = (bf16[256,2688]{1,0:T(8,128)(2,1)S(1)}, bf16[256,2688]{1,0:T(8,128)(2,1)S(1)}, u32[]{:S(2)}, u32[]{:S(2)}) collective-permute-start(bf16[256,2688]{1,0:T(8,128)(2,1)S(1)} %get-tuple-element.30.own), channel_id=1, source_target_pairs={{0,1},{1,0},{6,7},{7,6},{4,3},{3,4},{5,2},{2,5},{8,9},{9,8},{14,15... | collective-permute-start | bytes 4128776 | tf_op jit(solution)/shard_map/ppermute | solution.py:34
  338.3 34.0 %collective-permute-start.27 = (bf16[256,2688]{1,0:T(8,128)(2,1)S(1)}, bf16[256,2688]{1,0:T(8,128)(2,1)}, u32[]{:S(2)}, u32[]{:S(2)}) collective-permute-start(bf16[256,2688]{1,0:T(8,128)(2,1)S(1)} %get-tuple-element.30.own), channel_id=1, source_target_pairs={{5,3},{3,5},{4,2},{2,4},{13,11},{11,13},{12,10},{10,12},{21,19},{1... | collective-permute-start | bytes 4128776 | tf_op jit(solution)/shard_map/ppermute | solution.py:34
  365.1 42.4 %all-to-all-start.4 = ((bf16[32,16,2688]{2,1,0:T(8,128)(2,1)}), bf16[32,16,2688]{2,1,0:T(8,128)(2,1)}, u32[]{:S(2)}, u32[]{:S(2)}) async-start(bf16[32,16,2688]{2,1,0:T(8,128)(2,1)} %bitcast.18), calls=%async_computation.4 | async-start | bytes 5505024 | tf_op jit(solution)/shard_map/all_to_all | solution.py:233
  370.1 4.7 collective-permute-start.24
  372.2 4.6 collective-permute-start.26
  372.3 5.3 %collective-permute-start.28 = (bf16[256,2688]{1,0:T(8,128)(2,1)}, bf16[256,2688]{1,0:T(8,128)(2,1)S(1)}, u32[]{:S(2)}, u32[]{:S(2)}) collective-permute-start(bf16[256,2688]{1,0:T(8,128)(2,1)} %collective-permute-done.27.far), channel_id=1, source_target_pairs={{4,0},{5,1},{2,6},{3,7},{12,8},{13,9},{10,14},{11,15},{20,16},{21,... | collective-permute-start | bytes 4128776 | tf_op jit(solution)/shard_map/ppermute | solution.py:34
  374.5 51.7 %copy-start.17 = (bf16[128,512]{0,1:T(8,128)(2,1)}, bf16[128,512]{0,1:T(8,128)(2,1)S(1)}, u32[]{:S(2)}) copy-start(bf16[128,512]{0,1:T(8,128)(2,1)S(1)} %get-tuple-element.39) | copy-start | bytes 393220
  374.5 51.7 %copy-start.19 = (bf16[128,512]{0,1:T(8,128)(2,1)}, bf16[128,512]{0,1:T(8,128)(2,1)S(1)}, u32[]{:S(2)}) copy-start(bf16[128,512]{0,1:T(8,128)(2,1)S(1)} %get-tuple-element.40) | copy-start | bytes 393220
  407.6 41.6 %all-to-all-start.6 = ((bf16[32,16,2688]{2,1,0:T(8,128)(2,1)}), bf16[32,16,2688]{2,1,0:T(8,128)(2,1)S(1)}, u32[]{:S(2)}, u32[]{:S(2)}) async-start(bf16[32,16,2688]{2,1,0:T(8,128)(2,1)} %bitcast.22), calls=%async_computation.6 | async-start | bytes 5505024 | tf_op jit(solution)/shard_map/all_to_all | solution.py:233
  416.2 9.2 %collective-permute-start.17 = (bf16[64,1792]{1,0:T(8,128)(2,1)S(1)}, bf16[64,1792]{1,0:T(8,128)(2,1)S(1)}, u32[]{:S(2)}, u32[]{:S(2)}) collective-permute-start(bf16[64,1792]{1,0:T(8,128)(2,1)S(1)} %slice.135), channel_id=1, source_target_pairs={{0,3},{3,0},{1,2},{2,1},{4,7},{7,4},{5,6},{6,5},{8,11},{11,8},{9,1... | collective-permute-start | bytes 688136 | tf_op jit(solution)/shard_map/ppermute | solution.py:186
  449.1 16.0 %all-to-all-start.7 = ((bf16[16,8,2688]{2,1,0:T(8,128)(2,1)}), bf16[16,8,2688]{2,1,0:T(8,128)(2,1)S(1)}, u32[]{:S(2)}, u32[]{:S(2)}) async-start(bf16[16,8,2688]{2,1,0:T(8,128)(2,1)} %bitcast.24), calls=%async_computation.7 | async-start | bytes 1376256 | tf_op jit(solution)/shard_map/all_to_all | solution.py:234
  456.5 11.3 %collective-permute-start.23 = (bf16[64,2688]{1,0:T(8,128)(2,1)}, bf16[64,2688]{1,0:T(8,128)(2,1)}, u32[]{:S(2)}, u32[]{:S(2)}) collective-permute-start(bf16[64,2688]{1,0:T(8,128)(2,1)} %slice.134), channel_id=1, source_target_pairs={{0,3},{3,0},{1,2},{2,1},{4,7},{7,4},{5,6},{6,5},{8,11},{11,8},{9,1... | collective-permute-start | bytes 1032200 | tf_op jit(solution)/shard_map/ppermute | solution.py:186
  467.6 9.2 %copy-start.22 = (bf16[64,1792]{1,0:T(8,128)(2,1)S(1)}, bf16[64,1792]{1,0:T(8,128)(2,1)}, u32[]{:S(2)}) copy-start(bf16[64,1792]{1,0:T(8,128)(2,1)} %fusion.5) | copy-start | bytes 688132
  467.7 9.1 %collective-permute-start.29 = (bf16[64,2688]{1,0:T(8,128)(2,1)S(1)}, bf16[64,2688]{1,0:T(8,128)(2,1)S(1)}, u32[]{:S(2)}, u32[]{:S(2)}) collective-permute-start(bf16[64,2688]{1,0:T(8,128)(2,1)S(1)} %slice.133), channel_id=1, source_target_pairs={{0,3},{3,0},{1,2},{2,1},{4,7},{7,4},{5,6},{6,5},{8,11},{11,8},{9,1... | collective-permute-start | bytes 1032200 | tf_op jit(solution)/shard_map/ppermute | solution.py:186
  (16 other events, 37.0 us)
where the time goes:
time: 480 us; the launch traced here: 478 us
  waiting for transfers between devices  263 us (55%)
  starting transfers between devices  94.6 us (20%)
  Pallas kernels  51.9 us (11%)
  matrix products  21.8 us (5%)
  local copies, waits for them, and re-layouts  19.7 us (4%)
  blocking collectives  18.8 us (4%)
  other arithmetic  7.62 us (2%)
    ppermute x5, waiting for transfers between devices, pair_exchange(): return lax.ppermute(value, ('zh', 'zl'), PAIR)  109 us
    all_to_all x4, waiting for transfers between devices, exchange(): lax.all_to_all(main.reshape(2 * chips, 16, columns), EXP, 0, 0, tiled=True)  70 us
    ppermute x25, waiting for transfers between devices, along(): return lax.ppermute(value, COL, pairs)  57.3 us
    ppermute x25, starting transfers between devices, along(): return lax.ppermute(value, COL, pairs)  54.4 us
    pallas_call x2, Pallas kernels, hidden_units(): pl.pallas_call(functools.partial(hidden_kernel, quarters=kinds), grid_spe...  32.8 us
    all_to_all x3, waiting for transfers between devices, exchange(): lax.all_to_all(rest.reshape(chips, 8, columns), ('y', 'x'), 0, 0, tiled=T...  26.7 us
    pallas_call x3, Pallas kernels, down_rows(): pl.pallas_call(down_kernel, grid_spec=pltpu.PrefetchScalarGridSpec(num_sc...  19.1 us
    all_to_all x1, blocking collectives, exchange(): lax.all_to_all(rest.reshape(chips, 8, columns), ('y', 'x'), 0, 0, tiled=T...  18.8 us
  transfers between devices with their start and end apart: 37, of which 17 were waited for; matrix products, arithmetic and copies ran while one was open for 7% of the time, Pallas kernels for 11%

commit v1 on v0

v1 whole, which is shorter than its diff:
```python
import functools

import jax
import jax.numpy as jnp
from jax import lax
from jax.experimental import pallas as pl
from jax.experimental.pallas import tpu as pltpu
from jax.sharding import Mesh, PartitionSpec as P

EXP = ("y", "x", "c")
COL = ("c", "zh", "zl")
ALL = ("y", "x", "c", "zh", "zl")


def swaps(*pairs):
    return [way for a, b in pairs for way in ((a, b), (b, a))]


PAIR = swaps((0, 3), (1, 2))
NEXT = swaps((0, 1), (6, 7), (4, 3), (5, 2))
FAR = swaps((5, 3), (4, 2))
SIBLING = swaps((0, 4), (1, 5), (2, 6), (3, 7))
FROM_HOME = [(0, 4), (1, 5), (6, 2), (7, 3)]
TO_HOME = [(b, a) for a, b in FROM_HOME]
STEPS = (1792, 2688, 2688)
QUARTER = 256
MAIN = 256
REST = 128
TILE = 896
DEEP = 1792


def along(value, pairs):
    return lax.ppermute(value, COL, pairs)


def after(value, *earlier):
    return lax.optimization_barrier((value, *earlier))[0]


def share(own, near, far, near_after, far_after):
    across = along(after(near, near_after), SIBLING)
    brought = along(after(far, far_after), TO_HOME)
    return own, along(own, FROM_HOME), near, across, brought, far


def pick_block(flag, wanted, block):
    return jnp.where(flag[0] == wanted, block, 0)


def hidden_kernel(flag, *refs, quarters):
    mine, theirs, rest = refs[:3]
    panels, out, gate_sum, up_sum = refs[3:-3], refs[-3], refs[-2], refs[-1]
    part = pl.program_id(0)

    @pl.when(part == 0)
    def _():
        gate_sum[...] = jnp.zeros_like(gate_sum)
        up_sum[...] = jnp.zeros_like(up_sum)

    def add(total, place, weights):
        for rows, first in ((mine, 0), (theirs, MAIN), (rest, 2 * MAIN)):
            number = rows.shape[0]
            total[pl.ds(first, number), pl.ds(place * QUARTER, QUARTER)] += lax.dot_general(
                rows[...], weights, (((1,), (1,)), ((), ())), preferred_element_type=jnp.float32
            )

    at = 0
    for place, kind in enumerate(quarters):
        if kind == 1:
            both = panels[at][...]
        else:
            both = jnp.where(flag[0] == 1, panels[at][...], panels[at + 1][...])
        add(gate_sum, place, both[:QUARTER])
        add(up_sum, place, both[QUARTER:])
        at += kind

    @pl.when(part == pl.num_programs(0) - 1)
    def _():
        gate = gate_sum[...]
        out[...] = (gate / (1.0 + jnp.exp(-gate)) * up_sum[...]).astype(out.dtype)


def hidden_units(flag, mine, theirs, rest, quarters):
    width = rest.shape[1]
    count = len(quarters)
    kinds = tuple(len(quarter) for quarter in quarters)
    specs = [
        pl.BlockSpec((MAIN, DEEP), lambda i, f: (0, i)),
        pl.BlockSpec((MAIN, DEEP), lambda i, f: (0, i)),
        pl.BlockSpec((REST, DEEP), lambda i, f: (0, i)),
    ]
    operands = [mine, theirs, rest]
    for quarter in quarters:
        for place, both in enumerate(quarter):
            if len(quarter) == 1:
                spec = pl.BlockSpec((2 * QUARTER, DEEP), lambda i, f: (0, i))
            else:
                spec = pl.BlockSpec(
                    (2 * QUARTER, DEEP), lambda i, f, w=1 - place: (0, pick_block(f, w, i))
                )
            specs.append(spec)
            operands.append(both)
    rows = 2 * MAIN + REST
    return pl.pallas_call(
        functools.partial(hidden_kernel, quarters=kinds),
        grid_spec=pltpu.PrefetchScalarGridSpec(
            num_scalar_prefetch=1,
            grid=(width // DEEP,),
            in_specs=specs,
            out_specs=pl.BlockSpec((rows, count * QUARTER), lambda i, f: (0, 0)),
            scratch_shapes=[pltpu.VMEM((rows, count * QUARTER), jnp.float32)] * 2,
        ),
        out_shape=jax.ShapeDtypeStruct((rows, count * QUARTER), jnp.bfloat16),
        compiler_params=pltpu.CompilerParams(vmem_limit_bytes=48 * 2**20),
        cost_estimate=pl.CostEstimate(
            flops=4 * rows * width * count * QUARTER,
            bytes_accessed=2 * width * (rows + 2 * count * QUARTER),
            transcendentals=rows * count * QUARTER,
        ),
    )(flag, *operands)


def down_kernel(flag, first, last, own, copied, near, across, brought, far, out_main, out_rest):
    home = flag[0] == 1
    panels = (
        (first[:, :QUARTER], jnp.where(home, own[...], copied[...])),
        (first[:, QUARTER : 2 * QUARTER], near[...]),
        (first[:, 2 * QUARTER :], across[...]),
        (last[...], jnp.where(home, brought[...], far[...])),
    )
    total = None
    for hidden, weights in panels:
        term = jnp.dot(hidden, weights, preferred_element_type=jnp.float32)
        total = term if total is None else total + term
    total = total.astype(out_main.dtype)
    out_main[:, :8] = total[:MAIN].reshape(-1, 8, TILE)
    out_main[:, 8:] = total[MAIN : 2 * MAIN].reshape(-1, 8, TILE)
    out_rest[...] = total[2 * MAIN :]


def down_rows(flag, first, last, panels):
    step = panels[0].shape[1]
    rows = 2 * MAIN + REST

    def panel(wanted=None):
        if wanted is None:
            return pl.BlockSpec((QUARTER, TILE), lambda i, f: (0, i))
        return pl.BlockSpec((QUARTER, TILE), lambda i, f: (0, pick_block(f, wanted, i)))

    main, tail = pl.pallas_call(
        down_kernel,
        grid_spec=pltpu.PrefetchScalarGridSpec(
            num_scalar_prefetch=1,
            grid=(step // TILE,),
            in_specs=[
                pl.BlockSpec(first.shape, lambda i, f: (0, 0)),
                pl.BlockSpec(last.shape, lambda i, f: (0, 0)),
                panel(1),
                panel(0),
                panel(),
                panel(),
                panel(1),
                panel(0),
            ],
            out_specs=[
                pl.BlockSpec((MAIN // 8, 16, TILE), lambda i, f: (0, 0, i)),
                pl.BlockSpec((REST, TILE), lambda i, f: (0, i)),
            ],
        ),
        out_shape=[
            jax.ShapeDtypeStruct((MAIN // 8, 16, step), jnp.bfloat16),
            jax.ShapeDtypeStruct((REST, step), jnp.bfloat16),
        ],
        compiler_params=pltpu.CompilerParams(vmem_limit_bytes=32 * 2**20),
        cost_estimate=pl.CostEstimate(
            flops=8 * rows * QUARTER * step,
            bytes_accessed=2 * (4 * QUARTER * step + rows * (4 * QUARTER + step)),
            transcendentals=0,
        ),
    )(flag, first, last, *panels)
    return main.reshape(2 * MAIN, step), tail


def pair_exchange(value):
    return lax.ppermute(value, ("zh", "zl"), PAIR)


def body(tokens, route_ids, route_gates, gate_weight, up_weight, down_weight):
    tok_rows, width = tokens.shape
    chips = lax.axis_size("y") * lax.axis_size("x")
    side = lax.axis_index("zh")
    flag = (lax.axis_index("c") == side).astype(jnp.int32).reshape(1)

    routes = jnp.concatenate([route_ids.astype(jnp.float32), route_gates], axis=1)
    high = lax.reduce_precision(route_gates, 8, 7)
    extra = jnp.concatenate([route_ids.astype(jnp.float32), high, route_gates - high], axis=1)
    extra = jnp.pad(extra.astype(jnp.bfloat16), ((0, 0), (0, 128 - extra.shape[1])))
    other = pair_exchange(jnp.concatenate([tokens, extra], axis=1))

    top = route_ids.shape[1]
    hosted = (2 * jnp.arange(chips, dtype=jnp.int32) + side).astype(jnp.float32)
    place = jnp.arange(tok_rows)
    earlier = (place[:, None] > place[None, :]).astype(jnp.bfloat16)

    def slots(table, shift):
        match = (table[:, :top, None] == hosted[None, None, :]).astype(jnp.float32)
        named = jnp.sum(match, axis=1)
        weight = jnp.sum(table[:, top:, None] * match, axis=1)
        rank = jnp.dot(earlier, named.astype(jnp.bfloat16), preferred_element_type=jnp.float32)
        rank = jnp.where(named > 0, rank.astype(jnp.int32), -1)[:, :, None]
        on_tile = rank == jnp.arange(16)
        on_rest = (rank - 16 + 4 * shift == jnp.arange(8)) & (rank >= 16)
        on_main = jnp.zeros_like(on_tile[:, :, :8])
        halves = [on_tile[:, :, :8], on_tile[:, :, 8:]]
        on_main = jnp.concatenate(
            [piece for half in halves for piece in ((on_main, half) if shift else (half, on_main))],
            axis=2,
        )
        return (
            *(jnp.transpose(on, (1, 2, 0)).astype(jnp.bfloat16) for on in (on_tile, on_rest)),
            *(jnp.where(on, weight[:, :, None], 0.0) for on in (on_main, on_rest)),
        )

    def rows_of(part, rows):
        flat = part.reshape(-1, rows.shape[0])
        return jnp.dot(flat, rows, preferred_element_type=jnp.float32).astype(jnp.bfloat16)

    def exchange_main(rows):
        parts = rows.reshape(2 * chips, -1, rows.shape[1])
        return lax.all_to_all(parts, EXP, 0, 0, tiled=True).reshape(rows.shape)

    def exchange_rest(rows):
        parts = rows.reshape(chips, 8, rows.shape[1])
        return lax.all_to_all(parts, ("y", "x"), 0, 0, tiled=True).reshape(rows.shape)

    pick, pick_rest, mix_own, mix_own_rest = slots(routes, 0)
    sent = rows_of(pick, tokens)
    mine = exchange_main(sent)
    other = after(other, sent)
    extra, other = other[:, width:].astype(jnp.float32), other[:, :width]
    ids, gate, low = (extra[:, at : at + 8] for at in (0, 8, 16))
    other_routes = jnp.concatenate([ids, gate + low], axis=1)

    gate_up = jnp.concatenate([after(gate_weight[0], other), up_weight[0]], axis=0)
    near = along(gate_up, NEXT)
    far = along(gate_up, FAR)

    pick, other_rest, mix_other, mix_other_rest = slots(other_routes, 1)
    theirs = exchange_main(after(rows_of(pick, other), mine))
    rest = rows_of(
        jnp.concatenate([pick_rest, other_rest], axis=2), jnp.concatenate([tokens, other], axis=0)
    )
    rest = exchange_rest(after(rest, theirs))
    copied, across = along(gate_up, FROM_HOME), along(after(near, theirs), SIBLING)

    def halves(*parts):
        part = jnp.concatenate([part.reshape(tok_rows, -1) for part in parts], axis=0)
        high = lax.reduce_precision(part, 8, 7)
        return jnp.concatenate([high, part - high], axis=0).astype(jnp.bfloat16)

    mix_main, mix_rest = halves(mix_own, mix_other), halves(mix_own_rest, mix_other_rest)
    count = 2 * tok_rows

    def columns(number, *earlier):
        at = sum(STEPS[:number])
        own = after(down_weight[0][:, at : at + STEPS[number]], *earlier)
        return own, along(own, NEXT), along(own, FAR)

    down_0 = columns(0, near)
    first = hidden_units(flag, mine, theirs, rest, [(gate_up, copied), (near,), (across,)])
    brought = along(after(far, first), TO_HOME)
    down_1 = columns(1, far, first)
    last = hidden_units(flag, after(mine, first), theirs, rest, [(brought, far)])
    result_0 = down_rows(flag, first, last, share(*down_0, first, first))
    down_2 = columns(2, down_0[2], result_0[0])
    result_1 = down_rows(flag, first, last, share(*down_1, result_0[0], result_0[0]))
    result_2 = down_rows(flag, first, last, share(*down_2, result_1[0], result_1[0]))
    mains, rests = zip(result_0, result_1, result_2, strict=True)
    early = jnp.concatenate(rests[:2], axis=1)
    back_0 = exchange_main(mains[0])
    early = exchange_rest(after(early, back_0))
    back_1 = exchange_main(after(mains[1], early))
    late = exchange_rest(after(rests[2], back_1))
    back_2 = exchange_main(after(mains[2], late))
    outs = []
    for back, back_rest in (
        (back_0, early[:, : STEPS[0]]),
        (back_1, early[:, STEPS[0] :]),
        (back_2, late),
    ):
        sums = jnp.dot(mix_main, back, preferred_element_type=jnp.float32) + jnp.dot(
            mix_rest, back_rest, preferred_element_type=jnp.float32
        )
        sums = sums[:count] + sums[count:]
        partner = pair_exchange(sums[tok_rows:].astype(jnp.bfloat16))
        outs.append((sums[:tok_rows] + partner.astype(jnp.float32)).astype(jnp.bfloat16))
    return jnp.concatenate(outs, axis=1)


def solution(mesh):
    fine = Mesh(mesh.devices.reshape(4, 4, 2, 2, 2), ALL)
    rows = P(ALL, None)
    panels = P(EXP, ("zh", "zl"), None)
    return jax.shard_map(
        body,
        mesh=fine,
        in_specs=(rows, rows, rows, panels, panels, panels),
        out_specs=rows,
        check_vma=False,
    )
```

time: 480 us -> 496 us (1.033)
  starting transfers between devices: 94.6 us -> 170 us
  waiting for transfers between devices: 263 us -> 226 us
  blocking collectives: 18.8 us -> 0 us
  local copies, waits for them, and re-layouts: 19.7 us -> 6.15 us
  other arithmetic: 7.62 us -> 18.1 us
    all_to_all x7 -> x8, waiting for transfers between devices: 96.8 us -> 187 us  [the longest x5 144 us: exchange_main(): return lax.all_to_all(parts, EXP, 0, 0, tiled=True).reshape(rows.shape)]
    ppermute x5 -> x4, waiting for transfers between devices: 109 us -> 27.6 us  [pair_exchange(): return lax.ppermute(value, ('zh', 'zl'), PAIR)]
    ppermute x25 -> x20, starting transfers between devices: 54.4 us -> 114 us  [along(): return lax.ppermute(value, COL, pairs)]
    ppermute x25 -> x20, waiting for transfers between devices: 57.3 us -> 11.9 us  [along(): return lax.ppermute(value, COL, pairs)]
    all_to_all x1 -> x0, blocking collectives: 18.8 us -> none  [exchange(): lax.all_to_all(rest.reshape(chips, 8, columns), ('y', 'x'), 0, 0, tiled=T...]
    unnamed x55 -> x31, local copies, waits for them, and re-layouts: 14.5 us -> 3.64 us
    ppermute x5 -> x4, starting transfers between devices: 4.14 us -> 14.3 us  [pair_exchange(): return lax.ppermute(value, ('zh', 'zl'), PAIR)]
    concatenate x2 -> x4, other arithmetic: 0.76 us -> 9.23 us  [the longest x1 6.86 us: body(): jnp.concatenate([after(gate_weight[0], other), up_weight[0]], axis=0)]
  transfers between devices with their start and end apart: 37 -> 32, of which waited for: 17 -> 11; matrix products, arithmetic and copies ran while one was open for 7% -> 5% of each run, Pallas kernels for 11% -> 11%
where the time goes in v1:
time: 496 us; the launch traced here: 495 us
  waiting for transfers between devices  226 us (46%)
  starting transfers between devices  170 us (34%)
  Pallas kernels  52.6 us (11%)
  matrix products  20.7 us (4%)
  other arithmetic  18.1 us (4%)
  local copies, waits for them, and re-layouts  6.15 us (1%)
    all_to_all x5, waiting for transfers between devices, exchange_main(): return lax.all_to_all(parts, EXP, 0, 0, tiled=True).reshape(rows.shape)  144 us
    ppermute x20, starting transfers between devices, along(): return lax.ppermute(value, COL, pairs)  114 us
    all_to_all x3, waiting for transfers between devices, exchange_rest(): lax.all_to_all(parts, ('y', 'x'), 0, 0, tiled=True).reshape(rows.shape)  42.9 us
    pallas_call x2, Pallas kernels, hidden_units(): pl.pallas_call(functools.partial(hidden_kernel, quarters=kinds), grid_spe...  33.4 us
    all_to_all x5, starting transfers between devices, exchange_main(): return lax.all_to_all(parts, EXP, 0, 0, tiled=True).reshape(rows.shape)  30.2 us
    ppermute x4, waiting for transfers between devices, pair_exchange(): return lax.ppermute(value, ('zh', 'zl'), PAIR)  27.6 us
    pallas_call x3, Pallas kernels, down_rows(): pl.pallas_call(down_kernel, grid_spec=pltpu.PrefetchScalarGridSpec(num_sc...  19.2 us
    ppermute x4, starting transfers between devices, pair_exchange(): return lax.ppermute(value, ('zh', 'zl'), PAIR)  14.3 us
  transfers between devices with their start and end apart: 32, of which 11 were waited for; matrix products, arithmetic and copies ran while one was open for 5% of the time, Pallas kernels for 11%

profile of v1, /device:TPU:0, one launch (start us, length us, event | category | flops | bytes accessed | tf_op | source)
XLA Modules:
  0.0 494.7 jit_solution(10505154716430984035)
XLA Ops:
  2.8 4.2 collective-permute-start
  8.1 3.0 convolution_convert_fusion.1
  11.0 16.7 %collective-permute-done = bf16[64,7296]{1,0:T(8,128)(2,1)S(1)} collective-permute-done((bf16[64,7296]{1,0:T(8,128)(2,1)S(1)}, bf16[64,7296]{1,0:T(8,128)(2,1)S(1)}, u32[]{:S(2)}, u32[]{:S(2)}) %collective-permute-start) | collective-permute-done | bytes 933920 | tf_op jit(solution)/shard_map/ppermute | solution.py:186
  27.7 6.9 %pad_maximum_fusion.refs_3_ = bf16[512,7168]{1,0:T(8,128)(2,1)} fusion(bf16[256,7168]{1,0:T(8,128)(2,1)} %bitcast.81, bf16[256,7168]{1,0:T(8,128)(2,1)} %bitcast.82), kind=kLoop, calls=%fused_computation.3 | loop fusion | flops 14680064 | bytes 14680064 | tf_op jit(solution)/shard_map/concatenate | solution.py:245
  34.6 10.1 %all-to-all-start = ((bf16[32,8,7168]{2,1,0:T(8,128)(2,1)}), bf16[32,8,7168]{2,1,0:T(8,128)(2,1)}, u32[]{:S(2)}, u32[]{:S(2)}) async-start(bf16[32,8,7168]{2,1,0:T(8,128)(2,1)} %bitcast.76), calls=%async_computation | async-start | bytes 7340032 | tf_op jit(solution)/shard_map/all_to_all | solution.py:231
  45.9 3.0 convolution_convert_fusion
  48.8 43.5 %all-to-all-done = bf16[32,8,7168]{2,1,0:T(8,128)(2,1)} async-done(((bf16[32,8,7168]{2,1,0:T(8,128)(2,1)}), bf16[32,8,7168]{2,1,0:T(8,128)(2,1)}, u32[]{:S(2)}, u32[]{:S(2)}) %all-to-all-start) | async-done | bytes 3670048 | tf_op jit(solution)/shard_map/all_to_all | solution.py:231
  92.4 5.0 %all-to-all-start.1 = ((bf16[32,8,7168]{2,1,0:T(8,128)(2,1)}), bf16[32,8,7168]{2,1,0:T(8,128)(2,1)}, u32[]{:S(2)}, u32[]{:S(2)}) async-start(bf16[32,8,7168]{2,1,0:T(8,128)(2,1)} %bitcast.77), calls=%async_computation.1 | async-start | bytes 7340032 | tf_op jit(solution)/shard_map/all_to_all | solution.py:231
  97.3 5.0 %collective-permute-start.1 = (bf16[512,7168]{1,0:T(8,128)(2,1)}, bf16[512,7168]{1,0:T(8,128)(2,1)}, u32[]{:S(2)}, u32[]{:S(2)}) collective-permute-start(bf16[512,7168]{1,0:T(8,128)(2,1)} %pad_maximum_fusion.refs_3_), channel_id=1, source_target_pairs={{0,4},{1,5},{6,2},{7,3},{8,12},{9,13},{14,10},{15,11},{16,20},{17,... | collective-permute-start | bytes 22020104 | tf_op jit(solution)/shard_map/ppermute | solution.py:34
  102.4 42.7 %all-to-all-done.1 = bf16[32,8,7168]{2,1,0:T(8,128)(2,1)} async-done(((bf16[32,8,7168]{2,1,0:T(8,128)(2,1)}), bf16[32,8,7168]{2,1,0:T(8,128)(2,1)}, u32[]{:S(2)}, u32[]{:S(2)}) %all-to-all-start.1) | async-done | bytes 3670048 | tf_op jit(solution)/shard_map/all_to_all | solution.py:231
  145.0 3.7 collective-permute-start.4
  148.9 1.9 convolution_convert_fusion.2
  150.9 3.7 all-to-all-start.2
  154.6 26.6 %all-to-all-done.2 = bf16[16,8,7168]{2,1,0:T(8,128)(2,1)S(1)} async-done(((bf16[16,8,7168]{2,1,0:T(8,128)(2,1)}), bf16[16,8,7168]{2,1,0:T(8,128)(2,1)S(1)}, u32[]{:S(2)}, u32[]{:S(2)}) %all-to-all-start.2) | async-done | bytes 1835040 | tf_op jit(solution)/shard_map/all_to_all | solution.py:235
  181.2 23.2 %shard_map.64.first = bf16[640,768]{1,0:T(8,128)(2,1)S(1)} custom-call(s32[1]{0:T(128)} %bitcast.4.flag, bf16[256,7168]{1,0:T(8,128)(2,1)} %bitcast.6.refs_0_, bf16[256,7168]{1,0:T(8,128)(2,1)} %bitcast.10.refs_1_, bf16[128,7168]{1,0:T(8,128)(2,1)S(1)} %bitcast.74, bf16[512,7168]{1,0:T(8,128)(2,1)} %pad_maximum_fusion.refs_3_, ...), custom_call_target="tpu_custom_call" | custom-call | flops 14092861440 | bytes 31195136 | tf_op jit(solution)/shard_map/pallas_call | solution.py:105
  206.5 3.1 collective-permute-start.7
  210.9 1.7 collective-permute-start.14
  212.6 58.7 %collective-permute-start.6 = (bf16[256,1792]{1,0:T(8,128)(2,1)S(1)}, bf16[256,1792]{1,0:T(8,128)(2,1)S(1)}, u32[]{:S(2)}, u32[]{:S(2)}) collective-permute-start(bf16[256,1792]{1,0:T(8,128)(2,1)S(1)} %slice.114.own), channel_id=1, source_target_pairs={{0,4},{1,5},{6,2},{7,3},{8,12},{9,13},{14,10},{15,11},{16,20},{17,... | collective-permute-start | bytes 2752520 | tf_op jit(solution)/shard_map/ppermute | solution.py:34
  272.6 22.6 %collective-permute-start.8 = (bf16[256,1792]{1,0:T(8,128)(2,1)S(1)}, bf16[256,1792]{1,0:T(8,128)(2,1)S(1)}, u32[]{:S(2)}, u32[]{:S(2)}) collective-permute-start(bf16[256,1792]{1,0:T(8,128)(2,1)S(1)} %collective-permute-done.7.near), channel_id=1, source_target_pairs={{0,4},{4,0},{1,5},{5,1},{2,6},{6,2},{3,7},{7,3},{8,12},{12,8},{9,1... | collective-permute-start | bytes 2752520 | tf_op jit(solution)/shard_map/ppermute | solution.py:34
  295.3 10.2 %shard_map.65.last = bf16[640,256]{1,0:T(8,128)(2,1)S(1)} custom-call(s32[1]{0:T(128)} %bitcast.4.flag, bf16[256,7168]{1,0:T(8,128)(2,1)} %bitcast.6.refs_0_, bf16[256,7168]{1,0:T(8,128)(2,1)} %bitcast.10.refs_1_, bf16[128,7168]{1,0:T(8,128)(2,1)S(1)} %bitcast.75, bf16[512,7168]{1,0:T(8,128)(2,1)} %collective-permute-done.5.refs_3_, ...), custom_call_target="tpu_custom_call" | custom-call | flops 4697620480 | bytes 16515072 | tf_op jit(solution)/shard_map/pallas_call | solution.py:105
  305.4 3.0 collective-permute-start.11
  308.5 4.6 shard_map.66
  314.3 2.2 collective-permute-start.13
  317.4 6.1 %all-to-all-start.3 = ((bf16[32,16,1792]{2,1,0:T(8,128)(2,1)}), bf16[32,16,1792]{2,1,0:T(8,128)(2,1)}, u32[]{:S(2)}, u32[]{:S(2)}) async-start(bf16[32,16,1792]{2,1,0:T(8,128)(2,1)} %get-tuple-element.41), calls=%async_computation.3 | async-start | bytes 3670016 | tf_op jit(solution)/shard_map/all_to_all | solution.py:231
  323.5 4.2 collective-permute-start.18
  329.0 7.5 %shard_map.67 = (bf16[32,16,2688]{2,1,0:T(8,128)(2,1)}, bf16[128,2688]{1,0:T(8,128)(2,1)S(1)}) custom-call(s32[1]{0:T(128)} %bitcast.4.flag, bf16[640,768]{1,0:T(8,128)(2,1)S(1)} %copy-done.1, bf16[640,256]{1,0:T(8,128)(2,1)S(1)} %shard_map.65.last, bf16[256,2688]{1,0:T(8,128)(2,1)} %get-tuple-element.43.own, ...), custom_call_target="tpu_custom_call" | custom-call | flops 3523215360 | bytes 10256384 | tf_op jit(solution)/shard_map/pallas_call | solution.py:151
  337.7 11.8 %collective-permute-done.19.near = bf16[256,2688]{1,0:T(8,128)(2,1)} collective-permute-done((bf16[256,2688]{1,0:T(8,128)(2,1)S(1)}, bf16[256,2688]{1,0:T(8,128)(2,1)}, u32[]{:S(2)}, u32[]{:S(2)}) %collective-permute-start.19) | collective-permute-done | bytes 1376288 | tf_op jit(solution)/shard_map/ppermute | solution.py:34
  349.6 2.9 collective-permute-start.20
  353.7 4.4 all-to-all-start.4
  359.3 7.2 %shard_map.68 = (bf16[32,16,2688]{2,1,0:T(8,128)(2,1)}, bf16[128,2688]{1,0:T(8,128)(2,1)}) custom-call(s32[1]{0:T(128)} %bitcast.4.flag, bf16[640,768]{1,0:T(8,128)(2,1)S(1)} %copy-done.2, bf16[640,256]{1,0:T(8,128)(2,1)S(1)} %shard_map.65.last, bf16[256,2688]{1,0:T(8,128)(2,1)S(1)} %get-tuple-element.50.own, ...), custom_call_target="tpu_custom_call" | custom-call | flops 3523215360 | bytes 10256384 | tf_op jit(solution)/shard_map/pallas_call | solution.py:151
  366.5 11.1 %all-to-all-done.4 = bf16[16,8,4480]{2,1,0:T(8,128)(2,1)} async-done(((bf16[16,8,4480]{2,1,0:T(8,128)(2,1)}), bf16[16,8,4480]{2,1,0:T(8,128)(2,1)}, u32[]{:S(2)}, u32[]{:S(2)}) %all-to-all-start.4) | async-done | bytes 1146912 | tf_op jit(solution)/shard_map/all_to_all | solution.py:235
  377.5 4.2 all-to-all-start.7
  382.0 37.2 %all-to-all-done.7 = bf16[32,16,2688]{2,1,0:T(8,128)(2,1)S(1)} async-done(((bf16[32,16,2688]{2,1,0:T(8,128)(2,1)}), bf16[32,16,2688]{2,1,0:T(8,128)(2,1)S(1)}, u32[]{:S(2)}, u32[]{:S(2)}) %all-to-all-start.7) | async-done | bytes 2752544 | tf_op jit(solution)/shard_map/all_to_all | solution.py:231
  419.2 4.8 all-to-all-start.5
  424.4 1.4 fusion.11
  425.8 2.2 convolution_add_fusion.2
  428.1 3.6 collective-permute-start.16
  431.7 5.9 %collective-permute-done.16 = bf16[64,1792]{1,0:T(8,128)(2,1)S(1)} collective-permute-done((bf16[64,1792]{1,0:T(8,128)(2,1)S(1)}, bf16[64,1792]{1,0:T(8,128)(2,1)S(1)}, u32[]{:S(2)}, u32[]{:S(2)}) %collective-permute-start.16) | collective-permute-done | bytes 229408 | tf_op jit(solution)/shard_map/ppermute | solution.py:186
  438.3 2.5 fusion.14
  440.8 20.7 %all-to-all-done.5 = bf16[32,16,2688]{2,1,0:T(8,128)(2,1)} async-done(((bf16[32,16,2688]{2,1,0:T(8,128)(2,1)}), bf16[32,16,2688]{2,1,0:T(8,128)(2,1)}, u32[]{:S(2)}, u32[]{:S(2)}) %all-to-all-start.5) | async-done | bytes 2752544 | tf_op jit(solution)/shard_map/all_to_all | solution.py:231
  461.5 2.7 fusion.15
  464.2 3.2 convolution_add_fusion.1
  467.4 3.6 all-to-all-start.6
  471.0 2.0 slice_add_fusion.1
  475.0 3.2 collective-permute-start.17
  478.2 5.2 %all-to-all-done.6 = bf16[16,8,2688]{2,1,0:T(8,128)(2,1)S(1)} async-done(((bf16[16,8,2688]{2,1,0:T(8,128)(2,1)}), bf16[16,8,2688]{2,1,0:T(8,128)(2,1)S(1)}, u32[]{:S(2)}, u32[]{:S(2)}) %all-to-all-start.6) | async-done | bytes 688160 | tf_op jit(solution)/shard_map/all_to_all | solution.py:235
  484.2 3.3 collective-permute-start.23
  488.6 5.0 %collective-permute-done.23 = bf16[64,2688]{1,0:T(8,128)(2,1)S(1)} collective-permute-done((bf16[64,2688]{1,0:T(8,128)(2,1)S(1)}, bf16[64,2688]{1,0:T(8,128)(2,1)S(1)}, u32[]{:S(2)}, u32[]{:S(2)}) %collective-permute-start.23) | collective-permute-done | bytes 344096 | tf_op jit(solution)/shard_map/ppermute | solution.py:186
  (109 shorter events, 22.9 us)
Async XLA Ops:
  0.0 7.1 %copy-start.12 = (f32[64,8]{0,1:T(8,128)S(1)}, f32[64,8]{0,1:T(8,128)}, u32[]{:S(2)}) copy-start(f32[64,8]{0,1:T(8,128)} %param.8) | copy-start | bytes 6148
  0.0 8.1 %copy-start.4 = (bf16[64,7168]{1,0:T(8,128)(2,1)S(1)}, bf16[64,7168]{1,0:T(8,128)(2,1)}, u32[]{:S(2)}) copy-start(bf16[64,7168]{1,0:T(8,128)(2,1)} %param.6) | copy-start | bytes 2752516
  2.8 24.9 %collective-permute-start = (bf16[64,7296]{1,0:T(8,128)(2,1)S(1)}, bf16[64,7296]{1,0:T(8,128)(2,1)S(1)}, u32[]{:S(2)}, u32[]{:S(2)}) collective-permute-start(bf16[64,7296]{1,0:T(8,128)(2,1)S(1)} %fusion.6), channel_id=1, source_target_pairs={{0,3},{3,0},{1,2},{2,1},{4,7},{7,4},{5,6},{6,5},{8,11},{11,8},{9,1... | collective-permute-start | bytes 2801672 | tf_op jit(solution)/shard_map/ppermute | solution.py:186
  27.7 18.2 %copy-start.7 = (bf16[64,7296]{1,0:T(8,128)(2,1)}, bf16[64,7296]{1,0:T(8,128)(2,1)S(1)}, u32[]{:S(2)}) copy-start(bf16[64,7296]{1,0:T(8,128)(2,1)S(1)} %collective-permute-done) | copy-start | bytes 2801668
  34.6 110.4 %collective-permute-start.2 = (bf16[512,7168]{1,0:T(8,128)(2,1)}, bf16[512,7168]{1,0:T(8,128)(2,1)}, u32[]{:S(2)}, u32[]{:S(2)}) collective-permute-start(bf16[512,7168]{1,0:T(8,128)(2,1)} %pad_maximum_fusion.refs_3_), channel_id=1, source_target_pairs={{0,1},{1,0},{6,7},{7,6},{4,3},{3,4},{5,2},{2,5},{8,9},{9,8},{14,15... | collective-permute-start | bytes 22020104 | tf_op jit(solution)/shard_map/ppermute | solution.py:34
  34.6 57.8 %all-to-all-start = ((bf16[32,8,7168]{2,1,0:T(8,128)(2,1)}), bf16[32,8,7168]{2,1,0:T(8,128)(2,1)}, u32[]{:S(2)}, u32[]{:S(2)}) async-start(bf16[32,8,7168]{2,1,0:T(8,128)(2,1)} %bitcast.76), calls=%async_computation | async-start | bytes 7340032 | tf_op jit(solution)/shard_map/all_to_all | solution.py:231
  92.4 56.5 %slice-start = ((bf16[64,7296]{1,0:T(8,128)(2,1)}), bf16[64,7168]{1,0:T(8,128)(2,1)S(1)}, s32[]{:S(2)}) async-start(bf16[64,7296]{1,0:T(8,128)(2,1)} %copy-done.7), calls=%async_computation.8 | async-start | bytes 1835008 | tf_op jit(solution)/shard_map/slice | solution.py:241
  92.4 52.6 %all-to-all-start.1 = ((bf16[32,8,7168]{2,1,0:T(8,128)(2,1)}), bf16[32,8,7168]{2,1,0:T(8,128)(2,1)}, u32[]{:S(2)}, u32[]{:S(2)}) async-start(bf16[32,8,7168]{2,1,0:T(8,128)(2,1)} %bitcast.77), calls=%async_computation.1 | async-start | bytes 7340032 | tf_op jit(solution)/shard_map/all_to_all | solution.py:231
  97.3 57.2 %collective-permute-start.1 = (bf16[512,7168]{1,0:T(8,128)(2,1)}, bf16[512,7168]{1,0:T(8,128)(2,1)}, u32[]{:S(2)}, u32[]{:S(2)}) collective-permute-start(bf16[512,7168]{1,0:T(8,128)(2,1)} %pad_maximum_fusion.refs_3_), channel_id=1, source_target_pairs={{0,4},{1,5},{6,2},{7,3},{8,12},{9,13},{14,10},{15,11},{16,20},{17,... | collective-permute-start | bytes 22020104 | tf_op jit(solution)/shard_map/ppermute | solution.py:34
  145.0 36.1 %collective-permute-start.3 = (bf16[512,7168]{1,0:T(8,128)(2,1)}, bf16[512,7168]{1,0:T(8,128)(2,1)}, u32[]{:S(2)}, u32[]{:S(2)}) collective-permute-start(bf16[512,7168]{1,0:T(8,128)(2,1)} %collective-permute-done.2.refs_5_), channel_id=1, source_target_pairs={{0,4},{4,0},{1,5},{5,1},{2,6},{6,2},{3,7},{7,3},{8,12},{12,8},{9,1... | collective-permute-start | bytes 22020104 | tf_op jit(solution)/shard_map/ppermute | solution.py:34
  145.0 59.4 %collective-permute-start.4 = (bf16[512,7168]{1,0:T(8,128)(2,1)}, bf16[512,7168]{1,0:T(8,128)(2,1)}, u32[]{:S(2)}, u32[]{:S(2)}) collective-permute-start(bf16[512,7168]{1,0:T(8,128)(2,1)} %pad_maximum_fusion.refs_3_), channel_id=1, source_target_pairs={{5,3},{3,5},{4,2},{2,4},{13,11},{11,13},{12,10},{10,12},{21,19},{1... | collective-permute-start | bytes 22020104 | tf_op jit(solution)/shard_map/ppermute | solution.py:34
  148.8 2.1 copy-start.13
  150.9 30.3 %all-to-all-start.2 = ((bf16[16,8,7168]{2,1,0:T(8,128)(2,1)}), bf16[16,8,7168]{2,1,0:T(8,128)(2,1)S(1)}, u32[]{:S(2)}, u32[]{:S(2)}) async-start(bf16[16,8,7168]{2,1,0:T(8,128)(2,1)} %bitcast.79), calls=%async_computation.2 | async-start | bytes 3670016 | tf_op jit(solution)/shard_map/all_to_all | solution.py:235
  181.2 24.6 %copy-start.8 = (bf16[1,256,7168]{2,1,0:T(8,128)(2,1)S(1)}, bf16[1,256,7168]{2,1,0:T(8,128)(2,1)}, u32[]{:S(2)}) copy-start(bf16[1,256,7168]{2,1,0:T(8,128)(2,1)} %param.11) | copy-start | bytes 11010052
  204.4 104.1 %copy-start = (bf16[640,768]{1,0:T(8,128)(2,1)}, bf16[640,768]{1,0:T(8,128)(2,1)S(1)}, u32[]{:S(2)}) copy-start(bf16[640,768]{1,0:T(8,128)(2,1)S(1)} %shard_map.64.first) | copy-start | bytes 2949124
  204.4 68.2 %collective-permute-start.5 = (bf16[512,7168]{1,0:T(8,128)(2,1)}, bf16[512,7168]{1,0:T(8,128)(2,1)}, u32[]{:S(2)}, u32[]{:S(2)}) collective-permute-start(bf16[512,7168]{1,0:T(8,128)(2,1)} %collective-permute-done.4.refs_4_), channel_id=1, source_target_pairs={{4,0},{5,1},{2,6},{3,7},{12,8},{13,9},{10,14},{11,15},{20,16},{21,... | collective-permute-start | bytes 22020104 | tf_op jit(solution)/shard_map/ppermute | solution.py:34
  205.8 6.8 %collective-permute-start.9 = (bf16[256,1792]{1,0:T(8,128)(2,1)S(1)}, bf16[256,1792]{1,0:T(8,128)(2,1)S(1)}, u32[]{:S(2)}, u32[]{:S(2)}) collective-permute-start(bf16[256,1792]{1,0:T(8,128)(2,1)S(1)} %slice.114.own), channel_id=1, source_target_pairs={{5,3},{3,5},{4,2},{2,4},{13,11},{11,13},{12,10},{10,12},{21,19},{1... | collective-permute-start | bytes 2752520 | tf_op jit(solution)/shard_map/ppermute | solution.py:34
  206.5 64.8 %collective-permute-start.7 = (bf16[256,1792]{1,0:T(8,128)(2,1)S(1)}, bf16[256,1792]{1,0:T(8,128)(2,1)S(1)}, u32[]{:S(2)}, u32[]{:S(2)}) collective-permute-start(bf16[256,1792]{1,0:T(8,128)(2,1)S(1)} %slice.114.own), channel_id=1, source_target_pairs={{0,1},{1,0},{6,7},{7,6},{4,3},{3,4},{5,2},{2,5},{8,9},{9,8},{14,15... | collective-permute-start | bytes 2752520 | tf_op jit(solution)/shard_map/ppermute | solution.py:34
  210.9 102.2 %collective-permute-start.14 = (bf16[256,2688]{1,0:T(8,128)(2,1)}, bf16[256,2688]{1,0:T(8,128)(2,1)}, u32[]{:S(2)}, u32[]{:S(2)}) collective-permute-start(bf16[256,2688]{1,0:T(8,128)(2,1)} %get-tuple-element.43.own), channel_id=1, source_target_pairs={{5,3},{3,5},{4,2},{2,4},{13,11},{11,13},{12,10},{10,12},{21,19},{1... | collective-permute-start | bytes 4128776 | tf_op jit(solution)/shard_map/ppermute | solution.py:34
  212.6 101.7 %collective-permute-start.12 = (bf16[256,2688]{1,0:T(8,128)(2,1)}, bf16[256,2688]{1,0:T(8,128)(2,1)}, u32[]{:S(2)}, u32[]{:S(2)}) collective-permute-start(bf16[256,2688]{1,0:T(8,128)(2,1)} %get-tuple-element.43.own), channel_id=1, source_target_pairs={{0,1},{1,0},{6,7},{7,6},{4,3},{3,4},{5,2},{2,5},{8,9},{9,8},{14,15... | collective-permute-start | bytes 4128776 | tf_op jit(solution)/shard_map/ppermute | solution.py:34
  212.6 92.8 %collective-permute-start.6 = (bf16[256,1792]{1,0:T(8,128)(2,1)S(1)}, bf16[256,1792]{1,0:T(8,128)(2,1)S(1)}, u32[]{:S(2)}, u32[]{:S(2)}) collective-permute-start(bf16[256,1792]{1,0:T(8,128)(2,1)S(1)} %slice.114.own), channel_id=1, source_target_pairs={{0,4},{1,5},{6,2},{7,3},{8,12},{9,13},{14,10},{15,11},{16,20},{17,... | collective-permute-start | bytes 2752520 | tf_op jit(solution)/shard_map/ppermute | solution.py:34
  271.3 37.1 %collective-permute-start.10 = (bf16[256,1792]{1,0:T(8,128)(2,1)S(1)}, bf16[256,1792]{1,0:T(8,128)(2,1)S(1)}, u32[]{:S(2)}, u32[]{:S(2)}) collective-permute-start(bf16[256,1792]{1,0:T(8,128)(2,1)S(1)} %collective-permute-done.9.far), channel_id=1, source_target_pairs={{4,0},{5,1},{2,6},{3,7},{12,8},{13,9},{10,14},{11,15},{20,16},{21,... | collective-permute-start | bytes 2752520 | tf_op jit(solution)/shard_map/ppermute | solution.py:34
  272.6 35.8 %collective-permute-start.8 = (bf16[256,1792]{1,0:T(8,128)(2,1)S(1)}, bf16[256,1792]{1,0:T(8,128)(2,1)S(1)}, u32[]{:S(2)}, u32[]{:S(2)}) collective-permute-start(bf16[256,1792]{1,0:T(8,128)(2,1)S(1)} %collective-permute-done.7.near), channel_id=1, source_target_pairs={{0,4},{4,0},{1,5},{5,1},{2,6},{6,2},{3,7},{7,3},{8,12},{12,8},{9,1... | collective-permute-start | bytes 2752520 | tf_op jit(solution)/shard_map/ppermute | solution.py:34
  305.4 18.1 %collective-permute-start.11 = (bf16[256,2688]{1,0:T(8,128)(2,1)}, bf16[256,2688]{1,0:T(8,128)(2,1)}, u32[]{:S(2)}, u32[]{:S(2)}) collective-permute-start(bf16[256,2688]{1,0:T(8,128)(2,1)} %get-tuple-element.43.own), channel_id=1, source_target_pairs={{0,4},{1,5},{6,2},{7,3},{8,12},{9,13},{14,10},{15,11},{16,20},{17,... | collective-permute-start | bytes 4128776 | tf_op jit(solution)/shard_map/ppermute | solution.py:34
  313.0 14.7 %collective-permute-start.15 = (bf16[256,2688]{1,0:T(8,128)(2,1)}, bf16[256,2688]{1,0:T(8,128)(2,1)}, u32[]{:S(2)}, u32[]{:S(2)}) collective-permute-start(bf16[256,2688]{1,0:T(8,128)(2,1)} %collective-permute-done.14.far), channel_id=1, source_target_pairs={{4,0},{5,1},{2,6},{3,7},{12,8},{13,9},{10,14},{11,15},{20,16},{21,... | collective-permute-start | bytes 4128776 | tf_op jit(solution)/shard_map/ppermute | solution.py:34
  314.3 13.4 %collective-permute-start.13 = (bf16[256,2688]{1,0:T(8,128)(2,1)}, bf16[256,2688]{1,0:T(8,128)(2,1)}, u32[]{:S(2)}, u32[]{:S(2)}) collective-permute-start(bf16[256,2688]{1,0:T(8,128)(2,1)} %collective-permute-done.12.near), channel_id=1, source_target_pairs={{0,4},{4,0},{1,5},{5,1},{2,6},{6,2},{3,7},{7,3},{8,12},{12,8},{9,1... | collective-permute-start | bytes 4128776 | tf_op jit(solution)/shard_map/ppermute | solution.py:34
  316.5 19.9 %collective-permute-start.21 = (bf16[256,2688]{1,0:T(8,128)(2,1)S(1)}, bf16[256,2688]{1,0:T(8,128)(2,1)S(1)}, u32[]{:S(2)}, u32[]{:S(2)}) collective-permute-start(bf16[256,2688]{1,0:T(8,128)(2,1)S(1)} %get-tuple-element.50.own), channel_id=1, source_target_pairs={{5,3},{3,5},{4,2},{2,4},{13,11},{11,13},{12,10},{10,12},{21,19},{1... | collective-permute-start | bytes 4128776 | tf_op jit(solution)/shard_map/ppermute | solution.py:34
  317.3 32.3 %collective-permute-start.19 = (bf16[256,2688]{1,0:T(8,128)(2,1)S(1)}, bf16[256,2688]{1,0:T(8,128)(2,1)}, u32[]{:S(2)}, u32[]{:S(2)}) collective-permute-start(bf16[256,2688]{1,0:T(8,128)(2,1)S(1)} %get-tuple-element.50.own), channel_id=1, source_target_pairs={{0,1},{1,0},{6,7},{7,6},{4,3},{3,4},{5,2},{2,5},{8,9},{9,8},{14,15... | collective-permute-start | bytes 4128776 | tf_op jit(solution)/shard_map/ppermute | solution.py:34
  317.4 36.3 %all-to-all-start.3 = ((bf16[32,16,1792]{2,1,0:T(8,128)(2,1)}), bf16[32,16,1792]{2,1,0:T(8,128)(2,1)}, u32[]{:S(2)}, u32[]{:S(2)}) async-start(bf16[32,16,1792]{2,1,0:T(8,128)(2,1)} %get-tuple-element.41), calls=%async_computation.3 | async-start | bytes 3670016 | tf_op jit(solution)/shard_map/all_to_all | solution.py:231
  323.5 34.5 %collective-permute-start.18 = (bf16[256,2688]{1,0:T(8,128)(2,1)S(1)}, bf16[256,2688]{1,0:T(8,128)(2,1)}, u32[]{:S(2)}, u32[]{:S(2)}) collective-permute-start(bf16[256,2688]{1,0:T(8,128)(2,1)S(1)} %get-tuple-element.50.own), channel_id=1, source_target_pairs={{0,4},{1,5},{6,2},{7,3},{8,12},{9,13},{14,10},{15,11},{16,20},{17,... | collective-permute-start | bytes 4128776 | tf_op jit(solution)/shard_map/ppermute | solution.py:34
  327.8 1.2 copy-start.1
  336.4 21.6 %collective-permute-start.22 = (bf16[256,2688]{1,0:T(8,128)(2,1)S(1)}, bf16[256,2688]{1,0:T(8,128)(2,1)}, u32[]{:S(2)}, u32[]{:S(2)}) collective-permute-start(bf16[256,2688]{1,0:T(8,128)(2,1)S(1)} %collective-permute-done.21.far), channel_id=1, source_target_pairs={{4,0},{5,1},{2,6},{3,7},{12,8},{13,9},{10,14},{11,15},{20,16},{21,... | collective-permute-start | bytes 4128776 | tf_op jit(solution)/shard_map/ppermute | solution.py:34
  349.6 8.5 %collective-permute-start.20 = (bf16[256,2688]{1,0:T(8,128)(2,1)}, bf16[256,2688]{1,0:T(8,128)(2,1)}, u32[]{:S(2)}, u32[]{:S(2)}) collective-permute-start(bf16[256,2688]{1,0:T(8,128)(2,1)} %collective-permute-done.19.near), channel_id=1, source_target_pairs={{0,4},{4,0},{1,5},{5,1},{2,6},{6,2},{3,7},{7,3},{8,12},{12,8},{9,1... | collective-permute-start | bytes 4128776 | tf_op jit(solution)/shard_map/ppermute | solution.py:34
  353.7 23.9 %all-to-all-start.4 = ((bf16[16,8,4480]{2,1,0:T(8,128)(2,1)}), bf16[16,8,4480]{2,1,0:T(8,128)(2,1)}, u32[]{:S(2)}, u32[]{:S(2)}) async-start(bf16[16,8,4480]{2,1,0:T(8,128)(2,1)} %bitcast.80), calls=%async_computation.4 | async-start | bytes 2293760 | tf_op jit(solution)/shard_map/all_to_all | solution.py:235
  358.1 1.2 copy-start.2
  377.5 4.3 copy-start.10
  377.5 4.3 copy-start.11
  377.5 4.3 copy-start.14
  377.5 41.7 %all-to-all-start.7 = ((bf16[32,16,2688]{2,1,0:T(8,128)(2,1)}), bf16[32,16,2688]{2,1,0:T(8,128)(2,1)S(1)}, u32[]{:S(2)}, u32[]{:S(2)}) async-start(bf16[32,16,2688]{2,1,0:T(8,128)(2,1)} %bitcast.36), calls=%async_computation.7 | async-start | bytes 5505024 | tf_op jit(solution)/shard_map/all_to_all | solution.py:231
  419.2 42.3 %all-to-all-start.5 = ((bf16[32,16,2688]{2,1,0:T(8,128)(2,1)}), bf16[32,16,2688]{2,1,0:T(8,128)(2,1)}, u32[]{:S(2)}, u32[]{:S(2)}) async-start(bf16[32,16,2688]{2,1,0:T(8,128)(2,1)} %bitcast.31), calls=%async_computation.5 | async-start | bytes 5505024 | tf_op jit(solution)/shard_map/all_to_all | solution.py:231
  428.1 9.4 %collective-permute-start.16 = (bf16[64,1792]{1,0:T(8,128)(2,1)S(1)}, bf16[64,1792]{1,0:T(8,128)(2,1)S(1)}, u32[]{:S(2)}, u32[]{:S(2)}) collective-permute-start(bf16[64,1792]{1,0:T(8,128)(2,1)S(1)} %slice.160), channel_id=1, source_target_pairs={{0,3},{3,0},{1,2},{2,1},{4,7},{7,4},{5,6},{6,5},{8,11},{11,8},{9,1... | collective-permute-start | bytes 688136 | tf_op jit(solution)/shard_map/ppermute | solution.py:186
  467.4 16.0 %all-to-all-start.6 = ((bf16[16,8,2688]{2,1,0:T(8,128)(2,1)}), bf16[16,8,2688]{2,1,0:T(8,128)(2,1)S(1)}, u32[]{:S(2)}, u32[]{:S(2)}) async-start(bf16[16,8,2688]{2,1,0:T(8,128)(2,1)} %bitcast.34), calls=%async_computation.6 | async-start | bytes 1376256 | tf_op jit(solution)/shard_map/all_to_all | solution.py:235
  471.0 12.4 %copy-start.3 = (f32[256,2688]{1,0:T(8,128)S(1)}, f32[256,2688]{1,0:T(8,128)}, u32[]{:S(2)}) copy-start(f32[256,2688]{1,0:T(8,128)} %fusion.14) | copy-start | bytes 8257540
  473.1 1.1 copy-start.5
  475.0 12.6 %collective-permute-start.17 = (bf16[64,2688]{1,0:T(8,128)(2,1)}, bf16[64,2688]{1,0:T(8,128)(2,1)}, u32[]{:S(2)}, u32[]{:S(2)}) collective-permute-start(bf16[64,2688]{1,0:T(8,128)(2,1)} %slice.159), channel_id=1, source_target_pairs={{0,3},{3,0},{1,2},{2,1},{4,7},{7,4},{5,6},{6,5},{8,11},{11,8},{9,1... | collective-permute-start | bytes 1032200 | tf_op jit(solution)/shard_map/ppermute | solution.py:186
  484.0 3.6 copy-start.6
  484.2 9.5 %copy-start.9 = (bf16[64,1792]{1,0:T(8,128)(2,1)S(1)}, bf16[64,1792]{1,0:T(8,128)(2,1)}, u32[]{:S(2)}) copy-start(bf16[64,1792]{1,0:T(8,128)(2,1)} %fusion.10) | copy-start | bytes 688132
  484.2 9.4 %collective-permute-start.23 = (bf16[64,2688]{1,0:T(8,128)(2,1)S(1)}, bf16[64,2688]{1,0:T(8,128)(2,1)S(1)}, u32[]{:S(2)}, u32[]{:S(2)}) collective-permute-start(bf16[64,2688]{1,0:T(8,128)(2,1)S(1)} %slice.158), channel_id=1, source_target_pairs={{0,3},{3,0},{1,2},{2,1},{4,7},{7,4},{5,6},{6,5},{8,11},{11,8},{9,1... | collective-permute-start | bytes 1032200 | tf_op jit(solution)/shard_map/ppermute | solution.py:186

commit v2 on v1

--- a/solution.py
+++ b/solution.py
@@ -24,6 +24,7 @@
 TO_HOME = [(b, a) for a, b in FROM_HOME]
 STEPS = (1792, 2688, 2688)
 QUARTER = 256
+HALF = 128
 MAIN = 256
 REST = 128
 TILE = 896
@@ -38,85 +39,74 @@
     return lax.optimization_barrier((value, *earlier))[0]
 
 
-def share(own, near, far, near_after, far_after):
-    across = along(after(near, near_after), SIBLING)
-    brought = along(after(far, far_after), TO_HOME)
-    return own, along(own, FROM_HOME), near, across, brought, far
+def share(near, far, earlier):
+    across = along(after(near, earlier), SIBLING)
+    brought = along(after(far, earlier), TO_HOME)
+    return near, across, brought, far
 
 
 def pick_block(flag, wanted, block):
     return jnp.where(flag[0] == wanted, block, 0)
 
 
-def hidden_kernel(flag, *refs, quarters):
-    mine, theirs, rest = refs[:3]
-    panels, out, gate_sum, up_sum = refs[3:-3], refs[-3], refs[-2], refs[-1]
+def hidden_kernel(flag, mine, theirs, rest, *refs, kinds):
+    panels, out, total = refs[:-2], refs[-2], refs[-1]
     part = pl.program_id(0)
 
     @pl.when(part == 0)
     def _():
-        gate_sum[...] = jnp.zeros_like(gate_sum)
-        up_sum[...] = jnp.zeros_like(up_sum)
-
-    def add(total, place, weights):
+        total[...] = jnp.zeros_like(total)
+
+    at = 0
+    for unit, kind in enumerate(kinds):
+        panel = panels[at][...]
+        if kind == 2:
+            panel = jnp.where(flag[0] == 1, panel, panels[at + 1][...])
         for rows, first in ((mine, 0), (theirs, MAIN), (rest, 2 * MAIN)):
-            number = rows.shape[0]
-            total[pl.ds(first, number), pl.ds(place * QUARTER, QUARTER)] += lax.dot_general(
-                rows[...], weights, (((1,), (1,)), ((), ())), preferred_element_type=jnp.float32
+            total[pl.ds(first, rows.shape[0]), pl.ds(unit * 2 * HALF, 2 * HALF)] += lax.dot_general(
+                rows[...], panel, (((1,), (1,)), ((), ())), preferred_element_type=jnp.float32
             )
-
-    at = 0
-    for place, kind in enumerate(quarters):
-        if kind == 1:
-            both = panels[at][...]
-        else:
-            both = jnp.where(flag[0] == 1, panels[at][...], panels[at + 1][...])
-        add(gate_sum, place, both[:QUARTER])
-        add(up_sum, place, both[QUARTER:])
         at += kind
 
     @pl.when(part == pl.num_programs(0) - 1)
     def _():
-        gate = gate_sum[...]
-        out[...] = (gate / (1.0 + jnp.exp(-gate)) * up_sum[...]).astype(out.dtype)
-
-
-def hidden_units(flag, mine, theirs, rest, quarters):
-    width = rest.shape[1]
-    count = len(quarters)
-    kinds = tuple(len(quarter) for quarter in quarters)
-    specs = [
-        pl.BlockSpec((MAIN, DEEP), lambda i, f: (0, i)),
-        pl.BlockSpec((MAIN, DEEP), lambda i, f: (0, i)),
-        pl.BlockSpec((REST, DEEP), lambda i, f: (0, i)),
-    ]
+        for unit in range(len(kinds)):
+            gate = total[:, pl.ds(unit * 2 * HALF, HALF)]
+            upper = total[:, pl.ds(unit * 2 * HALF + HALF, HALF)]
+            hidden = gate / (1.0 + jnp.exp(-gate)) * upper
+            out[:, pl.ds(unit * HALF, HALF)] = hidden.astype(out.dtype)
+
+
+def hidden_units(flag, mine, theirs, rest, units):
+    rows, width = 2 * MAIN + REST, rest.shape[1]
+    kinds = tuple(len(unit) for unit in units)
+    specs = [pl.BlockSpec((part.shape[0], DEEP), lambda i, f: (0, i)) for part in (mine, theirs, rest)]
     operands = [mine, theirs, rest]
-    for quarter in quarters:
-        for place, both in enumerate(quarter):
-            if len(quarter) == 1:
-                spec = pl.BlockSpec((2 * QUARTER, DEEP), lambda i, f: (0, i))
+    for unit in units:
+        for place, panel in enumerate(unit):
+            if len(unit) == 1:
+                spec = pl.BlockSpec((2 * HALF, DEEP), lambda i, f: (0, i))
             else:
                 spec = pl.BlockSpec(
-                    (2 * QUARTER, DEEP), lambda i, f, w=1 - place: (0, pick_block(f, w, i))
+                    (2 * HALF, DEEP), lambda i, f, w=1 - place: (0, pick_block(f, w, i))
                 )
             specs.append(spec)
-            operands.append(both)
-    rows = 2 * MAIN + REST
+            operands.append(panel)
     return pl.pallas_call(
-        functools.partial(hidden_kernel, quarters=kinds),
+        functools.partial(hidden_kernel, kinds=kinds),
         grid_spec=pltpu.PrefetchScalarGridSpec(
             num_scalar_prefetch=1,
             grid=(width // DEEP,),
             in_specs=specs,
-            out_specs=pl.BlockSpec((rows, count * QUARTER), lambda i, f: (0, 0)),
-            scratch_shapes=[pltpu.VMEM((rows, count * QUARTER), jnp.float32)] * 2,
-        ),
-        out_shape=jax.ShapeDtypeStruct((rows, count * QUARTER), jnp.bfloat16),
+            out_specs=pl.BlockSpec((rows, len(units) * HALF), lambda i, f: (0, 0)),
+            scratch_shapes=[pltpu.VMEM((rows, len(units) * 2 * HALF), jnp.float32)],
+        ),
+        out_shape=jax.ShapeDtypeStruct((rows, len(units) * HALF), jnp.bfloat16),
         compiler_params=pltpu.CompilerParams(vmem_limit_bytes=48 * 2**20),
         cost_estimate=pl.CostEstimate(
-            flops=4 * rows * width * count * QUARTER,
-            bytes_accessed=2 * width * (rows + 2 * count * QUARTER),
-            transcendentals=rows * count * QUARTER,
+            flops=4 * rows * width * len(units) * HALF,
+            bytes_accessed=2 * width * (rows + 2 * len(units) * HALF),
+            transcendentals=rows * len(units) * HALF,
         ),
     )(flag, *operands)
 
@@ -126,8 +116,11 @@
     panels = (
         (first[:, :QUARTER], jnp.where(home, own[...], copied[...])),
         (first[:, QUARTER : 2 * QUARTER], near[...]),
-        (first[:, 2 * QUARTER :], across[...]),
-        (last[...], jnp.where(home, brought[...], far[...])),
+        (first[:, 2 * QUARTER : 3 * QUARTER], across[...]),
+        (
+            jnp.concatenate([first[:, 3 * QUARTER :], last[...]], axis=1),
+            jnp.where(home, brought[...], far[...]),
+        ),
     )
     total = None
     for hidden, weights in panels:
@@ -139,14 +132,16 @@
     out_rest[...] = total[2 * MAIN :]
 
 
-def down_rows(flag, first, last, panels):
+def down_rows(flag, first, last, whole, at, panels):
     step = panels[0].shape[1]
     rows = 2 * MAIN + REST
 
-    def panel(wanted=None):
+    def panel(wanted=None, skip=0):
         if wanted is None:
             return pl.BlockSpec((QUARTER, TILE), lambda i, f: (0, i))
-        return pl.BlockSpec((QUARTER, TILE), lambda i, f: (0, pick_block(f, wanted, i)))
+        return pl.BlockSpec(
+            (QUARTER, TILE), lambda i, f: (0, pick_block(f, wanted, skip // TILE + i))
+        )
 
     main, tail = pl.pallas_call(
         down_kernel,
@@ -156,8 +151,8 @@
             in_specs=[
                 pl.BlockSpec(first.shape, lambda i, f: (0, 0)),
                 pl.BlockSpec(last.shape, lambda i, f: (0, 0)),
-                panel(1),
-                panel(0),
+                panel(1, at),
+                panel(0, at),
                 panel(),
                 panel(),
                 panel(1),
@@ -178,7 +173,7 @@
             bytes_accessed=2 * (4 * QUARTER * step + rows * (4 * QUARTER + step)),
             transcendentals=0,
         ),
-    )(flag, first, last, *panels)
+    )(flag, first, last, *whole, *panels)
     return main.reshape(2 * MAIN, step), tail
 
 
@@ -242,9 +237,13 @@
     ids, gate, low = (extra[:, at : at + 8] for at in (0, 8, 16))
     other_routes = jnp.concatenate([ids, gate + low], axis=1)
 
-    gate_up = jnp.concatenate([after(gate_weight[0], other), up_weight[0]], axis=0)
-    near = along(gate_up, NEXT)
-    far = along(gate_up, FAR)
+    gate, upper = after(gate_weight[0], other), up_weight[0]
+    owns = [
+        jnp.concatenate([part[at : at + HALF] for part in (gate, upper)], axis=0)
+        for at in (0, HALF)
+    ]
+    nears = [along(own, NEXT) for own in owns]
+    fars = [along(owns[0], FAR), along(after(owns[1], *nears), FAR)]
 
     pick, other_rest, mix_other, mix_other_rest = slots(other_routes, 1)
     theirs = exchange_main(after(rows_of(pick, other), mine))
@@ -252,7 +251,9 @@
         jnp.concatenate([pick_rest, other_rest], axis=2), jnp.concatenate([tokens, other], axis=0)
     )
     rest = exchange_rest(after(rest, theirs))
-    copied, across = along(gate_up, FROM_HOME), along(after(near, theirs), SIBLING)
+    copied = [along(own, FROM_HOME) for own in owns]
+    across = [along(after(near, theirs), SIBLING) for near in nears]
+    brought_0 = along(after(fars[0], theirs), TO_HOME)
 
     def halves(*parts):
         part = jnp.concatenate([part.reshape(tok_rows, -1) for part in parts], axis=0)
@@ -262,20 +263,23 @@
     mix_main, mix_rest = halves(mix_own, mix_other), halves(mix_own_rest, mix_other_rest)
     count = 2 * tok_rows
 
-    def columns(number, *earlier):
-        at = sum(STEPS[:number])
-        own = after(down_weight[0][:, at : at + STEPS[number]], *earlier)
-        return own, along(own, NEXT), along(own, FAR)
-
-    down_0 = columns(0, near)
-    first = hidden_units(flag, mine, theirs, rest, [(gate_up, copied), (near,), (across,)])
-    brought = along(after(far, first), TO_HOME)
-    down_1 = columns(1, far, first)
-    last = hidden_units(flag, after(mine, first), theirs, rest, [(brought, far)])
-    result_0 = down_rows(flag, first, last, share(*down_0, first, first))
-    down_2 = columns(2, down_0[2], result_0[0])
-    result_1 = down_rows(flag, first, last, share(*down_1, result_0[0], result_0[0]))
-    result_2 = down_rows(flag, first, last, share(*down_2, result_1[0], result_1[0]))
+    def columns(at, step, *earlier):
+        own = after(down_weight[0][:, at : at + step], *earlier)
+        return along(own, NEXT), along(own, FAR)
+
+    whole = down_weight[0], along(after(down_weight[0], *copied), FROM_HOME)
+    down_0 = columns(0, STEPS[0], *nears)
+    units = [*zip(owns, copied, strict=True), *zip(nears), *zip(across), (brought_0, fars[0])]
+    first = hidden_units(flag, after(mine, whole[1]), theirs, rest, units)
+    brought_1 = along(after(fars[1], first), TO_HOME)
+    down_1 = columns(STEPS[0], STEPS[1], fars[1], first)
+    last = hidden_units(flag, after(mine, first), theirs, rest, [(brought_1, fars[1])])
+    result_0 = down_rows(flag, first, last, whole, 0, share(*down_0, first))
+    down_2 = columns(STEPS[0] + STEPS[1], STEPS[2], down_0[1], result_0[0])
+    result_1 = down_rows(flag, first, last, whole, STEPS[0], share(*down_1, result_0[0]))
+    result_2 = down_rows(
+        flag, first, last, whole, STEPS[0] + STEPS[1], share(*down_2, result_1[0])
+    )
     mains, rests = zip(result_0, result_1, result_2, strict=True)
     early = jnp.concatenate(rests[:2], axis=1)
     back_0 = exchange_main(mains[0])

time: 496 us -> 462 us (0.931)
  starting transfers between devices: 170 us -> 114 us
  local copies, waits for them, and re-layouts: 6.15 us -> 19 us
  waiting for transfers between devices: 226 us -> 238 us
    ppermute x20 -> x23, waiting for transfers between devices: 11.9 us -> 105 us  [along(): return lax.ppermute(value, COL, pairs)]
    all_to_all x5, waiting for transfers between devices: 144 us -> 74.4 us  [exchange_main(): return lax.all_to_all(parts, EXP, 0, 0, tiled=True).reshape(rows.shape)]
    ppermute x20 -> x23, starting transfers between devices: 114 us -> 54.2 us  [along(): return lax.ppermute(value, COL, pairs)]
    unnamed x31 -> x41, local copies, waits for them, and re-layouts: 3.64 us -> 13.4 us
    ppermute x4, waiting for transfers between devices: 27.6 us -> 18.3 us  [pair_exchange(): return lax.ppermute(value, ('zh', 'zl'), PAIR)]
  transfers between devices with their start and end apart: 32 -> 35, of which waited for: 11 -> 12; matrix products, arithmetic and copies ran while one was open for 5% -> 7% of each run, Pallas kernels for 11% -> 12%
where the time goes in v2:
time: 462 us; the launch traced here: 461 us
  waiting for transfers between devices  238 us (52%)
  starting transfers between devices  114 us (25%)
  Pallas kernels  53.6 us (12%)
  matrix products  20.6 us (4%)
  local copies, waits for them, and re-layouts  19 us (4%)
  other arithmetic  14.2 us (3%)
    ppermute x23, waiting for transfers between devices, along(): return lax.ppermute(value, COL, pairs)  105 us
    all_to_all x5, waiting for transfers between devices, exchange_main(): return lax.all_to_all(parts, EXP, 0, 0, tiled=True).reshape(rows.shape)  74.4 us
    ppermute x23, starting transfers between devices, along(): return lax.ppermute(value, COL, pairs)  54.2 us
    all_to_all x3, waiting for transfers between devices, exchange_rest(): lax.all_to_all(parts, ('y', 'x'), 0, 0, tiled=True).reshape(rows.shape)  40.6 us
    pallas_call x2, Pallas kernels, hidden_units(): pl.pallas_call(functools.partial(hidden_kernel, kinds=kinds), grid_spec=p...  33.9 us
    all_to_all x5, starting transfers between devices, exchange_main(): return lax.all_to_all(parts, EXP, 0, 0, tiled=True).reshape(rows.shape)  27.9 us
    pallas_call x3, Pallas kernels, down_rows(): pl.pallas_call(down_kernel, grid_spec=pltpu.PrefetchScalarGridSpec(num_sc...  19.7 us
    ppermute x4, waiting for transfers between devices, pair_exchange(): return lax.ppermute(value, ('zh', 'zl'), PAIR)  18.3 us
  transfers between devices with their start and end apart: 35, of which 12 were waited for; matrix products, arithmetic and copies ran while one was open for 7% of the time, Pallas kernels for 12%

profile of v2, /device:TPU:0, one launch (start us, length us, event | category | flops | bytes accessed | tf_op | source)
XLA Modules:
  0.0 460.7 jit_solution(4316537405617586043)
XLA Ops:
  2.8 4.2 collective-permute-start
  7.5 2.9 convolution_convert_fusion.1
  10.4 7.4 %all-to-all-start = ((bf16[32,8,7168]{2,1,0:T(8,128)(2,1)}), bf16[32,8,7168]{2,1,0:T(8,128)(2,1)}, u32[]{:S(2)}, u32[]{:S(2)}) async-start(bf16[32,8,7168]{2,1,0:T(8,128)(2,1)} %bitcast.85), calls=%async_computation | async-start | bytes 7340032 | tf_op jit(solution)/shard_map/all_to_all | solution.py:226
  17.8 2.4 slice_bitcast_fusion
  20.3 7.4 %collective-permute-done = bf16[64,7296]{1,0:T(8,128)(2,1)S(1)} collective-permute-done((bf16[64,7296]{1,0:T(8,128)(2,1)S(1)}, bf16[64,7296]{1,0:T(8,128)(2,1)S(1)}, u32[]{:S(2)}, u32[]{:S(2)}) %collective-permute-start) | collective-permute-done | bytes 933920 | tf_op jit(solution)/shard_map/ppermute | solution.py:181
  28.0 2.1 pad_maximum_fusion.refs_0_
  30.1 2.5 collective-permute-start.8
  32.6 6.3 %collective-permute-start.1 = (bf16[256,7168]{1,0:T(8,128)(2,1)}, bf16[256,7168]{1,0:T(8,128)(2,1)}, u32[]{:S(2)}, u32[]{:S(2)}) collective-permute-start(bf16[256,7168]{1,0:T(8,128)(2,1)} %pad_maximum_fusion.refs_0_), channel_id=1, source_target_pairs={{0,4},{1,5},{6,2},{7,3},{8,12},{9,13},{14,10},{15,11},{16,20},{17,... | collective-permute-start | bytes 11010056 | tf_op jit(solution)/shard_map/ppermute | solution.py:35
  38.8 2.1 pad_maximum_fusion.1.refs_2_
  41.8 3.2 collective-permute-start.2
  45.5 2.9 convolution_convert_fusion
  48.5 17.0 %all-to-all-done = bf16[32,8,7168]{2,1,0:T(8,128)(2,1)} async-done(((bf16[32,8,7168]{2,1,0:T(8,128)(2,1)}), bf16[32,8,7168]{2,1,0:T(8,128)(2,1)}, u32[]{:S(2)}, u32[]{:S(2)}) %all-to-all-start) | async-done | bytes 3670048 | tf_op jit(solution)/shard_map/all_to_all | solution.py:226
  65.5 5.0 %all-to-all-start.1 = ((bf16[32,8,7168]{2,1,0:T(8,128)(2,1)}), bf16[32,8,7168]{2,1,0:T(8,128)(2,1)}, u32[]{:S(2)}, u32[]{:S(2)}) async-start(bf16[32,8,7168]{2,1,0:T(8,128)(2,1)} %bitcast.86), calls=%async_computation.1 | async-start | bytes 7340032 | tf_op jit(solution)/shard_map/all_to_all | solution.py:226
  70.5 3.8 collective-permute-start.3
  74.3 77.6 %collective-permute-done.5.refs_5_ = bf16[256,7168]{1,0:T(8,128)(2,1)} collective-permute-done((bf16[256,7168]{1,0:T(8,128)(2,1)}, bf16[256,7168]{1,0:T(8,128)(2,1)}, u32[]{:S(2)}, u32[]{:S(2)}) %collective-permute-start.5) | collective-permute-done | bytes 3670048 | tf_op jit(solution)/shard_map/ppermute | solution.py:35
  154.2 2.5 collective-permute-start.10
  158.8 7.0 %all-to-all-start.2 = ((bf16[16,8,7168]{2,1,0:T(8,128)(2,1)}), bf16[16,8,7168]{2,1,0:T(8,128)(2,1)S(1)}, u32[]{:S(2)}, u32[]{:S(2)}) async-start(bf16[16,8,7168]{2,1,0:T(8,128)(2,1)} %bitcast.88), calls=%async_computation.2 | async-start | bytes 3670016 | tf_op jit(solution)/shard_map/all_to_all | solution.py:230
  165.9 27.6 %all-to-all-done.2 = bf16[16,8,7168]{2,1,0:T(8,128)(2,1)S(1)} async-done(((bf16[16,8,7168]{2,1,0:T(8,128)(2,1)}), bf16[16,8,7168]{2,1,0:T(8,128)(2,1)S(1)}, u32[]{:S(2)}, u32[]{:S(2)}) %all-to-all-start.2) | async-done | bytes 1835040 | tf_op jit(solution)/shard_map/all_to_all | solution.py:230
  193.5 26.9 %shard_map.64.first = bf16[640,896]{1,0:T(8,128)(2,1)S(1)} custom-call(s32[1]{0:T(128)} %bitcast.4.flag, bf16[256,7168]{1,0:T(8,128)(2,1)} %bitcast.6.mine, bf16[256,7168]{1,0:T(8,128)(2,1)} %bitcast.14.theirs, bf16[128,7168]{1,0:T(8,128)(2,1)S(1)} %bitcast.83, bf16[256,7168]{1,0:T(8,128)(2,1)} %pad_maximum_fusion.refs_0_, ...), custom_call_target="tpu_custom_call" | custom-call | flops 16441671680 | bytes 34865152 | tf_op jit(solution)/shard_map/pallas_call | solution.py:95
  229.5 12.7 %collective-permute-done.12.near = bf16[256,1792]{1,0:T(8,128)(2,1)S(1)} collective-permute-done((bf16[256,1792]{1,0:T(8,128)(2,1)S(1)}, bf16[256,1792]{1,0:T(8,128)(2,1)S(1)}, u32[]{:S(2)}, u32[]{:S(2)}) %collective-permute-start.12) | collective-permute-done | bytes 917536 | tf_op jit(solution)/shard_map/ppermute | solution.py:35
  242.2 10.4 %collective-permute-start.13 = (bf16[256,1792]{1,0:T(8,128)(2,1)S(1)}, bf16[256,1792]{1,0:T(8,128)(2,1)S(1)}, u32[]{:S(2)}, u32[]{:S(2)}) collective-permute-start(bf16[256,1792]{1,0:T(8,128)(2,1)S(1)} %collective-permute-done.12.near), channel_id=1, source_target_pairs={{0,4},{4,0},{1,5},{5,1},{2,6},{6,2},{3,7},{7,3},{8,12},{12,8},{9,1... | collective-permute-start | bytes 2752520 | tf_op jit(solution)/shard_map/ppermute | solution.py:35
  252.6 7.0 %shard_map.65.last = bf16[640,128]{1,0:T(8,128)(2,1)S(1)} custom-call(s32[1]{0:T(128)} %bitcast.4.flag, bf16[256,7168]{1,0:T(8,128)(2,1)} %bitcast.6.mine, bf16[256,7168]{1,0:T(8,128)(2,1)} %bitcast.14.theirs, bf16[128,7168]{1,0:T(8,128)(2,1)S(1)} %bitcast.84, bf16[256,7168]{1,0:T(8,128)(2,1)} %collective-permute-done.11.refs_0_, ...), custom_call_target="tpu_custom_call" | custom-call | flops 2348810240 | bytes 12845056 | tf_op jit(solution)/shard_map/pallas_call | solution.py:95
  266.3 5.2 %shard_map.66 = (bf16[32,16,1792]{2,1,0:T(8,128)(2,1)}, bf16[128,1792]{1,0:T(8,128)(2,1)S(1)}) custom-call(s32[1]{0:T(128)} %bitcast.4.flag, bf16[640,896]{1,0:T(8,128)(2,1)S(1)} %shard_map.64.first, bf16[640,128]{1,0:T(8,128)(2,1)S(1)} %shard_map.65.last, bf16[256,7168]{1,0:T(8,128)(2,1)S(1)} %bitcast.80, bf16[256,7168]{1,0:T(8,128)(2,1)} %collective-permute-done.3.copied, ...), custom_call_target="tpu_custom_call" | custom-call | flops 2348810240 | bytes 7274496 | tf_op jit(solution)/shard_map/pallas_call | solution.py:146
  272.7 7.8 %collective-permute-start.17 = (bf16[256,2688]{1,0:T(8,128)(2,1)}, bf16[256,2688]{1,0:T(8,128)(2,1)}, u32[]{:S(2)}, u32[]{:S(2)}) collective-permute-start(bf16[256,2688]{1,0:T(8,128)(2,1)} %collective-permute-done.16.near), channel_id=1, source_target_pairs={{0,4},{4,0},{1,5},{5,1},{2,6},{6,2},{3,7},{7,3},{8,12},{12,8},{9,1... | collective-permute-start | bytes 4128776 | tf_op jit(solution)/shard_map/ppermute | solution.py:35
  281.7 6.6 %all-to-all-start.3 = ((bf16[32,16,1792]{2,1,0:T(8,128)(2,1)}), bf16[32,16,1792]{2,1,0:T(8,128)(2,1)}, u32[]{:S(2)}, u32[]{:S(2)}) async-start(bf16[32,16,1792]{2,1,0:T(8,128)(2,1)} %get-tuple-element.51), calls=%async_computation.3 | async-start | bytes 3670016 | tf_op jit(solution)/shard_map/all_to_all | solution.py:226
  288.3 2.0 copy-done.1
  290.4 7.4 %shard_map.67 = (bf16[32,16,2688]{2,1,0:T(8,128)(2,1)}, bf16[128,2688]{1,0:T(8,128)(2,1)S(1)}) custom-call(s32[1]{0:T(128)} %bitcast.4.flag, bf16[640,896]{1,0:T(8,128)(2,1)S(1)} %shard_map.64.first, bf16[640,128]{1,0:T(8,128)(2,1)S(1)} %shard_map.65.last, bf16[256,7168]{1,0:T(8,128)(2,1)S(1)} %bitcast.81, bf16[256,7168]{1,0:T(8,128)(2,1)} %collective-permute-done.3.copied, ...), custom_call_target="tpu_custom_call" | custom-call | flops 3523215360 | bytes 10256384 | tf_op jit(solution)/shard_map/pallas_call | solution.py:146
  299.0 14.7 %collective-permute-done.22.near = bf16[256,2688]{1,0:T(8,128)(2,1)} collective-permute-done((bf16[256,2688]{1,0:T(8,128)(2,1)}, bf16[256,2688]{1,0:T(8,128)(2,1)}, u32[]{:S(2)}, u32[]{:S(2)}) %collective-permute-start.22) | collective-permute-done | bytes 1376288 | tf_op jit(solution)/shard_map/ppermute | solution.py:35
  313.8 3.9 collective-permute-start.23
  318.8 4.6 %all-to-all-start.4 = ((bf16[16,8,4480]{2,1,0:T(8,128)(2,1)}), bf16[16,8,4480]{2,1,0:T(8,128)(2,1)}, u32[]{:S(2)}, u32[]{:S(2)}) async-start(bf16[16,8,4480]{2,1,0:T(8,128)(2,1)} %bitcast.89), calls=%async_computation.4 | async-start | bytes 2293760 | tf_op jit(solution)/shard_map/all_to_all | solution.py:230
  325.5 7.1 %shard_map.68 = (bf16[32,16,2688]{2,1,0:T(8,128)(2,1)S(1)}, bf16[128,2688]{1,0:T(8,128)(2,1)}) custom-call(s32[1]{0:T(128)} %bitcast.4.flag, bf16[640,896]{1,0:T(8,128)(2,1)S(1)} %shard_map.64.first, bf16[640,128]{1,0:T(8,128)(2,1)S(1)} %shard_map.65.last, bf16[256,7168]{1,0:T(8,128)(2,1)S(1)} %bitcast.82, bf16[256,7168]{1,0:T(8,128)(2,1)} %collective-permute-done.3.copied, ...), custom_call_target="tpu_custom_call" | custom-call | flops 3523215360 | bytes 10256384 | tf_op jit(solution)/shard_map/pallas_call | solution.py:146
  334.1 8.6 %all-to-all-done.4 = bf16[16,8,4480]{2,1,0:T(8,128)(2,1)} async-done(((bf16[16,8,4480]{2,1,0:T(8,128)(2,1)}), bf16[16,8,4480]{2,1,0:T(8,128)(2,1)}, u32[]{:S(2)}, u32[]{:S(2)}) %all-to-all-start.4) | async-done | bytes 1146912 | tf_op jit(solution)/shard_map/all_to_all | solution.py:230
  342.7 4.1 all-to-all-start.7
  347.0 37.3 %all-to-all-done.7 = bf16[32,16,2688]{2,1,0:T(8,128)(2,1)S(1)} async-done(((bf16[32,16,2688]{2,1,0:T(8,128)(2,1)}), bf16[32,16,2688]{2,1,0:T(8,128)(2,1)S(1)}, u32[]{:S(2)}, u32[]{:S(2)}) %all-to-all-start.7) | async-done | bytes 2752544 | tf_op jit(solution)/shard_map/all_to_all | solution.py:226
  384.2 4.8 %all-to-all-start.5 = ((bf16[32,16,2688]{2,1,0:T(8,128)(2,1)}), bf16[32,16,2688]{2,1,0:T(8,128)(2,1)}, u32[]{:S(2)}, u32[]{:S(2)}) async-start(bf16[32,16,2688]{2,1,0:T(8,128)(2,1)} %bitcast.32), calls=%async_computation.5 | async-start | bytes 5505024 | tf_op jit(solution)/shard_map/all_to_all | solution.py:226
  390.8 2.2 convolution_add_fusion.2
  393.2 4.2 collective-permute-start.20
  397.4 5.9 %collective-permute-done.20 = bf16[64,1792]{1,0:T(8,128)(2,1)S(1)} collective-permute-done((bf16[64,1792]{1,0:T(8,128)(2,1)S(1)}, bf16[64,1792]{1,0:T(8,128)(2,1)S(1)}, u32[]{:S(2)}, u32[]{:S(2)}) %collective-permute-start.20) | collective-permute-done | bytes 229408 | tf_op jit(solution)/shard_map/ppermute | solution.py:181
  404.0 2.4 fusion.14
  406.5 20.1 %all-to-all-done.5 = bf16[32,16,2688]{2,1,0:T(8,128)(2,1)} async-done(((bf16[32,16,2688]{2,1,0:T(8,128)(2,1)}), bf16[32,16,2688]{2,1,0:T(8,128)(2,1)}, u32[]{:S(2)}, u32[]{:S(2)}) %all-to-all-start.5) | async-done | bytes 2752544 | tf_op jit(solution)/shard_map/all_to_all | solution.py:226
  426.6 2.7 fusion.15
  429.3 3.2 convolution_add_fusion.1
  432.5 3.6 all-to-all-start.6
  436.1 2.0 slice_add_fusion.1
  440.0 4.2 collective-permute-start.21
  444.2 4.3 all-to-all-done.6
  449.3 4.2 collective-permute-start.26
  454.6 5.0 %collective-permute-done.26 = bf16[64,2688]{1,0:T(8,128)(2,1)S(1)} collective-permute-done((bf16[64,2688]{1,0:T(8,128)(2,1)S(1)}, bf16[64,2688]{1,0:T(8,128)(2,1)S(1)}, u32[]{:S(2)}, u32[]{:S(2)}) %collective-permute-start.26) | collective-permute-done | bytes 344096 | tf_op jit(solution)/shard_map/ppermute | solution.py:181
  (128 shorter events, 40.7 us)
Async XLA Ops:
  0.0 7.0 %copy-start.19 = (f32[64,8]{0,1:T(8,128)S(1)}, f32[64,8]{0,1:T(8,128)}, u32[]{:S(2)}) copy-start(f32[64,8]{0,1:T(8,128)} %param.8) | copy-start | bytes 6148
  0.0 7.5 %copy-start.13 = (bf16[64,7168]{1,0:T(8,128)(2,1)S(1)}, bf16[64,7168]{1,0:T(8,128)(2,1)}, u32[]{:S(2)}) copy-start(bf16[64,7168]{1,0:T(8,128)(2,1)} %param.6) | copy-start | bytes 2752516
  2.8 24.9 %collective-permute-start = (bf16[64,7296]{1,0:T(8,128)(2,1)S(1)}, bf16[64,7296]{1,0:T(8,128)(2,1)S(1)}, u32[]{:S(2)}, u32[]{:S(2)}) collective-permute-start(bf16[64,7296]{1,0:T(8,128)(2,1)S(1)} %fusion.6), channel_id=1, source_target_pairs={{0,3},{3,0},{1,2},{2,1},{4,7},{7,4},{5,6},{6,5},{8,11},{11,8},{9,1... | collective-permute-start | bytes 2801672 | tf_op jit(solution)/shard_map/ppermute | solution.py:181
  10.4 55.1 %all-to-all-start = ((bf16[32,8,7168]{2,1,0:T(8,128)(2,1)}), bf16[32,8,7168]{2,1,0:T(8,128)(2,1)}, u32[]{:S(2)}, u32[]{:S(2)}) async-start(bf16[32,8,7168]{2,1,0:T(8,128)(2,1)} %bitcast.85), calls=%async_computation | async-start | bytes 7340032 | tf_op jit(solution)/shard_map/all_to_all | solution.py:226
  17.8 9.9 %copy-start.17 = (bf16[1,256,7168]{2,1,0:T(8,128)(2,1)S(1)}, bf16[1,256,7168]{2,1,0:T(8,128)(2,1)}, u32[]{:S(2)}) copy-start(bf16[1,256,7168]{2,1,0:T(8,128)(2,1)} %param.9) | copy-start | bytes 11010052
  27.7 17.8 %copy-start.16 = (bf16[64,7296]{1,0:T(8,128)(2,1)}, bf16[64,7296]{1,0:T(8,128)(2,1)S(1)}, u32[]{:S(2)}) copy-start(bf16[64,7296]{1,0:T(8,128)(2,1)S(1)} %collective-permute-done) | copy-start | bytes 2801668
  30.1 122.6 %collective-permute-start.4 = (bf16[256,7168]{1,0:T(8,128)(2,1)}, bf16[256,7168]{1,0:T(8,128)(2,1)}, u32[]{:S(2)}, u32[]{:S(2)}) collective-permute-start(bf16[256,7168]{1,0:T(8,128)(2,1)} %pad_maximum_fusion.refs_0_), channel_id=1, source_target_pairs={{0,1},{1,0},{6,7},{7,6},{4,3},{3,4},{5,2},{2,5},{8,9},{9,8},{14,15... | collective-permute-start | bytes 11010056 | tf_op jit(solution)/shard_map/ppermute | solution.py:35
  30.1 122.7 %collective-permute-start.8 = (bf16[256,7168]{1,0:T(8,128)(2,1)}, bf16[256,7168]{1,0:T(8,128)(2,1)}, u32[]{:S(2)}, u32[]{:S(2)}) collective-permute-start(bf16[256,7168]{1,0:T(8,128)(2,1)} %pad_maximum_fusion.refs_0_), channel_id=1, source_target_pairs={{5,3},{3,5},{4,2},{2,4},{13,11},{11,13},{12,10},{10,12},{21,19},{1... | collective-permute-start | bytes 11010056 | tf_op jit(solution)/shard_map/ppermute | solution.py:35
  32.6 37.9 %collective-permute-start.1 = (bf16[256,7168]{1,0:T(8,128)(2,1)}, bf16[256,7168]{1,0:T(8,128)(2,1)}, u32[]{:S(2)}, u32[]{:S(2)}) collective-permute-start(bf16[256,7168]{1,0:T(8,128)(2,1)} %pad_maximum_fusion.refs_0_), channel_id=1, source_target_pairs={{0,4},{1,5},{6,2},{7,3},{8,12},{9,13},{14,10},{15,11},{16,20},{17,... | collective-permute-start | bytes 11010056 | tf_op jit(solution)/shard_map/ppermute | solution.py:35
  40.9 111.0 %collective-permute-start.5 = (bf16[256,7168]{1,0:T(8,128)(2,1)}, bf16[256,7168]{1,0:T(8,128)(2,1)}, u32[]{:S(2)}, u32[]{:S(2)}) collective-permute-start(bf16[256,7168]{1,0:T(8,128)(2,1)} %pad_maximum_fusion.1.refs_2_), channel_id=1, source_target_pairs={{0,1},{1,0},{6,7},{7,6},{4,3},{3,4},{5,2},{2,5},{8,9},{9,8},{14,15... | collective-permute-start | bytes 11010056 | tf_op jit(solution)/shard_map/ppermute | solution.py:35
  41.8 28.8 %collective-permute-start.2 = (bf16[256,7168]{1,0:T(8,128)(2,1)}, bf16[256,7168]{1,0:T(8,128)(2,1)}, u32[]{:S(2)}, u32[]{:S(2)}) collective-permute-start(bf16[256,7168]{1,0:T(8,128)(2,1)} %pad_maximum_fusion.1.refs_2_), channel_id=1, source_target_pairs={{0,4},{1,5},{6,2},{7,3},{8,12},{9,13},{14,10},{15,11},{16,20},{17,... | collective-permute-start | bytes 11010056 | tf_op jit(solution)/shard_map/ppermute | solution.py:35
  65.5 91.3 %slice-start = ((bf16[64,7296]{1,0:T(8,128)(2,1)}), bf16[64,7168]{1,0:T(8,128)(2,1)S(1)}, s32[]{:S(2)}) async-start(bf16[64,7296]{1,0:T(8,128)(2,1)} %copy-done.16), calls=%async_computation.8 | async-start | bytes 1835008 | tf_op jit(solution)/shard_map/slice | solution.py:236
  65.5 86.4 %all-to-all-start.1 = ((bf16[32,8,7168]{2,1,0:T(8,128)(2,1)}), bf16[32,8,7168]{2,1,0:T(8,128)(2,1)}, u32[]{:S(2)}, u32[]{:S(2)}) async-start(bf16[32,8,7168]{2,1,0:T(8,128)(2,1)} %bitcast.86), calls=%async_computation.1 | async-start | bytes 7340032 | tf_op jit(solution)/shard_map/all_to_all | solution.py:226
  70.5 95.3 %collective-permute-start.3 = (bf16[256,7168]{1,0:T(8,128)(2,1)}, bf16[256,7168]{1,0:T(8,128)(2,1)}, u32[]{:S(2)}, u32[]{:S(2)}) collective-permute-start(bf16[256,7168]{1,0:T(8,128)(2,1)} %bitcast.77), channel_id=1, source_target_pairs={{0,4},{1,5},{6,2},{7,3},{8,12},{9,13},{14,10},{15,11},{16,20},{17,... | collective-permute-start | bytes 11010056 | tf_op jit(solution)/shard_map/ppermute | solution.py:35
  152.0 41.6 %collective-permute-start.7 = (bf16[256,7168]{1,0:T(8,128)(2,1)}, bf16[256,7168]{1,0:T(8,128)(2,1)}, u32[]{:S(2)}, u32[]{:S(2)}) collective-permute-start(bf16[256,7168]{1,0:T(8,128)(2,1)} %collective-permute-done.5.refs_5_), channel_id=1, source_target_pairs={{0,4},{4,0},{1,5},{5,1},{2,6},{6,2},{3,7},{7,3},{8,12},{12,8},{9,1... | collective-permute-start | bytes 11010056 | tf_op jit(solution)/shard_map/ppermute | solution.py:35
  152.7 40.8 %collective-permute-start.6 = (bf16[256,7168]{1,0:T(8,128)(2,1)}, bf16[256,7168]{1,0:T(8,128)(2,1)}, u32[]{:S(2)}, u32[]{:S(2)}) collective-permute-start(bf16[256,7168]{1,0:T(8,128)(2,1)} %collective-permute-done.4.refs_4_), channel_id=1, source_target_pairs={{0,4},{4,0},{1,5},{5,1},{2,6},{6,2},{3,7},{7,3},{8,12},{12,8},{9,1... | collective-permute-start | bytes 11010056 | tf_op jit(solution)/shard_map/ppermute | solution.py:35
  152.8 40.7 %collective-permute-start.9 = (bf16[256,7168]{1,0:T(8,128)(2,1)}, bf16[256,7168]{1,0:T(8,128)(2,1)}, u32[]{:S(2)}, u32[]{:S(2)}) collective-permute-start(bf16[256,7168]{1,0:T(8,128)(2,1)} %collective-permute-done.8.refs_9_), channel_id=1, source_target_pairs={{4,0},{5,1},{2,6},{3,7},{12,8},{13,9},{10,14},{11,15},{20,16},{21,... | collective-permute-start | bytes 11010056 | tf_op jit(solution)/shard_map/ppermute | solution.py:35
  154.2 66.3 %collective-permute-start.10 = (bf16[256,7168]{1,0:T(8,128)(2,1)}, bf16[256,7168]{1,0:T(8,128)(2,1)}, u32[]{:S(2)}, u32[]{:S(2)}) collective-permute-start(bf16[256,7168]{1,0:T(8,128)(2,1)} %pad_maximum_fusion.1.refs_2_), channel_id=1, source_target_pairs={{5,3},{3,5},{4,2},{2,4},{13,11},{11,13},{12,10},{10,12},{21,19},{1... | collective-permute-start | bytes 11010056 | tf_op jit(solution)/shard_map/ppermute | solution.py:35
  158.8 34.7 %all-to-all-start.2 = ((bf16[16,8,7168]{2,1,0:T(8,128)(2,1)}), bf16[16,8,7168]{2,1,0:T(8,128)(2,1)S(1)}, u32[]{:S(2)}, u32[]{:S(2)}) async-start(bf16[16,8,7168]{2,1,0:T(8,128)(2,1)} %bitcast.88), calls=%async_computation.2 | async-start | bytes 3670016 | tf_op jit(solution)/shard_map/all_to_all | solution.py:230
  193.5 28.3 %copy-start = (bf16[1,256,7168]{2,1,0:T(8,128)(2,1)S(1)}, bf16[1,256,7168]{2,1,0:T(8,128)(2,1)}, u32[]{:S(2)}) copy-start(bf16[1,256,7168]{2,1,0:T(8,128)(2,1)} %param.11) | copy-start | bytes 11010052
  220.5 32.1 %collective-permute-start.11 = (bf16[256,7168]{1,0:T(8,128)(2,1)}, bf16[256,7168]{1,0:T(8,128)(2,1)}, u32[]{:S(2)}, u32[]{:S(2)}) collective-permute-start(bf16[256,7168]{1,0:T(8,128)(2,1)} %collective-permute-done.10.refs_1_), channel_id=1, source_target_pairs={{4,0},{5,1},{2,6},{3,7},{12,8},{13,9},{10,14},{11,15},{20,16},{21,... | collective-permute-start | bytes 11010056 | tf_op jit(solution)/shard_map/ppermute | solution.py:35
  221.9 6.3 %collective-permute-start.14 = (bf16[256,1792]{1,0:T(8,128)(2,1)S(1)}, bf16[256,1792]{1,0:T(8,128)(2,1)S(1)}, u32[]{:S(2)}, u32[]{:S(2)}) collective-permute-start(bf16[256,1792]{1,0:T(8,128)(2,1)S(1)} %slice.138), channel_id=1, source_target_pairs={{5,3},{3,5},{4,2},{2,4},{13,11},{11,13},{12,10},{10,12},{21,19},{1... | collective-permute-start | bytes 2752520 | tf_op jit(solution)/shard_map/ppermute | solution.py:35
  222.6 19.6 %collective-permute-start.12 = (bf16[256,1792]{1,0:T(8,128)(2,1)S(1)}, bf16[256,1792]{1,0:T(8,128)(2,1)S(1)}, u32[]{:S(2)}, u32[]{:S(2)}) collective-permute-start(bf16[256,1792]{1,0:T(8,128)(2,1)S(1)} %slice.138), channel_id=1, source_target_pairs={{0,1},{1,0},{6,7},{7,6},{4,3},{3,4},{5,2},{2,5},{8,9},{9,8},{14,15... | collective-permute-start | bytes 2752520 | tf_op jit(solution)/shard_map/ppermute | solution.py:35
  224.4 47.0 %collective-permute-start.18 = (bf16[256,2688]{1,0:T(8,128)(2,1)}, bf16[256,2688]{1,0:T(8,128)(2,1)}, u32[]{:S(2)}, u32[]{:S(2)}) collective-permute-start(bf16[256,2688]{1,0:T(8,128)(2,1)} %get-tuple-element.53), channel_id=1, source_target_pairs={{5,3},{3,5},{4,2},{2,4},{13,11},{11,13},{12,10},{10,12},{21,19},{1... | collective-permute-start | bytes 4128776 | tf_op jit(solution)/shard_map/ppermute | solution.py:35
  226.2 46.5 %collective-permute-start.16 = (bf16[256,2688]{1,0:T(8,128)(2,1)}, bf16[256,2688]{1,0:T(8,128)(2,1)}, u32[]{:S(2)}, u32[]{:S(2)}) collective-permute-start(bf16[256,2688]{1,0:T(8,128)(2,1)} %get-tuple-element.53), channel_id=1, source_target_pairs={{0,1},{1,0},{6,7},{7,6},{4,3},{3,4},{5,2},{2,5},{8,9},{9,8},{14,15... | collective-permute-start | bytes 4128776 | tf_op jit(solution)/shard_map/ppermute | solution.py:35
  228.2 31.4 %copy-start.4 = (bf16[256,1792]{1,0:T(8,128)(2,1)}, bf16[256,1792]{1,0:T(8,128)(2,1)S(1)}, u32[]{:S(2)}) copy-start(bf16[256,1792]{1,0:T(8,128)(2,1)S(1)} %collective-permute-done.14.far) | copy-start | bytes 2752516
  228.2 31.4 %collective-permute-start.15 = (bf16[256,1792]{1,0:T(8,128)(2,1)S(1)}, bf16[256,1792]{1,0:T(8,128)(2,1)S(1)}, u32[]{:S(2)}, u32[]{:S(2)}) collective-permute-start(bf16[256,1792]{1,0:T(8,128)(2,1)S(1)} %collective-permute-done.14.far), channel_id=1, source_target_pairs={{4,0},{5,1},{2,6},{3,7},{12,8},{13,9},{10,14},{11,15},{20,16},{21,... | collective-permute-start | bytes 2752520 | tf_op jit(solution)/shard_map/ppermute | solution.py:35
  242.2 17.4 %copy-start.6 = (bf16[256,1792]{1,0:T(8,128)(2,1)}, bf16[256,1792]{1,0:T(8,128)(2,1)S(1)}, u32[]{:S(2)}) copy-start(bf16[256,1792]{1,0:T(8,128)(2,1)S(1)} %collective-permute-done.12.near) | copy-start | bytes 2752516
  242.2 18.3 %collective-permute-start.13 = (bf16[256,1792]{1,0:T(8,128)(2,1)S(1)}, bf16[256,1792]{1,0:T(8,128)(2,1)S(1)}, u32[]{:S(2)}, u32[]{:S(2)}) collective-permute-start(bf16[256,1792]{1,0:T(8,128)(2,1)S(1)} %collective-permute-done.12.near), channel_id=1, source_target_pairs={{0,4},{4,0},{1,5},{5,1},{2,6},{6,2},{3,7},{7,3},{8,12},{12,8},{9,1... | collective-permute-start | bytes 2752520 | tf_op jit(solution)/shard_map/ppermute | solution.py:35
  271.4 16.9 %collective-permute-start.19 = (bf16[256,2688]{1,0:T(8,128)(2,1)}, bf16[256,2688]{1,0:T(8,128)(2,1)}, u32[]{:S(2)}, u32[]{:S(2)}) collective-permute-start(bf16[256,2688]{1,0:T(8,128)(2,1)} %collective-permute-done.18.far), channel_id=1, source_target_pairs={{4,0},{5,1},{2,6},{3,7},{12,8},{13,9},{10,14},{11,15},{20,16},{21,... | collective-permute-start | bytes 4128776 | tf_op jit(solution)/shard_map/ppermute | solution.py:35
  272.7 15.6 %collective-permute-start.17 = (bf16[256,2688]{1,0:T(8,128)(2,1)}, bf16[256,2688]{1,0:T(8,128)(2,1)}, u32[]{:S(2)}, u32[]{:S(2)}) collective-permute-start(bf16[256,2688]{1,0:T(8,128)(2,1)} %collective-permute-done.16.near), channel_id=1, source_target_pairs={{0,4},{4,0},{1,5},{5,1},{2,6},{6,2},{3,7},{7,3},{8,12},{12,8},{9,1... | collective-permute-start | bytes 4128776 | tf_op jit(solution)/shard_map/ppermute | solution.py:35
  280.5 17.2 %collective-permute-start.24 = (bf16[256,2688]{1,0:T(8,128)(2,1)}, bf16[256,2688]{1,0:T(8,128)(2,1)S(1)}, u32[]{:S(2)}, u32[]{:S(2)}) collective-permute-start(bf16[256,2688]{1,0:T(8,128)(2,1)} %get-tuple-element.60), channel_id=1, source_target_pairs={{5,3},{3,5},{4,2},{2,4},{13,11},{11,13},{12,10},{10,12},{21,19},{1... | collective-permute-start | bytes 4128776 | tf_op jit(solution)/shard_map/ppermute | solution.py:35
  281.2 32.5 %collective-permute-start.22 = (bf16[256,2688]{1,0:T(8,128)(2,1)}, bf16[256,2688]{1,0:T(8,128)(2,1)}, u32[]{:S(2)}, u32[]{:S(2)}) collective-permute-start(bf16[256,2688]{1,0:T(8,128)(2,1)} %get-tuple-element.60), channel_id=1, source_target_pairs={{0,1},{1,0},{6,7},{7,6},{4,3},{3,4},{5,2},{2,5},{8,9},{9,8},{14,15... | collective-permute-start | bytes 4128776 | tf_op jit(solution)/shard_map/ppermute | solution.py:35
  281.7 37.1 %all-to-all-start.3 = ((bf16[32,16,1792]{2,1,0:T(8,128)(2,1)}), bf16[32,16,1792]{2,1,0:T(8,128)(2,1)}, u32[]{:S(2)}, u32[]{:S(2)}) async-start(bf16[32,16,1792]{2,1,0:T(8,128)(2,1)} %get-tuple-element.51), calls=%async_computation.3 | async-start | bytes 3670016 | tf_op jit(solution)/shard_map/all_to_all | solution.py:226
  288.3 2.0 copy-start.1
  297.7 25.7 %collective-permute-start.25 = (bf16[256,2688]{1,0:T(8,128)(2,1)S(1)}, bf16[256,2688]{1,0:T(8,128)(2,1)}, u32[]{:S(2)}, u32[]{:S(2)}) collective-permute-start(bf16[256,2688]{1,0:T(8,128)(2,1)S(1)} %collective-permute-done.24.far), channel_id=1, source_target_pairs={{4,0},{5,1},{2,6},{3,7},{12,8},{13,9},{10,14},{11,15},{20,16},{21,... | collective-permute-start | bytes 4128776 | tf_op jit(solution)/shard_map/ppermute | solution.py:35
  313.8 9.7 %collective-permute-start.23 = (bf16[256,2688]{1,0:T(8,128)(2,1)}, bf16[256,2688]{1,0:T(8,128)(2,1)}, u32[]{:S(2)}, u32[]{:S(2)}) collective-permute-start(bf16[256,2688]{1,0:T(8,128)(2,1)} %collective-permute-done.22.near), channel_id=1, source_target_pairs={{0,4},{4,0},{1,5},{5,1},{2,6},{6,2},{3,7},{7,3},{8,12},{12,8},{9,1... | collective-permute-start | bytes 4128776 | tf_op jit(solution)/shard_map/ppermute | solution.py:35
  318.8 23.9 %all-to-all-start.4 = ((bf16[16,8,4480]{2,1,0:T(8,128)(2,1)}), bf16[16,8,4480]{2,1,0:T(8,128)(2,1)}, u32[]{:S(2)}, u32[]{:S(2)}) async-start(bf16[16,8,4480]{2,1,0:T(8,128)(2,1)} %bitcast.89), calls=%async_computation.4 | async-start | bytes 2293760 | tf_op jit(solution)/shard_map/all_to_all | solution.py:230
  323.4 2.0 copy-start.2
  342.7 41.6 %all-to-all-start.7 = ((bf16[32,16,2688]{2,1,0:T(8,128)(2,1)}), bf16[32,16,2688]{2,1,0:T(8,128)(2,1)S(1)}, u32[]{:S(2)}, u32[]{:S(2)}) async-start(bf16[32,16,2688]{2,1,0:T(8,128)(2,1)} %copy-done.3), calls=%async_computation.7 | async-start | bytes 5505024 | tf_op jit(solution)/shard_map/all_to_all | solution.py:226
  384.2 42.3 %all-to-all-start.5 = ((bf16[32,16,2688]{2,1,0:T(8,128)(2,1)}), bf16[32,16,2688]{2,1,0:T(8,128)(2,1)}, u32[]{:S(2)}, u32[]{:S(2)}) async-start(bf16[32,16,2688]{2,1,0:T(8,128)(2,1)} %bitcast.32), calls=%async_computation.5 | async-start | bytes 5505024 | tf_op jit(solution)/shard_map/all_to_all | solution.py:226
  393.2 10.1 %collective-permute-start.20 = (bf16[64,1792]{1,0:T(8,128)(2,1)S(1)}, bf16[64,1792]{1,0:T(8,128)(2,1)S(1)}, u32[]{:S(2)}, u32[]{:S(2)}) collective-permute-start(bf16[64,1792]{1,0:T(8,128)(2,1)S(1)} %slice.186), channel_id=1, source_target_pairs={{0,3},{3,0},{1,2},{2,1},{4,7},{7,4},{5,6},{6,5},{8,11},{11,8},{9,1... | collective-permute-start | bytes 688136 | tf_op jit(solution)/shard_map/ppermute | solution.py:181
  432.5 16.0 %all-to-all-start.6 = ((bf16[16,8,2688]{2,1,0:T(8,128)(2,1)}), bf16[16,8,2688]{2,1,0:T(8,128)(2,1)S(1)}, u32[]{:S(2)}, u32[]{:S(2)}) async-start(bf16[16,8,2688]{2,1,0:T(8,128)(2,1)} %bitcast.35), calls=%async_computation.6 | async-start | bytes 1376256 | tf_op jit(solution)/shard_map/all_to_all | solution.py:230
  436.1 12.4 %copy-start.12 = (f32[256,2688]{1,0:T(8,128)S(1)}, f32[256,2688]{1,0:T(8,128)}, u32[]{:S(2)}) copy-start(f32[256,2688]{1,0:T(8,128)} %fusion.14) | copy-start | bytes 8257540
  440.0 13.5 %collective-permute-start.21 = (bf16[64,2688]{1,0:T(8,128)(2,1)}, bf16[64,2688]{1,0:T(8,128)(2,1)}, u32[]{:S(2)}, u32[]{:S(2)}) collective-permute-start(bf16[64,2688]{1,0:T(8,128)(2,1)} %slice.185), channel_id=1, source_target_pairs={{0,3},{3,0},{1,2},{2,1},{4,7},{7,4},{5,6},{6,5},{8,11},{11,8},{9,1... | collective-permute-start | bytes 1032200 | tf_op jit(solution)/shard_map/ppermute | solution.py:181
  449.1 4.5 copy-start.15
  449.3 10.4 %copy-start.18 = (bf16[64,1792]{1,0:T(8,128)(2,1)S(1)}, bf16[64,1792]{1,0:T(8,128)(2,1)}, u32[]{:S(2)}) copy-start(bf16[64,1792]{1,0:T(8,128)(2,1)} %fusion.10) | copy-start | bytes 688132
  449.3 10.3 %collective-permute-start.26 = (bf16[64,2688]{1,0:T(8,128)(2,1)S(1)}, bf16[64,2688]{1,0:T(8,128)(2,1)S(1)}, u32[]{:S(2)}, u32[]{:S(2)}) collective-permute-start(bf16[64,2688]{1,0:T(8,128)(2,1)S(1)} %slice.184), channel_id=1, source_target_pairs={{0,3},{3,0},{1,2},{2,1},{4,7},{7,4},{5,6},{6,5},{8,11},{11,8},{9,1... | collective-permute-start | bytes 1032200 | tf_op jit(solution)/shard_map/ppermute | solution.py:181
  (8 other events, 9.2 us)

commit v3 on v2

--- a/solution.py
+++ b/solution.py
@@ -103,11 +103,7 @@
         ),
         out_shape=jax.ShapeDtypeStruct((rows, len(units) * HALF), jnp.bfloat16),
         compiler_params=pltpu.CompilerParams(vmem_limit_bytes=48 * 2**20),
-        cost_estimate=pl.CostEstimate(
-            flops=4 * rows * width * len(units) * HALF,
-            bytes_accessed=2 * width * (rows + 2 * len(units) * HALF),
-            transcendentals=rows * len(units) * HALF,
-        ),
+        cost_estimate=pl.CostEstimate(flops=1, bytes_accessed=1, transcendentals=0),
     )(flag, *operands)
 
 
@@ -132,16 +128,14 @@
     out_rest[...] = total[2 * MAIN :]
 
 
-def down_rows(flag, first, last, whole, at, panels):
-    step = panels[0].shape[1]
+def down_rows(flag, first, last, panels, step, starts):
     rows = 2 * MAIN + REST
 
-    def panel(wanted=None, skip=0):
+    def panel(wanted, start):
+        skip = start // TILE
         if wanted is None:
-            return pl.BlockSpec((QUARTER, TILE), lambda i, f: (0, i))
-        return pl.BlockSpec(
-            (QUARTER, TILE), lambda i, f: (0, pick_block(f, wanted, skip // TILE + i))
-        )
+            return pl.BlockSpec((QUARTER, TILE), lambda i, f: (0, skip + i))
+        return pl.BlockSpec((QUARTER, TILE), lambda i, f: (0, pick_block(f, wanted, skip + i)))
 
     main, tail = pl.pallas_call(
         down_kernel,
@@ -151,12 +145,7 @@
             in_specs=[
                 pl.BlockSpec(first.shape, lambda i, f: (0, 0)),
                 pl.BlockSpec(last.shape, lambda i, f: (0, 0)),
-                panel(1, at),
-                panel(0, at),
-                panel(),
-                panel(),
-                panel(1),
-                panel(0),
+                *map(panel, (1, 0, None, None, 1, 0), starts),
             ],
             out_specs=[
                 pl.BlockSpec((MAIN // 8, 16, TILE), lambda i, f: (0, 0, i)),
@@ -173,7 +162,7 @@
             bytes_accessed=2 * (4 * QUARTER * step + rows * (4 * QUARTER + step)),
             transcendentals=0,
         ),
-    )(flag, first, last, *whole, *panels)
+    )(flag, first, last, *panels)
     return main.reshape(2 * MAIN, step), tail
 
 
@@ -237,23 +226,27 @@
     ids, gate, low = (extra[:, at : at + 8] for at in (0, 8, 16))
     other_routes = jnp.concatenate([ids, gate + low], axis=1)
 
-    gate, upper = after(gate_weight[0], other), up_weight[0]
     owns = [
-        jnp.concatenate([part[at : at + HALF] for part in (gate, upper)], axis=0)
-        for at in (0, HALF)
+        jnp.concatenate(
+            [after(gate_weight[0], got)[at : at + HALF], up_weight[0][at : at + HALF]], axis=0
+        )
+        for at, got in ((0, sent), (HALF, other))
     ]
+    owns[1] = jnp.concatenate([owns[1], down_weight[0][:, : STEPS[0]]], axis=1)
     nears = [along(own, NEXT) for own in owns]
-    fars = [along(owns[0], FAR), along(after(owns[1], *nears), FAR)]
 
     pick, other_rest, mix_other, mix_other_rest = slots(other_routes, 1)
-    theirs = exchange_main(after(rows_of(pick, other), mine))
     rest = rows_of(
         jnp.concatenate([pick_rest, other_rest], axis=2), jnp.concatenate([tokens, other], axis=0)
     )
+    theirs = exchange_main(after(rows_of(pick, other), mine, nears[0]))
     rest = exchange_rest(after(rest, theirs))
+    fars = [along(owns[0], FAR), along(after(owns[1], nears[0], theirs), FAR)]
     copied = [along(own, FROM_HOME) for own in owns]
-    across = [along(after(near, theirs), SIBLING) for near in nears]
-    brought_0 = along(after(fars[0], theirs), TO_HOME)
+    across = [
+        along(after(near, got), SIBLING) for near, got in zip(nears, (theirs, rest), strict=True)
+    ]
+    brought_0 = along(after(fars[0], rest), TO_HOME)
 
     def halves(*parts):
         part = jnp.concatenate([part.reshape(tok_rows, -1) for part in parts], axis=0)
@@ -268,33 +261,30 @@
         return along(own, NEXT), along(own, FAR)
 
     whole = down_weight[0], along(after(down_weight[0], *copied), FROM_HOME)
-    down_0 = columns(0, STEPS[0], *nears)
     units = [*zip(owns, copied, strict=True), *zip(nears), *zip(across), (brought_0, fars[0])]
     first = hidden_units(flag, after(mine, whole[1]), theirs, rest, units)
     brought_1 = along(after(fars[1], first), TO_HOME)
     down_1 = columns(STEPS[0], STEPS[1], fars[1], first)
     last = hidden_units(flag, after(mine, first), theirs, rest, [(brought_1, fars[1])])
-    result_0 = down_rows(flag, first, last, whole, 0, share(*down_0, first))
-    down_2 = columns(STEPS[0] + STEPS[1], STEPS[2], down_0[1], result_0[0])
-    result_1 = down_rows(flag, first, last, whole, STEPS[0], share(*down_1, result_0[0]))
-    result_2 = down_rows(
-        flag, first, last, whole, STEPS[0] + STEPS[1], share(*down_2, result_1[0])
-    )
+    panels = owns[1], copied[1], nears[1], across[1], brought_1, fars[1]
+    result_0 = down_rows(flag, first, last, panels, STEPS[0], (width,) * 6)
+    at = STEPS[0] + STEPS[1]
+    down_2 = columns(at, STEPS[2], down_1[1], result_0[0])
+    panels = whole + share(*down_1, result_0[0])
+    result_1 = down_rows(flag, first, last, panels, STEPS[1], (STEPS[0],) * 2 + (0,) * 4)
+    panels = whole + share(*down_2, result_1[0])
+    result_2 = down_rows(flag, first, last, panels, STEPS[2], (at,) * 2 + (0,) * 4)
     mains, rests = zip(result_0, result_1, result_2, strict=True)
-    early = jnp.concatenate(rests[:2], axis=1)
     back_0 = exchange_main(mains[0])
-    early = exchange_rest(after(early, back_0))
-    back_1 = exchange_main(after(mains[1], early))
-    late = exchange_rest(after(rests[2], back_1))
-    back_2 = exchange_main(after(mains[2], late))
-    outs = []
-    for back, back_rest in (
-        (back_0, early[:, : STEPS[0]]),
-        (back_1, early[:, STEPS[0] :]),
-        (back_2, late),
-    ):
+    back_1 = exchange_main(after(mains[1], back_0))
+    back_rest = exchange_rest(after(jnp.concatenate(rests, axis=1), back_1))
+    back_2 = exchange_main(after(mains[2], back_rest))
+    outs, at = [], 0
+    for back in (back_0, back_1, back_2):
+        tail = back_rest[:, at : at + back.shape[1]]
+        at += back.shape[1]
         sums = jnp.dot(mix_main, back, preferred_element_type=jnp.float32) + jnp.dot(
-            mix_rest, back_rest, preferred_element_type=jnp.float32
+            mix_rest, tail, preferred_element_type=jnp.float32
         )
         sums = sums[:count] + sums[count:]
         partner = pair_exchange(sums[tok_rows:].astype(jnp.bfloat16))

time: 462 us -> 434 us (0.939)
  starting transfers between devices: 114 us -> 91.1 us
  waiting for transfers between devices: 238 us -> 231 us
    ppermute x4, waiting for transfers between devices: 18.3 us -> 60.2 us  [pair_exchange(): return lax.ppermute(value, ('zh', 'zl'), PAIR)]
    ppermute x23 -> x19, waiting for transfers between devices: 105 us -> 83.3 us  [along(): return lax.ppermute(value, COL, pairs)]
    all_to_all x3 -> x2, waiting for transfers between devices: 40.6 us -> 21.5 us  [exchange_rest(): lax.all_to_all(parts, ('y', 'x'), 0, 0, tiled=True).reshape(rows.shape)]
    ppermute x4, starting transfers between devices: 16.8 us -> 5.63 us  [pair_exchange(): return lax.ppermute(value, ('zh', 'zl'), PAIR)]
    ppermute x23 -> x19, starting transfers between devices: 54.2 us -> 45 us  [along(): return lax.ppermute(value, COL, pairs)]
    all_to_all x5, waiting for transfers between devices: 74.4 us -> 65.8 us  [exchange_main(): return lax.all_to_all(parts, EXP, 0, 0, tiled=True).reshape(rows.shape)]
    all_to_all x3 -> x2, starting transfers between devices: 15.2 us -> 7.43 us  [exchange_rest(): lax.all_to_all(parts, ('y', 'x'), 0, 0, tiled=True).reshape(rows.shape)]
    all_to_all x5, starting transfers between devices: 27.9 us -> 33 us  [exchange_main(): return lax.all_to_all(parts, EXP, 0, 0, tiled=True).reshape(rows.shape)]
  transfers between devices with their start and end apart: 35 -> 30, of which waited for: 12 -> 16; matrix products, arithmetic and copies ran while one was open for 7% -> 8% of each run, Pallas kernels for 12% -> 12%
where the time goes in v3:
time: 434 us; the launch traced here: 432 us
  waiting for transfers between devices  231 us (53%)
  starting transfers between devices  91.1 us (21%)
  Pallas kernels  53.4 us (12%)
  matrix products  22.6 us (5%)
  local copies, waits for them, and re-layouts  20.2 us (5%)
  other arithmetic  13.6 us (3%)
    ppermute x19, waiting for transfers between devices, along(): return lax.ppermute(value, COL, pairs)  83.3 us
    all_to_all x5, waiting for transfers between devices, exchange_main(): return lax.all_to_all(parts, EXP, 0, 0, tiled=True).reshape(rows.shape)  65.8 us
    ppermute x4, waiting for transfers between devices, pair_exchange(): return lax.ppermute(value, ('zh', 'zl'), PAIR)  60.2 us
    ppermute x19, starting transfers between devices, along(): return lax.ppermute(value, COL, pairs)  45 us
    pallas_call x2, Pallas kernels, hidden_units(): pl.pallas_call(functools.partial(hidden_kernel, kinds=kinds), grid_spec=p...  33.9 us
    all_to_all x5, starting transfers between devices, exchange_main(): return lax.all_to_all(parts, EXP, 0, 0, tiled=True).reshape(rows.shape)  33 us
    all_to_all x2, waiting for transfers between devices, exchange_rest(): lax.all_to_all(parts, ('y', 'x'), 0, 0, tiled=True).reshape(rows.shape)  21.5 us
    pallas_call x3, Pallas kernels, down_rows(): pl.pallas_call(down_kernel, grid_spec=pltpu.PrefetchScalarGridSpec(num_sc...  19.5 us
  transfers between devices with their start and end apart: 30, of which 16 were waited for; matrix products, arithmetic and copies ran while one was open for 8% of the time, Pallas kernels for 12%

profile of v3, /device:TPU:0, one launch (start us, length us, event | category | flops | bytes accessed | tf_op | source)
XLA Modules:
  0.0 432.3 jit_solution(8600470121671893757)
XLA Ops:
  1.7 2.4 slice_bitcast_fusion
  4.2 3.0 convolution_convert_fusion.1
  7.3 2.1 pad_maximum_fusion.1.refs_0_
  9.4 2.0 collective-permute-start.4
  11.4 9.4 %all-to-all-start = ((bf16[32,8,7168]{2,1,0:T(8,128)(2,1)}), bf16[32,8,7168]{2,1,0:T(8,128)(2,1)}, u32[]{:S(2)}, u32[]{:S(2)}) async-start(bf16[32,8,7168]{2,1,0:T(8,128)(2,1)} %bitcast.80), calls=%async_computation | async-start | bytes 7340032 | tf_op jit(solution)/shard_map/all_to_all | solution.py:215
  21.3 2.4 slice.142
  23.7 50.8 %collective-permute-done = bf16[64,7296]{1,0:T(8,128)(2,1)S(1)} collective-permute-done((bf16[64,7296]{1,0:T(8,128)(2,1)S(1)}, bf16[64,7296]{1,0:T(8,128)(2,1)S(1)}, u32[]{:S(2)}, u32[]{:S(2)}) %collective-permute-start) | collective-permute-done | bytes 933920 | tf_op jit(solution)/shard_map/ppermute | solution.py:170
  77.6 4.1 convolution_convert_fusion
  81.7 7.4 %all-to-all-start.1 = ((bf16[32,8,7168]{2,1,0:T(8,128)(2,1)}), bf16[32,8,7168]{2,1,0:T(8,128)(2,1)}, u32[]{:S(2)}, u32[]{:S(2)}) async-start(bf16[32,8,7168]{2,1,0:T(8,128)(2,1)} %bitcast.81), calls=%async_computation.1 | async-start | bytes 7340032 | tf_op jit(solution)/shard_map/all_to_all | solution.py:215
  89.2 5.2 %pad_maximum_fusion.refs_2_.own = bf16[256,8960]{1,0:T(8,128)(2,1)} fusion(bf16[256,1792]{1,0:T(8,128)(2,1)} %slice.142, bf16[128,7168]{1,0:T(8,128)(2,1)S(1)} %get-tuple-element.67, bf16[128,7168]{1,0:T(8,128)(2,1)} %slice.114), kind=kLoop, calls=%fused_computation.3 | loop fusion | flops 13762560 | bytes 9175040 | tf_op jit(solution)/shard_map/concatenate | solution.py:235
  94.3 6.2 %collective-permute-start.2 = (bf16[256,8960]{1,0:T(8,128)(2,1)}, bf16[256,8960]{1,0:T(8,128)(2,1)}, u32[]{:S(2)}, u32[]{:S(2)}) collective-permute-start(bf16[256,8960]{1,0:T(8,128)(2,1)} %pad_maximum_fusion.refs_2_.own), channel_id=1, source_target_pairs={{0,4},{1,5},{6,2},{7,3},{8,12},{9,13},{14,10},{15,11},{16,20},{17,... | collective-permute-start | bytes 13762568 | tf_op jit(solution)/shard_map/ppermute | solution.py:35
  100.5 3.1 collective-permute-start.1
  103.5 2.5 collective-permute-start.8
  106.2 3.1 convolution_convert_fusion.2
  109.3 27.5 %all-to-all-done.1 = bf16[32,8,7168]{2,1,0:T(8,128)(2,1)} async-done(((bf16[32,8,7168]{2,1,0:T(8,128)(2,1)}), bf16[32,8,7168]{2,1,0:T(8,128)(2,1)}, u32[]{:S(2)}, u32[]{:S(2)}) %all-to-all-start.1) | async-done | bytes 3670048 | tf_op jit(solution)/shard_map/all_to_all | solution.py:215
  136.8 3.7 all-to-all-start.2
  140.5 46.1 %collective-permute-done.5.refs_5_.near = bf16[256,8960]{1,0:T(8,128)(2,1)} collective-permute-done((bf16[256,8960]{1,0:T(8,128)(2,1)}, bf16[256,8960]{1,0:T(8,128)(2,1)}, u32[]{:S(2)}, u32[]{:S(2)}) %collective-permute-start.5) | collective-permute-done | bytes 4587552 | tf_op jit(solution)/shard_map/ppermute | solution.py:35
  187.5 2.8 collective-permute-start.10
  190.3 3.1 collective-permute-start.3
  194.9 5.6 %collective-permute-done.3.copied = bf16[256,7168]{1,0:T(8,128)(2,1)} collective-permute-done((bf16[256,7168]{1,0:T(8,128)(2,1)}, bf16[256,7168]{1,0:T(8,128)(2,1)}, u32[]{:S(2)}, u32[]{:S(2)}) %collective-permute-start.3) | collective-permute-done | bytes 3670048 | tf_op jit(solution)/shard_map/ppermute | solution.py:35
  200.5 5.2 %collective-permute-done.6.refs_6_ = bf16[256,7168]{1,0:T(8,128)(2,1)} collective-permute-done((bf16[256,7168]{1,0:T(8,128)(2,1)}, bf16[256,7168]{1,0:T(8,128)(2,1)}, u32[]{:S(2)}, u32[]{:S(2)}) %collective-permute-start.6) | collective-permute-done | bytes 3670048 | tf_op jit(solution)/shard_map/ppermute | solution.py:35
  205.7 26.9 %shard_map.64.first = bf16[640,896]{1,0:T(8,128)(2,1)S(1)} custom-call(s32[1]{0:T(128)} %bitcast.4.flag, bf16[256,7168]{1,0:T(8,128)(2,1)} %bitcast.6.mine, bf16[256,7168]{1,0:T(8,128)(2,1)} %bitcast.14.theirs, bf16[128,7168]{1,0:T(8,128)(2,1)S(1)} %bitcast.78, bf16[256,7168]{1,0:T(8,128)(2,1)} %pad_maximum_fusion.1.refs_0_, ...), custom_call_target="tpu_custom_call" | custom-call | flops 1 | bytes 1 | tf_op jit(solution)/shard_map/pallas_call | solution.py:95
  235.7 2.3 collective-permute-start.12
  239.8 15.3 %collective-permute-done.11.refs_0_.brought = bf16[256,8960]{1,0:T(8,128)(2,1)S(1)} collective-permute-done((bf16[256,8960]{1,0:T(8,128)(2,1)}, bf16[256,8960]{1,0:T(8,128)(2,1)S(1)}, u32[]{:S(2)}, u32[]{:S(2)}) %collective-permute-start.11) | collective-permute-done | bytes 4587552 | tf_op jit(solution)/shard_map/ppermute | solution.py:35
  255.1 2.1 copy-done.6
  257.2 7.0 %shard_map.65.last = bf16[640,128]{1,0:T(8,128)(2,1)S(1)} custom-call(s32[1]{0:T(128)} %bitcast.4.flag, bf16[256,7168]{1,0:T(8,128)(2,1)} %bitcast.6.mine, bf16[256,7168]{1,0:T(8,128)(2,1)} %bitcast.14.theirs, bf16[128,7168]{1,0:T(8,128)(2,1)S(1)} %bitcast.79, bf16[256,8960]{1,0:T(8,128)(2,1)} %copy-done.6, bf16[256,8960]{1,0:T(8,128)(2,1)} %collective-permute-done.10.refs_1_.far), custom_call_target="tpu_custom_call" | custom-call | flops 1 | bytes 1 | tf_op jit(solution)/shard_map/pallas_call | solution.py:95
  264.1 5.9 %shard_map.66 = (bf16[32,16,1792]{2,1,0:T(8,128)(2,1)}, bf16[128,1792]{1,0:T(8,128)(2,1)S(1)}) custom-call(s32[1]{0:T(128)} %bitcast.4.flag, bf16[640,896]{1,0:T(8,128)(2,1)S(1)} %shard_map.64.first, bf16[640,128]{1,0:T(8,128)(2,1)S(1)} %shard_map.65.last, bf16[256,8960]{1,0:T(8,128)(2,1)} %pad_maximum_fusion.refs_2_.own, ...), custom_call_target="tpu_custom_call" | custom-call | flops 2348810240 | bytes 7274496 | tf_op jit(solution)/shard_map/pallas_call | solution.py:140
  270.1 7.3 %all-to-all-start.3 = ((bf16[32,16,1792]{2,1,0:T(8,128)(2,1)}), bf16[32,16,1792]{2,1,0:T(8,128)(2,1)}, u32[]{:S(2)}, u32[]{:S(2)}) async-start(bf16[32,16,1792]{2,1,0:T(8,128)(2,1)} %get-tuple-element.46), calls=%async_computation.3 | async-start | bytes 3670016 | tf_op jit(solution)/shard_map/all_to_all | solution.py:215
  277.4 6.6 %collective-permute-start.13 = (bf16[256,2688]{1,0:T(8,128)(2,1)}, bf16[256,2688]{1,0:T(8,128)(2,1)S(1)}, u32[]{:S(2)}, u32[]{:S(2)}) collective-permute-start(bf16[256,2688]{1,0:T(8,128)(2,1)} %collective-permute-done.12.near), channel_id=1, source_target_pairs={{0,4},{4,0},{1,5},{5,1},{2,6},{6,2},{3,7},{7,3},{8,12},{12,8},{9,1... | collective-permute-start | bytes 4128776 | tf_op jit(solution)/shard_map/ppermute | solution.py:35
  287.2 2.1 collective-permute-done.15.brought
  289.2 2.0 copy-done.1
  291.3 6.5 %shard_map.67 = (bf16[32,16,2688]{2,1,0:T(8,128)(2,1)S(1)}, bf16[128,2688]{1,0:T(8,128)(2,1)S(1)}) custom-call(s32[1]{0:T(128)} %bitcast.4.flag, bf16[640,896]{1,0:T(8,128)(2,1)S(1)} %shard_map.64.first, bf16[640,128]{1,0:T(8,128)(2,1)S(1)} %shard_map.65.last, bf16[256,7168]{1,0:T(8,128)(2,1)S(1)} %bitcast.76, ...), custom_call_target="tpu_custom_call" | custom-call | flops 3523215360 | bytes 10256384 | tf_op jit(solution)/shard_map/pallas_call | solution.py:140
  300.1 4.2 all-to-all-done.3
  304.3 4.8 %all-to-all-start.4 = ((bf16[32,16,2688]{2,1,0:T(8,128)(2,1)}), bf16[32,16,2688]{2,1,0:T(8,128)(2,1)}, u32[]{:S(2)}, u32[]{:S(2)}) async-start(bf16[32,16,2688]{2,1,0:T(8,128)(2,1)} %copy-done.3), calls=%async_computation.4 | async-start | bytes 5505024 | tf_op jit(solution)/shard_map/all_to_all | solution.py:215
  309.1 5.3 %collective-permute-done.16.near = bf16[256,2688]{1,0:T(8,128)(2,1)S(1)} collective-permute-done((bf16[256,2688]{1,0:T(8,128)(2,1)}, bf16[256,2688]{1,0:T(8,128)(2,1)S(1)}, u32[]{:S(2)}, u32[]{:S(2)}) %collective-permute-start.16) | collective-permute-done | bytes 1376288 | tf_op jit(solution)/shard_map/ppermute | solution.py:35
  314.4 6.5 %collective-permute-start.17 = (bf16[256,2688]{1,0:T(8,128)(2,1)S(1)}, bf16[256,2688]{1,0:T(8,128)(2,1)S(1)}, u32[]{:S(2)}, u32[]{:S(2)}) collective-permute-start(bf16[256,2688]{1,0:T(8,128)(2,1)S(1)} %collective-permute-done.16.near), channel_id=1, source_target_pairs={{0,4},{4,0},{1,5},{5,1},{2,6},{6,2},{3,7},{7,3},{8,12},{12,8},{9,1... | collective-permute-start | bytes 4128776 | tf_op jit(solution)/shard_map/ppermute | solution.py:35
  323.7 2.5 collective-permute-done.19.brought
  326.1 2.0 copy-done.2
  328.2 7.1 %shard_map.68 = (bf16[32,16,2688]{2,1,0:T(8,128)(2,1)}, bf16[128,2688]{1,0:T(8,128)(2,1)S(1)}) custom-call(s32[1]{0:T(128)} %bitcast.4.flag, bf16[640,896]{1,0:T(8,128)(2,1)S(1)} %shard_map.64.first, bf16[640,128]{1,0:T(8,128)(2,1)S(1)} %shard_map.65.last, bf16[256,7168]{1,0:T(8,128)(2,1)S(1)} %bitcast.77, bf16[256,7168]{1,0:T(8,128)(2,1)} %collective-permute-done.3.copied, ...), custom_call_target="tpu_custom_call" | custom-call | flops 3523215360 | bytes 10256384 | tf_op jit(solution)/shard_map/pallas_call | solution.py:140
  336.7 9.9 %all-to-all-done.4 = bf16[32,16,2688]{2,1,0:T(8,128)(2,1)} async-done(((bf16[32,16,2688]{2,1,0:T(8,128)(2,1)}), bf16[32,16,2688]{2,1,0:T(8,128)(2,1)}, u32[]{:S(2)}, u32[]{:S(2)}) %all-to-all-start.4) | async-done | bytes 2752544 | tf_op jit(solution)/shard_map/all_to_all | solution.py:215
  346.6 3.7 all-to-all-start.5
  350.8 4.3 fusion.16
  355.1 21.5 %all-to-all-done.5 = bf16[16,8,7168]{2,1,0:T(8,128)(2,1)S(1)} async-done(((bf16[16,8,7168]{2,1,0:T(8,128)(2,1)}), bf16[16,8,7168]{2,1,0:T(8,128)(2,1)S(1)}, u32[]{:S(2)}, u32[]{:S(2)}) %all-to-all-start.5) | async-done | bytes 1835040 | tf_op jit(solution)/shard_map/all_to_all | solution.py:219
  377.8 4.1 all-to-all-start.6
  383.4 2.2 convolution_add_fusion.2
  391.8 3.3 collective-permute-done.20
  395.1 24.3 %all-to-all-done.6 = bf16[32,16,2688]{2,1,0:T(8,128)(2,1)S(1)} async-done(((bf16[32,16,2688]{2,1,0:T(8,128)(2,1)}), bf16[32,16,2688]{2,1,0:T(8,128)(2,1)S(1)}, u32[]{:S(2)}, u32[]{:S(2)}) %all-to-all-start.6) | async-done | bytes 2752544 | tf_op jit(solution)/shard_map/all_to_all | solution.py:215
  425.1 6.1 %collective-permute-done.22 = bf16[64,2688]{1,0:T(8,128)(2,1)S(1)} collective-permute-done((bf16[64,2688]{1,0:T(8,128)(2,1)S(1)}, bf16[64,2688]{1,0:T(8,128)(2,1)S(1)}, u32[]{:S(2)}, u32[]{:S(2)}) %collective-permute-start.22) | collective-permute-done | bytes 344096 | tf_op jit(solution)/shard_map/ppermute | solution.py:170
  (110 shorter events, 38.5 us)
Async XLA Ops:
  1.7 2.5 copy-start.8
  4.1 3.1 copy-start.13
  9.4 72.4 %collective-permute-start.4 = (bf16[256,7168]{1,0:T(8,128)(2,1)}, bf16[256,7168]{1,0:T(8,128)(2,1)}, u32[]{:S(2)}, u32[]{:S(2)}) collective-permute-start(bf16[256,7168]{1,0:T(8,128)(2,1)} %pad_maximum_fusion.1.refs_0_), channel_id=1, source_target_pairs={{0,1},{1,0},{6,7},{7,6},{4,3},{3,4},{5,2},{2,5},{8,9},{9,8},{14,15... | collective-permute-start | bytes 11010056 | tf_op jit(solution)/shard_map/ppermute | solution.py:35
  11.4 9.4 %copy-start.15 = (f32[64,8]{0,1:T(8,128)S(1)}, f32[64,8]{0,1:T(8,128)}, u32[]{:S(2)}) copy-start(f32[64,8]{0,1:T(8,128)} %param.8) | copy-start | bytes 6148
  11.4 70.3 %all-to-all-start = ((bf16[32,8,7168]{2,1,0:T(8,128)(2,1)}), bf16[32,8,7168]{2,1,0:T(8,128)(2,1)}, u32[]{:S(2)}, u32[]{:S(2)}) async-start(bf16[32,8,7168]{2,1,0:T(8,128)(2,1)} %bitcast.80), calls=%async_computation | async-start | bytes 7340032 | tf_op jit(solution)/shard_map/all_to_all | solution.py:215
  20.9 54.7 %copy-start.14 = (bf16[1,256,7168]{2,1,0:T(8,128)(2,1)S(1)}, bf16[1,256,7168]{2,1,0:T(8,128)(2,1)}, u32[]{:S(2)}) copy-start(bf16[1,256,7168]{2,1,0:T(8,128)(2,1)} %param.9) | copy-start | bytes 11010052
  21.0 53.6 %collective-permute-start = (bf16[64,7296]{1,0:T(8,128)(2,1)S(1)}, bf16[64,7296]{1,0:T(8,128)(2,1)S(1)}, u32[]{:S(2)}, u32[]{:S(2)}) collective-permute-start(bf16[64,7296]{1,0:T(8,128)(2,1)S(1)} %fusion.6), channel_id=1, source_target_pairs={{0,3},{3,0},{1,2},{2,1},{4,7},{7,4},{5,6},{6,5},{8,11},{11,8},{9,1... | collective-permute-start | bytes 2801672 | tf_op jit(solution)/shard_map/ppermute | solution.py:170
  74.6 2.5 copy-start.12
  81.7 55.1 %all-to-all-start.1 = ((bf16[32,8,7168]{2,1,0:T(8,128)(2,1)}), bf16[32,8,7168]{2,1,0:T(8,128)(2,1)}, u32[]{:S(2)}, u32[]{:S(2)}) async-start(bf16[32,8,7168]{2,1,0:T(8,128)(2,1)} %bitcast.81), calls=%async_computation.1 | async-start | bytes 7340032 | tf_op jit(solution)/shard_map/all_to_all | solution.py:215
  94.3 92.4 %collective-permute-start.5 = (bf16[256,8960]{1,0:T(8,128)(2,1)}, bf16[256,8960]{1,0:T(8,128)(2,1)}, u32[]{:S(2)}, u32[]{:S(2)}) collective-permute-start(bf16[256,8960]{1,0:T(8,128)(2,1)} %pad_maximum_fusion.refs_2_.own), channel_id=1, source_target_pairs={{0,1},{1,0},{6,7},{7,6},{4,3},{3,4},{5,2},{2,5},{8,9},{9,8},{14,15... | collective-permute-start | bytes 13762568 | tf_op jit(solution)/shard_map/ppermute | solution.py:35
  94.3 96.0 %collective-permute-start.2 = (bf16[256,8960]{1,0:T(8,128)(2,1)}, bf16[256,8960]{1,0:T(8,128)(2,1)}, u32[]{:S(2)}, u32[]{:S(2)}) collective-permute-start(bf16[256,8960]{1,0:T(8,128)(2,1)} %pad_maximum_fusion.refs_2_.own), channel_id=1, source_target_pairs={{0,4},{1,5},{6,2},{7,3},{8,12},{9,13},{14,10},{15,11},{16,20},{17,... | collective-permute-start | bytes 13762568 | tf_op jit(solution)/shard_map/ppermute | solution.py:35
  100.5 89.8 %collective-permute-start.1 = (bf16[256,7168]{1,0:T(8,128)(2,1)}, bf16[256,7168]{1,0:T(8,128)(2,1)}, u32[]{:S(2)}, u32[]{:S(2)}) collective-permute-start(bf16[256,7168]{1,0:T(8,128)(2,1)} %pad_maximum_fusion.1.refs_0_), channel_id=1, source_target_pairs={{0,4},{1,5},{6,2},{7,3},{8,12},{9,13},{14,10},{15,11},{16,20},{17,... | collective-permute-start | bytes 11010056 | tf_op jit(solution)/shard_map/ppermute | solution.py:35
  103.5 89.8 %collective-permute-start.8 = (bf16[256,7168]{1,0:T(8,128)(2,1)}, bf16[256,7168]{1,0:T(8,128)(2,1)}, u32[]{:S(2)}, u32[]{:S(2)}) collective-permute-start(bf16[256,7168]{1,0:T(8,128)(2,1)} %pad_maximum_fusion.1.refs_0_), channel_id=1, source_target_pairs={{5,3},{3,5},{4,2},{2,4},{13,11},{11,13},{12,10},{10,12},{21,19},{1... | collective-permute-start | bytes 11010056 | tf_op jit(solution)/shard_map/ppermute | solution.py:35
  136.8 49.8 %all-to-all-start.2 = ((bf16[16,8,7168]{2,1,0:T(8,128)(2,1)}), bf16[16,8,7168]{2,1,0:T(8,128)(2,1)S(1)}, u32[]{:S(2)}, u32[]{:S(2)}) async-start(bf16[16,8,7168]{2,1,0:T(8,128)(2,1)} %bitcast.87), calls=%async_computation.2 | async-start | bytes 3670016 | tf_op jit(solution)/shard_map/all_to_all | solution.py:219
  186.7 19.0 %collective-permute-start.7 = (bf16[256,8960]{1,0:T(8,128)(2,1)}, bf16[256,8960]{1,0:T(8,128)(2,1)}, u32[]{:S(2)}, u32[]{:S(2)}) collective-permute-start(bf16[256,8960]{1,0:T(8,128)(2,1)} %collective-permute-done.5.refs_5_.near), channel_id=1, source_target_pairs={{0,4},{4,0},{1,5},{5,1},{2,6},{6,2},{3,7},{7,3},{8,12},{12,8},{9,1... | collective-permute-start | bytes 13762568 | tf_op jit(solution)/shard_map/ppermute | solution.py:35
  187.5 45.1 %collective-permute-start.10 = (bf16[256,8960]{1,0:T(8,128)(2,1)}, bf16[256,8960]{1,0:T(8,128)(2,1)}, u32[]{:S(2)}, u32[]{:S(2)}) collective-permute-start(bf16[256,8960]{1,0:T(8,128)(2,1)} %pad_maximum_fusion.refs_2_.own), channel_id=1, source_target_pairs={{5,3},{3,5},{4,2},{2,4},{13,11},{11,13},{12,10},{10,12},{21,19},{1... | collective-permute-start | bytes 13762568 | tf_op jit(solution)/shard_map/ppermute | solution.py:35
  190.3 10.2 %collective-permute-start.3 = (bf16[256,7168]{1,0:T(8,128)(2,1)}, bf16[256,7168]{1,0:T(8,128)(2,1)}, u32[]{:S(2)}, u32[]{:S(2)}) collective-permute-start(bf16[256,7168]{1,0:T(8,128)(2,1)} %bitcast.74), channel_id=1, source_target_pairs={{0,4},{1,5},{6,2},{7,3},{8,12},{9,13},{14,10},{15,11},{16,20},{17,... | collective-permute-start | bytes 11010056 | tf_op jit(solution)/shard_map/ppermute | solution.py:35
  193.4 12.3 %collective-permute-start.6 = (bf16[256,7168]{1,0:T(8,128)(2,1)}, bf16[256,7168]{1,0:T(8,128)(2,1)}, u32[]{:S(2)}, u32[]{:S(2)}) collective-permute-start(bf16[256,7168]{1,0:T(8,128)(2,1)} %collective-permute-done.4.refs_4_), channel_id=1, source_target_pairs={{0,4},{4,0},{1,5},{5,1},{2,6},{6,2},{3,7},{7,3},{8,12},{12,8},{9,1... | collective-permute-start | bytes 11010056 | tf_op jit(solution)/shard_map/ppermute | solution.py:35
  193.4 12.3 %collective-permute-start.9 = (bf16[256,7168]{1,0:T(8,128)(2,1)}, bf16[256,7168]{1,0:T(8,128)(2,1)}, u32[]{:S(2)}, u32[]{:S(2)}) collective-permute-start(bf16[256,7168]{1,0:T(8,128)(2,1)} %collective-permute-done.8.refs_9_), channel_id=1, source_target_pairs={{4,0},{5,1},{2,6},{3,7},{12,8},{13,9},{10,14},{11,15},{20,16},{21,... | collective-permute-start | bytes 11010056 | tf_op jit(solution)/shard_map/ppermute | solution.py:35
  205.7 28.3 %copy-start = (bf16[1,256,7168]{2,1,0:T(8,128)(2,1)S(1)}, bf16[1,256,7168]{2,1,0:T(8,128)(2,1)}, u32[]{:S(2)}) copy-start(bf16[1,256,7168]{2,1,0:T(8,128)(2,1)} %param.11) | copy-start | bytes 11010052
  232.7 22.4 %collective-permute-start.11 = (bf16[256,8960]{1,0:T(8,128)(2,1)}, bf16[256,8960]{1,0:T(8,128)(2,1)S(1)}, u32[]{:S(2)}, u32[]{:S(2)}) collective-permute-start(bf16[256,8960]{1,0:T(8,128)(2,1)} %collective-permute-done.10.refs_1_.far), channel_id=1, source_target_pairs={{4,0},{5,1},{2,6},{3,7},{12,8},{13,9},{10,14},{11,15},{20,16},{21,... | collective-permute-start | bytes 13762568 | tf_op jit(solution)/shard_map/ppermute | solution.py:35
  235.7 41.6 %collective-permute-start.12 = (bf16[256,2688]{1,0:T(8,128)(2,1)}, bf16[256,2688]{1,0:T(8,128)(2,1)}, u32[]{:S(2)}, u32[]{:S(2)}) collective-permute-start(bf16[256,2688]{1,0:T(8,128)(2,1)} %get-tuple-element.48), channel_id=1, source_target_pairs={{0,1},{1,0},{6,7},{7,6},{4,3},{3,4},{5,2},{2,5},{8,9},{9,8},{14,15... | collective-permute-start | bytes 4128776 | tf_op jit(solution)/shard_map/ppermute | solution.py:35
  238.0 46.0 %collective-permute-start.14 = (bf16[256,2688]{1,0:T(8,128)(2,1)}, bf16[256,2688]{1,0:T(8,128)(2,1)}, u32[]{:S(2)}, u32[]{:S(2)}) collective-permute-start(bf16[256,2688]{1,0:T(8,128)(2,1)} %get-tuple-element.48), channel_id=1, source_target_pairs={{5,3},{3,5},{4,2},{2,4},{13,11},{11,13},{12,10},{10,12},{21,19},{1... | collective-permute-start | bytes 4128776 | tf_op jit(solution)/shard_map/ppermute | solution.py:35
  255.1 2.1 copy-start.6
  270.1 34.2 %all-to-all-start.3 = ((bf16[32,16,1792]{2,1,0:T(8,128)(2,1)}), bf16[32,16,1792]{2,1,0:T(8,128)(2,1)}, u32[]{:S(2)}, u32[]{:S(2)}) async-start(bf16[32,16,1792]{2,1,0:T(8,128)(2,1)} %get-tuple-element.46), calls=%async_computation.3 | async-start | bytes 3670016 | tf_op jit(solution)/shard_map/all_to_all | solution.py:215
  277.4 9.8 %collective-permute-start.13 = (bf16[256,2688]{1,0:T(8,128)(2,1)}, bf16[256,2688]{1,0:T(8,128)(2,1)S(1)}, u32[]{:S(2)}, u32[]{:S(2)}) collective-permute-start(bf16[256,2688]{1,0:T(8,128)(2,1)} %collective-permute-done.12.near), channel_id=1, source_target_pairs={{0,4},{4,0},{1,5},{5,1},{2,6},{6,2},{3,7},{7,3},{8,12},{12,8},{9,1... | collective-permute-start | bytes 4128776 | tf_op jit(solution)/shard_map/ppermute | solution.py:35
  284.0 5.2 %collective-permute-start.15 = (bf16[256,2688]{1,0:T(8,128)(2,1)}, bf16[256,2688]{1,0:T(8,128)(2,1)S(1)}, u32[]{:S(2)}, u32[]{:S(2)}) collective-permute-start(bf16[256,2688]{1,0:T(8,128)(2,1)} %collective-permute-done.14.far), channel_id=1, source_target_pairs={{4,0},{5,1},{2,6},{3,7},{12,8},{13,9},{10,14},{11,15},{20,16},{21,... | collective-permute-start | bytes 4128776 | tf_op jit(solution)/shard_map/ppermute | solution.py:35
  285.3 29.1 %collective-permute-start.16 = (bf16[256,2688]{1,0:T(8,128)(2,1)}, bf16[256,2688]{1,0:T(8,128)(2,1)S(1)}, u32[]{:S(2)}, u32[]{:S(2)}) collective-permute-start(bf16[256,2688]{1,0:T(8,128)(2,1)} %get-tuple-element.52), channel_id=1, source_target_pairs={{0,1},{1,0},{6,7},{7,6},{4,3},{3,4},{5,2},{2,5},{8,9},{9,8},{14,15... | collective-permute-start | bytes 4128776 | tf_op jit(solution)/shard_map/ppermute | solution.py:35
  285.4 35.5 %collective-permute-start.18 = (bf16[256,2688]{1,0:T(8,128)(2,1)}, bf16[256,2688]{1,0:T(8,128)(2,1)}, u32[]{:S(2)}, u32[]{:S(2)}) collective-permute-start(bf16[256,2688]{1,0:T(8,128)(2,1)} %get-tuple-element.52), channel_id=1, source_target_pairs={{5,3},{3,5},{4,2},{2,4},{13,11},{11,13},{12,10},{10,12},{21,19},{1... | collective-permute-start | bytes 4128776 | tf_op jit(solution)/shard_map/ppermute | solution.py:35
  289.2 2.0 copy-start.1
  297.8 1.5 copy-start.3
  299.3 0.8 copy-start.4
  304.3 42.3 %all-to-all-start.4 = ((bf16[32,16,2688]{2,1,0:T(8,128)(2,1)}), bf16[32,16,2688]{2,1,0:T(8,128)(2,1)}, u32[]{:S(2)}, u32[]{:S(2)}) async-start(bf16[32,16,2688]{2,1,0:T(8,128)(2,1)} %copy-done.3), calls=%async_computation.4 | async-start | bytes 5505024 | tf_op jit(solution)/shard_map/all_to_all | solution.py:215
  314.4 9.3 %collective-permute-start.17 = (bf16[256,2688]{1,0:T(8,128)(2,1)S(1)}, bf16[256,2688]{1,0:T(8,128)(2,1)S(1)}, u32[]{:S(2)}, u32[]{:S(2)}) collective-permute-start(bf16[256,2688]{1,0:T(8,128)(2,1)S(1)} %collective-permute-done.16.near), channel_id=1, source_target_pairs={{0,4},{4,0},{1,5},{5,1},{2,6},{6,2},{3,7},{7,3},{8,12},{12,8},{9,1... | collective-permute-start | bytes 4128776 | tf_op jit(solution)/shard_map/ppermute | solution.py:35
  320.9 5.2 %collective-permute-start.19 = (bf16[256,2688]{1,0:T(8,128)(2,1)}, bf16[256,2688]{1,0:T(8,128)(2,1)S(1)}, u32[]{:S(2)}, u32[]{:S(2)}) collective-permute-start(bf16[256,2688]{1,0:T(8,128)(2,1)} %collective-permute-done.18.far), channel_id=1, source_target_pairs={{4,0},{5,1},{2,6},{3,7},{12,8},{13,9},{10,14},{11,15},{20,16},{21,... | collective-permute-start | bytes 4128776 | tf_op jit(solution)/shard_map/ppermute | solution.py:35
  326.1 2.0 copy-start.2
  328.2 7.1 %copy-start.5 = (bf16[128,2688]{1,0:T(8,128)(2,1)S(1)}, bf16[128,2688]{1,0:T(8,128)(2,1)}, u32[]{:S(2)}) copy-start(bf16[128,2688]{1,0:T(8,128)(2,1)} %copy-done.4) | copy-start | bytes 2064388
  346.6 30.0 %all-to-all-start.5 = ((bf16[16,8,7168]{2,1,0:T(8,128)(2,1)}), bf16[16,8,7168]{2,1,0:T(8,128)(2,1)S(1)}, u32[]{:S(2)}, u32[]{:S(2)}) async-start(bf16[16,8,7168]{2,1,0:T(8,128)(2,1)} %bitcast.86), calls=%async_computation.5 | async-start | bytes 3670016 | tf_op jit(solution)/shard_map/all_to_all | solution.py:219
  376.6 1.2 copy-start.9
  377.8 41.6 %all-to-all-start.6 = ((bf16[32,16,2688]{2,1,0:T(8,128)(2,1)}), bf16[32,16,2688]{2,1,0:T(8,128)(2,1)S(1)}, u32[]{:S(2)}, u32[]{:S(2)}) async-start(bf16[32,16,2688]{2,1,0:T(8,128)(2,1)} %bitcast.35), calls=%async_computation.6 | async-start | bytes 5505024 | tf_op jit(solution)/shard_map/all_to_all | solution.py:215
  385.5 2.0 copy-start.7
  385.7 9.4 %collective-permute-start.20 = (bf16[64,1792]{1,0:T(8,128)(2,1)S(1)}, bf16[64,1792]{1,0:T(8,128)(2,1)S(1)}, u32[]{:S(2)}, u32[]{:S(2)}) collective-permute-start(bf16[64,1792]{1,0:T(8,128)(2,1)S(1)} %slice.193), channel_id=1, source_target_pairs={{0,3},{3,0},{1,2},{2,1},{4,7},{7,4},{5,6},{6,5},{8,11},{11,8},{9,1... | collective-permute-start | bytes 688136 | tf_op jit(solution)/shard_map/ppermute | solution.py:170
  389.4 5.7 %copy-start.10 = (f32[128,2688]{1,0:T(8,128)}, f32[128,2688]{1,0:T(8,128)S(1)}, u32[]{:S(2)}) copy-start(f32[128,2688]{1,0:T(8,128)S(1)} %slice_add_fusion.1) | copy-start | bytes 4128772
  390.2 33.9 %collective-permute-start.21 = (bf16[64,2688]{1,0:T(8,128)(2,1)}, bf16[64,2688]{1,0:T(8,128)(2,1)}, u32[]{:S(2)}, u32[]{:S(2)}) collective-permute-start(bf16[64,2688]{1,0:T(8,128)(2,1)} %slice.192), channel_id=1, source_target_pairs={{0,3},{3,0},{1,2},{2,1},{4,7},{7,4},{5,6},{6,5},{8,11},{11,8},{9,1... | collective-permute-start | bytes 1032200 | tf_op jit(solution)/shard_map/ppermute | solution.py:170
  422.0 2.1 copy-start.11
  422.2 9.0 %collective-permute-start.22 = (bf16[64,2688]{1,0:T(8,128)(2,1)S(1)}, bf16[64,2688]{1,0:T(8,128)(2,1)S(1)}, u32[]{:S(2)}, u32[]{:S(2)}) collective-permute-start(bf16[64,2688]{1,0:T(8,128)(2,1)S(1)} %slice.191), channel_id=1, source_target_pairs={{0,3},{3,0},{1,2},{2,1},{4,7},{7,4},{5,6},{6,5},{8,11},{11,8},{9,1... | collective-permute-start | bytes 1032200 | tf_op jit(solution)/shard_map/ppermute | solution.py:170

commit v4 on v3

--- a/solution.py
+++ b/solution.py
@@ -230,9 +230,9 @@
         jnp.concatenate(
             [after(gate_weight[0], got)[at : at + HALF], up_weight[0][at : at + HALF]], axis=0
         )
-        for at, got in ((0, sent), (HALF, other))
+        for at, got in ((0, other), (HALF, other))
     ]
-    owns[1] = jnp.concatenate([owns[1], down_weight[0][:, : STEPS[0]]], axis=1)
+    owns[0] = jnp.concatenate([owns[0], down_weight[0][:, : STEPS[0]]], axis=1)
     nears = [along(own, NEXT) for own in owns]
 
     pick, other_rest, mix_other, mix_other_rest = slots(other_routes, 1)
@@ -266,7 +266,7 @@
     brought_1 = along(after(fars[1], first), TO_HOME)
     down_1 = columns(STEPS[0], STEPS[1], fars[1], first)
     last = hidden_units(flag, after(mine, first), theirs, rest, [(brought_1, fars[1])])
-    panels = owns[1], copied[1], nears[1], across[1], brought_1, fars[1]
+    panels = owns[0], copied[0], nears[0], across[0], brought_0, fars[0]
     result_0 = down_rows(flag, first, last, panels, STEPS[0], (width,) * 6)
     at = STEPS[0] + STEPS[1]
     down_2 = columns(at, STEPS[2], down_1[1], result_0[0])

time: 434 us -> 439 us (1.012)
  waiting for transfers between devices: 231 us -> 212 us
  starting transfers between devices: 91.1 us -> 109 us
  other arithmetic: 13.6 us -> 18.2 us
    ppermute x19, waiting for transfers between devices: 83.3 us -> 35.6 us  [along(): return lax.ppermute(value, COL, pairs)]
    all_to_all x5, waiting for transfers between devices: 65.8 us -> 108 us  [exchange_main(): return lax.all_to_all(parts, EXP, 0, 0, tiled=True).reshape(rows.shape)]
    ppermute x4, waiting for transfers between devices: 60.2 us -> 20.8 us  [pair_exchange(): return lax.ppermute(value, ('zh', 'zl'), PAIR)]
    all_to_all x2, waiting for transfers between devices: 21.5 us -> 47.9 us  [exchange_rest(): lax.all_to_all(parts, ('y', 'x'), 0, 0, tiled=True).reshape(rows.shape)]
    ppermute x19, starting transfers between devices: 45 us -> 60.1 us  [along(): return lax.ppermute(value, COL, pairs)]
    ppermute x4, starting transfers between devices: 5.63 us -> 10.2 us  [pair_exchange(): return lax.ppermute(value, ('zh', 'zl'), PAIR)]
    unnamed x33 -> x31, local copies, waits for them, and re-layouts: 9.89 us -> 10.4 us
  transfers between devices with their start and end apart: 30 -> 30, of which waited for: 16 -> 17; matrix products, arithmetic and copies ran while one was open for 8% -> 9% of each run, Pallas kernels for 12% -> 12%
where the time goes in v4:
time: 439 us; the launch traced here: 438 us
  waiting for transfers between devices  212 us (48%)
  starting transfers between devices  109 us (25%)
  Pallas kernels  53.4 us (12%)
  matrix products  22.8 us (5%)
  local copies, waits for them, and re-layouts  21.9 us (5%)
  other arithmetic  18.2 us (4%)
    all_to_all x5, waiting for transfers between devices, exchange_main(): return lax.all_to_all(parts, EXP, 0, 0, tiled=True).reshape(rows.shape)  108 us
    ppermute x19, starting transfers between devices, along(): return lax.ppermute(value, COL, pairs)  60.1 us
    all_to_all x2, waiting for transfers between devices, exchange_rest(): lax.all_to_all(parts, ('y', 'x'), 0, 0, tiled=True).reshape(rows.shape)  47.9 us
    ppermute x19, waiting for transfers between devices, along(): return lax.ppermute(value, COL, pairs)  35.6 us
    pallas_call x2, Pallas kernels, hidden_units(): pl.pallas_call(functools.partial(hidden_kernel, kinds=kinds), grid_spec=p...  33.9 us
    all_to_all x5, starting transfers between devices, exchange_main(): return lax.all_to_all(parts, EXP, 0, 0, tiled=True).reshape(rows.shape)  31.4 us
    ppermute x4, waiting for transfers between devices, pair_exchange(): return lax.ppermute(value, ('zh', 'zl'), PAIR)  20.8 us
    pallas_call x3, Pallas kernels, down_rows(): pl.pallas_call(down_kernel, grid_spec=pltpu.PrefetchScalarGridSpec(num_sc...  19.5 us
  transfers between devices with their start and end apart: 30, of which 17 were waited for; matrix products, arithmetic and copies ran while one was open for 9% of the time, Pallas kernels for 12%

profile of v4, /device:TPU:0, one launch (start us, length us, event | category | flops | bytes accessed | tf_op | source)
XLA Modules:
  0.0 437.7 jit_solution(7541927535420587577)
XLA Ops:
  1.5 2.2 fusion.6
  3.7 4.1 collective-permute-start
  7.8 3.6 slice_bitcast_fusion
  13.1 3.0 convolution_convert_fusion.1
  16.2 12.6 %collective-permute-done = bf16[64,7296]{1,0:T(8,128)(2,1)} collective-permute-done((bf16[64,7296]{1,0:T(8,128)(2,1)}, bf16[64,7296]{1,0:T(8,128)(2,1)}, u32[]{:S(2)}, u32[]{:S(2)}) %collective-permute-start) | collective-permute-done | bytes 933920 | tf_op jit(solution)/shard_map/ppermute | solution.py:170
  28.8 2.2 slice.110
  33.1 5.4 %pad_maximum_fusion.refs_0_.own = bf16[256,8960]{1,0:T(8,128)(2,1)} fusion(bf16[256,1792]{1,0:T(8,128)(2,1)S(1)} %slice.142, bf16[128,7168]{1,0:T(8,128)(2,1)S(1)} %copy-done.9, bf16[128,7168]{1,0:T(8,128)(2,1)S(1)} %get-tuple-element.66), kind=kLoop, calls=%fused_computation.3 | loop fusion | flops 13762560 | bytes 9175040 | tf_op jit(solution)/shard_map/concatenate | solution.py:235
  38.5 10.1 %all-to-all-start = ((bf16[32,8,7168]{2,1,0:T(8,128)(2,1)}), bf16[32,8,7168]{2,1,0:T(8,128)(2,1)}, u32[]{:S(2)}, u32[]{:S(2)}) async-start(bf16[32,8,7168]{2,1,0:T(8,128)(2,1)} %bitcast.81), calls=%async_computation | async-start | bytes 7340032 | tf_op jit(solution)/shard_map/all_to_all | solution.py:215
  49.9 4.1 convolution_convert_fusion
  54.0 42.2 %all-to-all-done = bf16[32,8,7168]{2,1,0:T(8,128)(2,1)} async-done(((bf16[32,8,7168]{2,1,0:T(8,128)(2,1)}), bf16[32,8,7168]{2,1,0:T(8,128)(2,1)}, u32[]{:S(2)}, u32[]{:S(2)}) %all-to-all-start) | async-done | bytes 3670048 | tf_op jit(solution)/shard_map/all_to_all | solution.py:215
  96.3 4.8 %all-to-all-start.1 = ((bf16[32,8,7168]{2,1,0:T(8,128)(2,1)}), bf16[32,8,7168]{2,1,0:T(8,128)(2,1)}, u32[]{:S(2)}, u32[]{:S(2)}) async-start(bf16[32,8,7168]{2,1,0:T(8,128)(2,1)} %bitcast.80), calls=%async_computation.1 | async-start | bytes 7340032 | tf_op jit(solution)/shard_map/all_to_all | solution.py:215
  101.1 2.7 collective-permute-start.8
  103.9 3.5 collective-permute-start.1
  107.3 3.5 pad_maximum_fusion.1.refs_2_
  110.9 3.1 collective-permute-start.2
  113.9 2.2 collective-permute-start.5
  116.4 3.1 convolution_convert_fusion.2
  119.5 29.3 %all-to-all-done.1 = bf16[32,8,7168]{2,1,0:T(8,128)(2,1)} async-done(((bf16[32,8,7168]{2,1,0:T(8,128)(2,1)}), bf16[32,8,7168]{2,1,0:T(8,128)(2,1)}, u32[]{:S(2)}, u32[]{:S(2)}) %all-to-all-start.1) | async-done | bytes 3670048 | tf_op jit(solution)/shard_map/all_to_all | solution.py:215
  148.8 3.7 all-to-all-start.2
  152.6 26.3 %all-to-all-done.2 = bf16[16,8,7168]{2,1,0:T(8,128)(2,1)S(1)} async-done(((bf16[16,8,7168]{2,1,0:T(8,128)(2,1)}), bf16[16,8,7168]{2,1,0:T(8,128)(2,1)S(1)}, u32[]{:S(2)}, u32[]{:S(2)}) %all-to-all-start.2) | async-done | bytes 1835040 | tf_op jit(solution)/shard_map/all_to_all | solution.py:219
  180.3 22.7 %collective-permute-start.3 = (bf16[256,7168]{1,0:T(8,128)(2,1)}, bf16[256,7168]{1,0:T(8,128)(2,1)}, u32[]{:S(2)}, u32[]{:S(2)}) collective-permute-start(bf16[256,7168]{1,0:T(8,128)(2,1)} %bitcast.74), channel_id=1, source_target_pairs={{0,4},{1,5},{6,2},{7,3},{8,12},{9,13},{14,10},{15,11},{16,20},{17,... | collective-permute-start | bytes 11010056 | tf_op jit(solution)/shard_map/ppermute | solution.py:35
  203.0 2.5 collective-permute-start.10
  207.4 5.2 %collective-permute-done.7.refs_7_ = bf16[256,7168]{1,0:T(8,128)(2,1)} collective-permute-done((bf16[256,7168]{1,0:T(8,128)(2,1)}, bf16[256,7168]{1,0:T(8,128)(2,1)}, u32[]{:S(2)}, u32[]{:S(2)}) %collective-permute-start.7) | collective-permute-done | bytes 3670048 | tf_op jit(solution)/shard_map/ppermute | solution.py:35
  212.7 26.9 %shard_map.64.first = bf16[640,896]{1,0:T(8,128)(2,1)S(1)} custom-call(s32[1]{0:T(128)} %bitcast.4.flag, bf16[256,7168]{1,0:T(8,128)(2,1)} %bitcast.6.mine, bf16[256,7168]{1,0:T(8,128)(2,1)} %bitcast.14.theirs, bf16[128,7168]{1,0:T(8,128)(2,1)S(1)} %bitcast.78, bf16[256,8960]{1,0:T(8,128)(2,1)} %pad_maximum_fusion.refs_0_.own, ...), custom_call_target="tpu_custom_call" | custom-call | flops 1 | bytes 1 | tf_op jit(solution)/shard_map/pallas_call | solution.py:95
  244.5 16.0 %collective-permute-done.11.refs_0_ = bf16[256,7168]{1,0:T(8,128)(2,1)S(1)} collective-permute-done((bf16[256,7168]{1,0:T(8,128)(2,1)}, bf16[256,7168]{1,0:T(8,128)(2,1)S(1)}, u32[]{:S(2)}, u32[]{:S(2)}) %collective-permute-start.11) | collective-permute-done | bytes 3670048 | tf_op jit(solution)/shard_map/ppermute | solution.py:35
  262.2 7.0 %shard_map.65.last = bf16[640,128]{1,0:T(8,128)(2,1)S(1)} custom-call(s32[1]{0:T(128)} %bitcast.4.flag, bf16[256,7168]{1,0:T(8,128)(2,1)} %bitcast.6.mine, bf16[256,7168]{1,0:T(8,128)(2,1)} %bitcast.14.theirs, bf16[128,7168]{1,0:T(8,128)(2,1)S(1)} %bitcast.79, bf16[256,7168]{1,0:T(8,128)(2,1)} %copy-done.12, bf16[256,7168]{1,0:T(8,128)(2,1)} %collective-permute-done.10.refs_1_), custom_call_target="tpu_custom_call" | custom-call | flops 1 | bytes 1 | tf_op jit(solution)/shard_map/pallas_call | solution.py:95
  269.2 5.9 %shard_map.66 = (bf16[32,16,1792]{2,1,0:T(8,128)(2,1)}, bf16[128,1792]{1,0:T(8,128)(2,1)S(1)}) custom-call(s32[1]{0:T(128)} %bitcast.4.flag, bf16[640,896]{1,0:T(8,128)(2,1)S(1)} %shard_map.64.first, bf16[640,128]{1,0:T(8,128)(2,1)S(1)} %shard_map.65.last, bf16[256,8960]{1,0:T(8,128)(2,1)} %pad_maximum_fusion.refs_0_.own, ...), custom_call_target="tpu_custom_call" | custom-call | flops 2348810240 | bytes 7274496 | tf_op jit(solution)/shard_map/pallas_call | solution.py:140
  275.1 7.5 %all-to-all-start.3 = ((bf16[32,16,1792]{2,1,0:T(8,128)(2,1)}), bf16[32,16,1792]{2,1,0:T(8,128)(2,1)}, u32[]{:S(2)}, u32[]{:S(2)}) async-start(bf16[32,16,1792]{2,1,0:T(8,128)(2,1)} %get-tuple-element.44), calls=%async_computation.3 | async-start | bytes 3670016 | tf_op jit(solution)/shard_map/all_to_all | solution.py:215
  282.7 7.9 %collective-permute-start.13 = (bf16[256,2688]{1,0:T(8,128)(2,1)}, bf16[256,2688]{1,0:T(8,128)(2,1)S(1)}, u32[]{:S(2)}, u32[]{:S(2)}) collective-permute-start(bf16[256,2688]{1,0:T(8,128)(2,1)} %collective-permute-done.12.near), channel_id=1, source_target_pairs={{0,4},{4,0},{1,5},{5,1},{2,6},{6,2},{3,7},{7,3},{8,12},{12,8},{9,1... | collective-permute-start | bytes 4128776 | tf_op jit(solution)/shard_map/ppermute | solution.py:35
  293.8 2.1 collective-permute-done.15.brought
  297.9 6.5 %shard_map.67 = (bf16[32,16,2688]{2,1,0:T(8,128)(2,1)S(1)}, bf16[128,2688]{1,0:T(8,128)(2,1)S(1)}) custom-call(s32[1]{0:T(128)} %bitcast.4.flag, bf16[640,896]{1,0:T(8,128)(2,1)S(1)} %shard_map.64.first, bf16[640,128]{1,0:T(8,128)(2,1)S(1)} %shard_map.65.last, bf16[256,7168]{1,0:T(8,128)(2,1)S(1)} %bitcast.76, ...), custom_call_target="tpu_custom_call" | custom-call | flops 3523215360 | bytes 10256384 | tf_op jit(solution)/shard_map/pallas_call | solution.py:140
  306.8 2.8 all-to-all-done.3
  309.6 4.8 %all-to-all-start.4 = ((bf16[32,16,2688]{2,1,0:T(8,128)(2,1)}), bf16[32,16,2688]{2,1,0:T(8,128)(2,1)}, u32[]{:S(2)}, u32[]{:S(2)}) async-start(bf16[32,16,2688]{2,1,0:T(8,128)(2,1)} %copy-done.3), calls=%async_computation.4 | async-start | bytes 5505024 | tf_op jit(solution)/shard_map/all_to_all | solution.py:215
  314.4 6.6 %collective-permute-done.16.near = bf16[256,2688]{1,0:T(8,128)(2,1)S(1)} collective-permute-done((bf16[256,2688]{1,0:T(8,128)(2,1)}, bf16[256,2688]{1,0:T(8,128)(2,1)S(1)}, u32[]{:S(2)}, u32[]{:S(2)}) %collective-permute-start.16) | collective-permute-done | bytes 1376288 | tf_op jit(solution)/shard_map/ppermute | solution.py:35
  321.0 6.5 %collective-permute-start.17 = (bf16[256,2688]{1,0:T(8,128)(2,1)S(1)}, bf16[256,2688]{1,0:T(8,128)(2,1)S(1)}, u32[]{:S(2)}, u32[]{:S(2)}) collective-permute-start(bf16[256,2688]{1,0:T(8,128)(2,1)S(1)} %collective-permute-done.16.near), channel_id=1, source_target_pairs={{0,4},{4,0},{1,5},{5,1},{2,6},{6,2},{3,7},{7,3},{8,12},{12,8},{9,1... | collective-permute-start | bytes 4128776 | tf_op jit(solution)/shard_map/ppermute | solution.py:35
  330.3 2.5 collective-permute-done.19.brought
  334.8 7.1 %shard_map.68 = (bf16[32,16,2688]{2,1,0:T(8,128)(2,1)}, bf16[128,2688]{1,0:T(8,128)(2,1)S(1)}) custom-call(s32[1]{0:T(128)} %bitcast.4.flag, bf16[640,896]{1,0:T(8,128)(2,1)S(1)} %shard_map.64.first, bf16[640,128]{1,0:T(8,128)(2,1)S(1)} %shard_map.65.last, bf16[256,7168]{1,0:T(8,128)(2,1)S(1)} %bitcast.77, bf16[256,7168]{1,0:T(8,128)(2,1)} %collective-permute-done.3.copied, ...), custom_call_target="tpu_custom_call" | custom-call | flops 3523215360 | bytes 10256384 | tf_op jit(solution)/shard_map/pallas_call | solution.py:140
  343.3 8.6 %all-to-all-done.4 = bf16[32,16,2688]{2,1,0:T(8,128)(2,1)} async-done(((bf16[32,16,2688]{2,1,0:T(8,128)(2,1)}), bf16[32,16,2688]{2,1,0:T(8,128)(2,1)}, u32[]{:S(2)}, u32[]{:S(2)}) %all-to-all-start.4) | async-done | bytes 2752544 | tf_op jit(solution)/shard_map/all_to_all | solution.py:215
  351.9 3.7 all-to-all-start.5
  356.1 4.3 fusion.16
  360.5 21.5 %all-to-all-done.5 = bf16[16,8,7168]{2,1,0:T(8,128)(2,1)S(1)} async-done(((bf16[16,8,7168]{2,1,0:T(8,128)(2,1)}), bf16[16,8,7168]{2,1,0:T(8,128)(2,1)S(1)}, u32[]{:S(2)}, u32[]{:S(2)}) %all-to-all-start.5) | async-done | bytes 1835040 | tf_op jit(solution)/shard_map/all_to_all | solution.py:219
  383.2 4.1 all-to-all-start.6
  388.7 2.2 convolution_add_fusion.2
  391.1 2.3 collective-permute-start.20
  397.6 2.5 collective-permute-done.20
  400.1 24.6 %all-to-all-done.6 = bf16[32,16,2688]{2,1,0:T(8,128)(2,1)S(1)} async-done(((bf16[32,16,2688]{2,1,0:T(8,128)(2,1)}), bf16[32,16,2688]{2,1,0:T(8,128)(2,1)S(1)}, u32[]{:S(2)}, u32[]{:S(2)}) %all-to-all-start.6) | async-done | bytes 2752544 | tf_op jit(solution)/shard_map/all_to_all | solution.py:215
  427.6 2.3 collective-permute-start.22
  430.9 5.7 %collective-permute-done.22 = bf16[64,2688]{1,0:T(8,128)(2,1)S(1)} collective-permute-done((bf16[64,2688]{1,0:T(8,128)(2,1)S(1)}, bf16[64,2688]{1,0:T(8,128)(2,1)S(1)}, u32[]{:S(2)}, u32[]{:S(2)}) %collective-permute-start.22) | collective-permute-done | bytes 344096 | tf_op jit(solution)/shard_map/ppermute | solution.py:170
  (107 shorter events, 43.0 us)
Async XLA Ops:
  3.7 25.1 %collective-permute-start = (bf16[64,7296]{1,0:T(8,128)(2,1)}, bf16[64,7296]{1,0:T(8,128)(2,1)}, u32[]{:S(2)}, u32[]{:S(2)}) collective-permute-start(bf16[64,7296]{1,0:T(8,128)(2,1)} %fusion.6), channel_id=1, source_target_pairs={{0,3},{3,0},{1,2},{2,1},{4,7},{7,4},{5,6},{6,5},{8,11},{11,8},{9,1... | collective-permute-start | bytes 2801672 | tf_op jit(solution)/shard_map/ppermute | solution.py:170
  11.3 1.4 copy-start.14
  11.3 1.8 copy-start.7
  13.1 17.8 %copy-start.13 = (bf16[1,256,7168]{2,1,0:T(8,128)(2,1)S(1)}, bf16[1,256,7168]{2,1,0:T(8,128)(2,1)}, u32[]{:S(2)}) copy-start(bf16[1,256,7168]{2,1,0:T(8,128)(2,1)} %param.9) | copy-start | bytes 11010052
  31.0 2.2 copy-start.9
  38.5 57.8 %collective-permute-start.4 = (bf16[256,8960]{1,0:T(8,128)(2,1)}, bf16[256,8960]{1,0:T(8,128)(2,1)}, u32[]{:S(2)}, u32[]{:S(2)}) collective-permute-start(bf16[256,8960]{1,0:T(8,128)(2,1)} %pad_maximum_fusion.refs_0_.own), channel_id=1, source_target_pairs={{0,1},{1,0},{6,7},{7,6},{4,3},{3,4},{5,2},{2,5},{8,9},{9,8},{14,15... | collective-permute-start | bytes 13762568 | tf_op jit(solution)/shard_map/ppermute | solution.py:35
  38.5 57.8 %all-to-all-start = ((bf16[32,8,7168]{2,1,0:T(8,128)(2,1)}), bf16[32,8,7168]{2,1,0:T(8,128)(2,1)}, u32[]{:S(2)}, u32[]{:S(2)}) async-start(bf16[32,8,7168]{2,1,0:T(8,128)(2,1)} %bitcast.81), calls=%async_computation | async-start | bytes 7340032 | tf_op jit(solution)/shard_map/all_to_all | solution.py:215
  96.3 52.5 %all-to-all-start.1 = ((bf16[32,8,7168]{2,1,0:T(8,128)(2,1)}), bf16[32,8,7168]{2,1,0:T(8,128)(2,1)}, u32[]{:S(2)}, u32[]{:S(2)}) async-start(bf16[32,8,7168]{2,1,0:T(8,128)(2,1)} %bitcast.80), calls=%async_computation.1 | async-start | bytes 7340032 | tf_op jit(solution)/shard_map/all_to_all | solution.py:215
  101.1 51.5 %collective-permute-start.8 = (bf16[256,8960]{1,0:T(8,128)(2,1)}, bf16[256,8960]{1,0:T(8,128)(2,1)}, u32[]{:S(2)}, u32[]{:S(2)}) collective-permute-start(bf16[256,8960]{1,0:T(8,128)(2,1)} %pad_maximum_fusion.refs_0_.own), channel_id=1, source_target_pairs={{5,3},{3,5},{4,2},{2,4},{13,11},{11,13},{12,10},{10,12},{21,19},{1... | collective-permute-start | bytes 13762568 | tf_op jit(solution)/shard_map/ppermute | solution.py:35
  103.9 76.4 %collective-permute-start.1 = (bf16[256,8960]{1,0:T(8,128)(2,1)}, bf16[256,8960]{1,0:T(8,128)(2,1)}, u32[]{:S(2)}, u32[]{:S(2)}) collective-permute-start(bf16[256,8960]{1,0:T(8,128)(2,1)} %pad_maximum_fusion.refs_0_.own), channel_id=1, source_target_pairs={{0,4},{1,5},{6,2},{7,3},{8,12},{9,13},{14,10},{15,11},{16,20},{17,... | collective-permute-start | bytes 13762568 | tf_op jit(solution)/shard_map/ppermute | solution.py:35
  110.9 69.4 %collective-permute-start.2 = (bf16[256,7168]{1,0:T(8,128)(2,1)}, bf16[256,7168]{1,0:T(8,128)(2,1)}, u32[]{:S(2)}, u32[]{:S(2)}) collective-permute-start(bf16[256,7168]{1,0:T(8,128)(2,1)} %pad_maximum_fusion.1.refs_2_), channel_id=1, source_target_pairs={{0,4},{1,5},{6,2},{7,3},{8,12},{9,13},{14,10},{15,11},{16,20},{17,... | collective-permute-start | bytes 11010056 | tf_op jit(solution)/shard_map/ppermute | solution.py:35
  113.9 89.0 %collective-permute-start.5 = (bf16[256,7168]{1,0:T(8,128)(2,1)}, bf16[256,7168]{1,0:T(8,128)(2,1)}, u32[]{:S(2)}, u32[]{:S(2)}) collective-permute-start(bf16[256,7168]{1,0:T(8,128)(2,1)} %pad_maximum_fusion.1.refs_2_), channel_id=1, source_target_pairs={{0,1},{1,0},{6,7},{7,6},{4,3},{3,4},{5,2},{2,5},{8,9},{9,8},{14,15... | collective-permute-start | bytes 11010056 | tf_op jit(solution)/shard_map/ppermute | solution.py:35
  148.8 30.2 %all-to-all-start.2 = ((bf16[16,8,7168]{2,1,0:T(8,128)(2,1)}), bf16[16,8,7168]{2,1,0:T(8,128)(2,1)S(1)}, u32[]{:S(2)}, u32[]{:S(2)}) async-start(bf16[16,8,7168]{2,1,0:T(8,128)(2,1)} %bitcast.87), calls=%async_computation.2 | async-start | bytes 3670016 | tf_op jit(solution)/shard_map/all_to_all | solution.py:219
  152.5 54.9 %collective-permute-start.6 = (bf16[256,8960]{1,0:T(8,128)(2,1)}, bf16[256,8960]{1,0:T(8,128)(2,1)}, u32[]{:S(2)}, u32[]{:S(2)}) collective-permute-start(bf16[256,8960]{1,0:T(8,128)(2,1)} %collective-permute-done.4.refs_4_.near), channel_id=1, source_target_pairs={{0,4},{4,0},{1,5},{5,1},{2,6},{6,2},{3,7},{7,3},{8,12},{12,8},{9,1... | collective-permute-start | bytes 13762568 | tf_op jit(solution)/shard_map/ppermute | solution.py:35
  179.0 33.7 %collective-permute-start.9 = (bf16[256,8960]{1,0:T(8,128)(2,1)}, bf16[256,8960]{1,0:T(8,128)(2,1)}, u32[]{:S(2)}, u32[]{:S(2)}) collective-permute-start(bf16[256,8960]{1,0:T(8,128)(2,1)} %collective-permute-done.8.refs_9_.far), channel_id=1, source_target_pairs={{4,0},{5,1},{2,6},{3,7},{12,8},{13,9},{10,14},{11,15},{20,16},{21,... | collective-permute-start | bytes 13762568 | tf_op jit(solution)/shard_map/ppermute | solution.py:35
  180.3 27.2 %collective-permute-start.3 = (bf16[256,7168]{1,0:T(8,128)(2,1)}, bf16[256,7168]{1,0:T(8,128)(2,1)}, u32[]{:S(2)}, u32[]{:S(2)}) collective-permute-start(bf16[256,7168]{1,0:T(8,128)(2,1)} %bitcast.74), channel_id=1, source_target_pairs={{0,4},{1,5},{6,2},{7,3},{8,12},{9,13},{14,10},{15,11},{16,20},{17,... | collective-permute-start | bytes 11010056 | tf_op jit(solution)/shard_map/ppermute | solution.py:35
  203.0 9.7 %collective-permute-start.7 = (bf16[256,7168]{1,0:T(8,128)(2,1)}, bf16[256,7168]{1,0:T(8,128)(2,1)}, u32[]{:S(2)}, u32[]{:S(2)}) collective-permute-start(bf16[256,7168]{1,0:T(8,128)(2,1)} %collective-permute-done.5.refs_5_), channel_id=1, source_target_pairs={{0,4},{4,0},{1,5},{5,1},{2,6},{6,2},{3,7},{7,3},{8,12},{12,8},{9,1... | collective-permute-start | bytes 11010056 | tf_op jit(solution)/shard_map/ppermute | solution.py:35
  203.0 36.7 %collective-permute-start.10 = (bf16[256,7168]{1,0:T(8,128)(2,1)}, bf16[256,7168]{1,0:T(8,128)(2,1)}, u32[]{:S(2)}, u32[]{:S(2)}) collective-permute-start(bf16[256,7168]{1,0:T(8,128)(2,1)} %pad_maximum_fusion.1.refs_2_), channel_id=1, source_target_pairs={{5,3},{3,5},{4,2},{2,4},{13,11},{11,13},{12,10},{10,12},{21,19},{1... | collective-permute-start | bytes 11010056 | tf_op jit(solution)/shard_map/ppermute | solution.py:35
  212.7 28.3 %copy-start = (bf16[1,256,7168]{2,1,0:T(8,128)(2,1)S(1)}, bf16[1,256,7168]{2,1,0:T(8,128)(2,1)}, u32[]{:S(2)}) copy-start(bf16[1,256,7168]{2,1,0:T(8,128)(2,1)} %param.11) | copy-start | bytes 11010052
  239.7 20.8 %collective-permute-start.11 = (bf16[256,7168]{1,0:T(8,128)(2,1)}, bf16[256,7168]{1,0:T(8,128)(2,1)S(1)}, u32[]{:S(2)}, u32[]{:S(2)}) collective-permute-start(bf16[256,7168]{1,0:T(8,128)(2,1)} %collective-permute-done.10.refs_1_), channel_id=1, source_target_pairs={{4,0},{5,1},{2,6},{3,7},{12,8},{13,9},{10,14},{11,15},{20,16},{21,... | collective-permute-start | bytes 11010056 | tf_op jit(solution)/shard_map/ppermute | solution.py:35
  242.7 40.0 %collective-permute-start.12 = (bf16[256,2688]{1,0:T(8,128)(2,1)}, bf16[256,2688]{1,0:T(8,128)(2,1)}, u32[]{:S(2)}, u32[]{:S(2)}) collective-permute-start(bf16[256,2688]{1,0:T(8,128)(2,1)} %get-tuple-element.46), channel_id=1, source_target_pairs={{0,1},{1,0},{6,7},{7,6},{4,3},{3,4},{5,2},{2,5},{8,9},{9,8},{14,15... | collective-permute-start | bytes 4128776 | tf_op jit(solution)/shard_map/ppermute | solution.py:35
  242.7 47.9 %collective-permute-start.14 = (bf16[256,2688]{1,0:T(8,128)(2,1)}, bf16[256,2688]{1,0:T(8,128)(2,1)}, u32[]{:S(2)}, u32[]{:S(2)}) collective-permute-start(bf16[256,2688]{1,0:T(8,128)(2,1)} %get-tuple-element.46), channel_id=1, source_target_pairs={{5,3},{3,5},{4,2},{2,4},{13,11},{11,13},{12,10},{10,12},{21,19},{1... | collective-permute-start | bytes 4128776 | tf_op jit(solution)/shard_map/ppermute | solution.py:35
  260.4 1.8 copy-start.12
  275.1 34.5 %all-to-all-start.3 = ((bf16[32,16,1792]{2,1,0:T(8,128)(2,1)}), bf16[32,16,1792]{2,1,0:T(8,128)(2,1)}, u32[]{:S(2)}, u32[]{:S(2)}) async-start(bf16[32,16,1792]{2,1,0:T(8,128)(2,1)} %get-tuple-element.44), calls=%async_computation.3 | async-start | bytes 3670016 | tf_op jit(solution)/shard_map/all_to_all | solution.py:215
  282.7 11.1 %collective-permute-start.13 = (bf16[256,2688]{1,0:T(8,128)(2,1)}, bf16[256,2688]{1,0:T(8,128)(2,1)S(1)}, u32[]{:S(2)}, u32[]{:S(2)}) collective-permute-start(bf16[256,2688]{1,0:T(8,128)(2,1)} %collective-permute-done.12.near), channel_id=1, source_target_pairs={{0,4},{4,0},{1,5},{5,1},{2,6},{6,2},{3,7},{7,3},{8,12},{12,8},{9,1... | collective-permute-start | bytes 4128776 | tf_op jit(solution)/shard_map/ppermute | solution.py:35
  290.6 5.2 %collective-permute-start.15 = (bf16[256,2688]{1,0:T(8,128)(2,1)}, bf16[256,2688]{1,0:T(8,128)(2,1)S(1)}, u32[]{:S(2)}, u32[]{:S(2)}) collective-permute-start(bf16[256,2688]{1,0:T(8,128)(2,1)} %collective-permute-done.14.far), channel_id=1, source_target_pairs={{4,0},{5,1},{2,6},{3,7},{12,8},{13,9},{10,14},{11,15},{20,16},{21,... | collective-permute-start | bytes 4128776 | tf_op jit(solution)/shard_map/ppermute | solution.py:35
  291.9 29.1 %collective-permute-start.16 = (bf16[256,2688]{1,0:T(8,128)(2,1)}, bf16[256,2688]{1,0:T(8,128)(2,1)S(1)}, u32[]{:S(2)}, u32[]{:S(2)}) collective-permute-start(bf16[256,2688]{1,0:T(8,128)(2,1)} %get-tuple-element.50), channel_id=1, source_target_pairs={{0,1},{1,0},{6,7},{7,6},{4,3},{3,4},{5,2},{2,5},{8,9},{9,8},{14,15... | collective-permute-start | bytes 4128776 | tf_op jit(solution)/shard_map/ppermute | solution.py:35
  292.0 35.5 %collective-permute-start.18 = (bf16[256,2688]{1,0:T(8,128)(2,1)}, bf16[256,2688]{1,0:T(8,128)(2,1)}, u32[]{:S(2)}, u32[]{:S(2)}) collective-permute-start(bf16[256,2688]{1,0:T(8,128)(2,1)} %get-tuple-element.50), channel_id=1, source_target_pairs={{5,3},{3,5},{4,2},{2,4},{13,11},{11,13},{12,10},{10,12},{21,19},{1... | collective-permute-start | bytes 4128776 | tf_op jit(solution)/shard_map/ppermute | solution.py:35
  295.9 2.0 copy-start.1
  304.4 1.6 copy-start.3
  306.0 0.8 copy-start.4
  309.6 42.3 %all-to-all-start.4 = ((bf16[32,16,2688]{2,1,0:T(8,128)(2,1)}), bf16[32,16,2688]{2,1,0:T(8,128)(2,1)}, u32[]{:S(2)}, u32[]{:S(2)}) async-start(bf16[32,16,2688]{2,1,0:T(8,128)(2,1)} %copy-done.3), calls=%async_computation.4 | async-start | bytes 5505024 | tf_op jit(solution)/shard_map/all_to_all | solution.py:215
  321.0 9.3 %collective-permute-start.17 = (bf16[256,2688]{1,0:T(8,128)(2,1)S(1)}, bf16[256,2688]{1,0:T(8,128)(2,1)S(1)}, u32[]{:S(2)}, u32[]{:S(2)}) collective-permute-start(bf16[256,2688]{1,0:T(8,128)(2,1)S(1)} %collective-permute-done.16.near), channel_id=1, source_target_pairs={{0,4},{4,0},{1,5},{5,1},{2,6},{6,2},{3,7},{7,3},{8,12},{12,8},{9,1... | collective-permute-start | bytes 4128776 | tf_op jit(solution)/shard_map/ppermute | solution.py:35
  327.5 5.2 %collective-permute-start.19 = (bf16[256,2688]{1,0:T(8,128)(2,1)}, bf16[256,2688]{1,0:T(8,128)(2,1)S(1)}, u32[]{:S(2)}, u32[]{:S(2)}) collective-permute-start(bf16[256,2688]{1,0:T(8,128)(2,1)} %collective-permute-done.18.far), channel_id=1, source_target_pairs={{4,0},{5,1},{2,6},{3,7},{12,8},{13,9},{10,14},{11,15},{20,16},{21,... | collective-permute-start | bytes 4128776 | tf_op jit(solution)/shard_map/ppermute | solution.py:35
  332.7 2.0 copy-start.2
  334.8 7.1 %copy-start.5 = (bf16[128,2688]{1,0:T(8,128)(2,1)S(1)}, bf16[128,2688]{1,0:T(8,128)(2,1)}, u32[]{:S(2)}) copy-start(bf16[128,2688]{1,0:T(8,128)(2,1)} %copy-done.4) | copy-start | bytes 2064388
  351.9 30.1 %all-to-all-start.5 = ((bf16[16,8,7168]{2,1,0:T(8,128)(2,1)}), bf16[16,8,7168]{2,1,0:T(8,128)(2,1)S(1)}, u32[]{:S(2)}, u32[]{:S(2)}) async-start(bf16[16,8,7168]{2,1,0:T(8,128)(2,1)} %bitcast.86), calls=%async_computation.5 | async-start | bytes 3670016 | tf_op jit(solution)/shard_map/all_to_all | solution.py:219
  382.0 1.3 copy-start.8
  383.2 41.6 %all-to-all-start.6 = ((bf16[32,16,2688]{2,1,0:T(8,128)(2,1)}), bf16[32,16,2688]{2,1,0:T(8,128)(2,1)S(1)}, u32[]{:S(2)}, u32[]{:S(2)}) async-start(bf16[32,16,2688]{2,1,0:T(8,128)(2,1)} %bitcast.35), calls=%async_computation.6 | async-start | bytes 5505024 | tf_op jit(solution)/shard_map/all_to_all | solution.py:215
  390.9 2.4 copy-start.6
  391.1 9.0 %collective-permute-start.20 = (bf16[64,1792]{1,0:T(8,128)(2,1)S(1)}, bf16[64,1792]{1,0:T(8,128)(2,1)S(1)}, u32[]{:S(2)}, u32[]{:S(2)}) collective-permute-start(bf16[64,1792]{1,0:T(8,128)(2,1)S(1)} %slice.193), channel_id=1, source_target_pairs={{0,3},{3,0},{1,2},{2,1},{4,7},{7,4},{5,6},{6,5},{8,11},{11,8},{9,1... | collective-permute-start | bytes 688136 | tf_op jit(solution)/shard_map/ppermute | solution.py:170
  395.2 4.9 %copy-start.10 = (f32[128,2688]{1,0:T(8,128)}, f32[128,2688]{1,0:T(8,128)S(1)}, u32[]{:S(2)}) copy-start(f32[128,2688]{1,0:T(8,128)S(1)} %slice_add_fusion.1) | copy-start | bytes 4128772
  396.0 33.9 %collective-permute-start.21 = (bf16[64,2688]{1,0:T(8,128)(2,1)}, bf16[64,2688]{1,0:T(8,128)(2,1)}, u32[]{:S(2)}, u32[]{:S(2)}) collective-permute-start(bf16[64,2688]{1,0:T(8,128)(2,1)} %slice.192), channel_id=1, source_target_pairs={{0,3},{3,0},{1,2},{2,1},{4,7},{7,4},{5,6},{6,5},{8,11},{11,8},{9,1... | collective-permute-start | bytes 1032200 | tf_op jit(solution)/shard_map/ppermute | solution.py:170
  427.4 2.5 copy-start.11
  427.6 9.0 %collective-permute-start.22 = (bf16[64,2688]{1,0:T(8,128)(2,1)S(1)}, bf16[64,2688]{1,0:T(8,128)(2,1)S(1)}, u32[]{:S(2)}, u32[]{:S(2)}) collective-permute-start(bf16[64,2688]{1,0:T(8,128)(2,1)S(1)} %slice.191), channel_id=1, source_target_pairs={{0,3},{3,0},{1,2},{2,1},{4,7},{7,4},{5,6},{6,5},{8,11},{11,8},{9,1... | collective-permute-start | bytes 1032200 | tf_op jit(solution)/shard_map/ppermute | solution.py:170

commit v5 on v4

--- a/solution.py
+++ b/solution.py
@@ -239,14 +239,14 @@
     rest = rows_of(
         jnp.concatenate([pick_rest, other_rest], axis=2), jnp.concatenate([tokens, other], axis=0)
     )
-    theirs = exchange_main(after(rows_of(pick, other), mine, nears[0]))
-    rest = exchange_rest(after(rest, theirs))
+    theirs = exchange_main(after(rows_of(pick, other), mine))
     fars = [along(owns[0], FAR), along(after(owns[1], nears[0], theirs), FAR)]
     copied = [along(own, FROM_HOME) for own in owns]
-    across = [
-        along(after(near, got), SIBLING) for near, got in zip(nears, (theirs, rest), strict=True)
-    ]
-    brought_0 = along(after(fars[0], rest), TO_HOME)
+    whole = down_weight[0], along(after(down_weight[0], *copied), FROM_HOME)
+    across_0 = along(after(nears[0], theirs), SIBLING)
+    brought_0 = along(after(fars[0], theirs), TO_HOME)
+    rest = exchange_rest(after(rest, theirs, across_0, brought_0, whole[1]))
+    across = [across_0, along(after(nears[1], rest), SIBLING)]
 
     def halves(*parts):
         part = jnp.concatenate([part.reshape(tok_rows, -1) for part in parts], axis=0)
@@ -260,7 +260,6 @@
         own = after(down_weight[0][:, at : at + step], *earlier)
         return along(own, NEXT), along(own, FAR)
 
-    whole = down_weight[0], along(after(down_weight[0], *copied), FROM_HOME)
     units = [*zip(owns, copied, strict=True), *zip(nears), *zip(across), (brought_0, fars[0])]
     first = hidden_units(flag, after(mine, whole[1]), theirs, rest, units)
     brought_1 = along(after(fars[1], first), TO_HOME)

time: 439 us -> 446 us (1.016)
  waiting for transfers between devices: 212 us -> 240 us
  starting transfers between devices: 109 us -> 94.2 us
  local copies, waits for them, and re-layouts: 21.9 us -> 16.8 us
    ppermute x19, waiting for transfers between devices: 35.6 us -> 152 us  [along(): return lax.ppermute(value, COL, pairs)]
    all_to_all x5, waiting for transfers between devices: 108 us -> 38.6 us  [exchange_main(): return lax.all_to_all(parts, EXP, 0, 0, tiled=True).reshape(rows.shape)]
    all_to_all x2, waiting for transfers between devices: 47.9 us -> 21.7 us  [exchange_rest(): lax.all_to_all(parts, ('y', 'x'), 0, 0, tiled=True).reshape(rows.shape)]
    ppermute x19, starting transfers between devices: 60.1 us -> 44.8 us  [along(): return lax.ppermute(value, COL, pairs)]
    ppermute x4, waiting for transfers between devices: 20.8 us -> 28.1 us  [pair_exchange(): return lax.ppermute(value, ('zh', 'zl'), PAIR)]
    unnamed x31 -> x33, local copies, waits for them, and re-layouts: 10.4 us -> 9.71 us
  transfers between devices with their start and end apart: 30 -> 30, of which waited for: 17 -> 18; matrix products, arithmetic and copies ran while one was open for 9% -> 9% of each run, Pallas kernels for 12% -> 12%
where the time goes in v5:
time: 446 us; the launch traced here: 444 us
  waiting for transfers between devices  240 us (54%)
  starting transfers between devices  94.2 us (21%)
  Pallas kernels  53.4 us (12%)
  matrix products  23.8 us (5%)
  local copies, waits for them, and re-layouts  16.8 us (4%)
  other arithmetic  15.4 us (3%)
    ppermute x19, waiting for transfers between devices, along(): return lax.ppermute(value, COL, pairs)  152 us
    ppermute x19, starting transfers between devices, along(): return lax.ppermute(value, COL, pairs)  44.8 us
    all_to_all x5, waiting for transfers between devices, exchange_main(): return lax.all_to_all(parts, EXP, 0, 0, tiled=True).reshape(rows.shape)  38.6 us
    pallas_call x2, Pallas kernels, hidden_units(): pl.pallas_call(functools.partial(hidden_kernel, kinds=kinds), grid_spec=p...  33.9 us
    all_to_all x5, starting transfers between devices, exchange_main(): return lax.all_to_all(parts, EXP, 0, 0, tiled=True).reshape(rows.shape)  28.8 us
    ppermute x4, waiting for transfers between devices, pair_exchange(): return lax.ppermute(value, ('zh', 'zl'), PAIR)  28.1 us
    all_to_all x2, waiting for transfers between devices, exchange_rest(): lax.all_to_all(parts, ('y', 'x'), 0, 0, tiled=True).reshape(rows.shape)  21.7 us
    pallas_call x3, Pallas kernels, down_rows(): pl.pallas_call(down_kernel, grid_spec=pltpu.PrefetchScalarGridSpec(num_sc...  19.5 us
  transfers between devices with their start and end apart: 30, of which 18 were waited for; matrix products, arithmetic and copies ran while one was open for 9% of the time, Pallas kernels for 12%

profile of v5, /device:TPU:0, one launch (start us, length us, event | category | flops | bytes accessed | tf_op | source)
XLA Modules:
  0.0 444.0 jit_solution(14237006572892215897)
XLA Ops:
  1.8 4.1 convolution_convert_fusion.1
  6.0 7.7 %all-to-all-start = ((bf16[32,8,7168]{2,1,0:T(8,128)(2,1)}), bf16[32,8,7168]{2,1,0:T(8,128)(2,1)}, u32[]{:S(2)}, u32[]{:S(2)}) async-start(bf16[32,8,7168]{2,1,0:T(8,128)(2,1)} %bitcast.80), calls=%async_computation | async-start | bytes 7340032 | tf_op jit(solution)/shard_map/all_to_all | solution.py:215
  13.8 4.1 collective-permute-start
  19.5 19.6 %collective-permute-done = bf16[64,7296]{1,0:T(8,128)(2,1)S(1)} collective-permute-done((bf16[64,7296]{1,0:T(8,128)(2,1)S(1)}, bf16[64,7296]{1,0:T(8,128)(2,1)S(1)}, u32[]{:S(2)}, u32[]{:S(2)}) %collective-permute-start) | collective-permute-done | bytes 933920 | tf_op jit(solution)/shard_map/ppermute | solution.py:170
  41.6 5.4 %pad_maximum_fusion.refs_0_.own = bf16[256,8960]{1,0:T(8,128)(2,1)} fusion(bf16[256,1792]{1,0:T(8,128)(2,1)S(1)} %slice.142, bf16[128,7168]{1,0:T(8,128)(2,1)S(1)} %get-tuple-element.68, bf16[128,7168]{1,0:T(8,128)(2,1)S(1)} %get-tuple-element.66), kind=kLoop, calls=%fused_computation.3 | loop fusion | flops 13762560 | bytes 9175040 | tf_op jit(solution)/shard_map/concatenate | solution.py:235
  47.0 3.9 collective-permute-start.1
  50.9 2.8 collective-permute-start.6
  54.2 4.1 convolution_convert_fusion
  58.3 2.9 all-to-all-done
  61.3 4.8 %all-to-all-start.1 = ((bf16[32,8,7168]{2,1,0:T(8,128)(2,1)}), bf16[32,8,7168]{2,1,0:T(8,128)(2,1)}, u32[]{:S(2)}, u32[]{:S(2)}) async-start(bf16[32,8,7168]{2,1,0:T(8,128)(2,1)} %bitcast.81), calls=%async_computation.1 | async-start | bytes 7340032 | tf_op jit(solution)/shard_map/all_to_all | solution.py:215
  66.1 3.6 pad_maximum_fusion.1.refs_2_
  69.7 3.8 collective-permute-start.2
  73.5 79.0 %collective-permute-done.4.refs_4_.near = bf16[256,8960]{1,0:T(8,128)(2,1)} collective-permute-done((bf16[256,8960]{1,0:T(8,128)(2,1)}, bf16[256,8960]{1,0:T(8,128)(2,1)}, u32[]{:S(2)}, u32[]{:S(2)}) %collective-permute-start.4) | collective-permute-done | bytes 4587552 | tf_op jit(solution)/shard_map/ppermute | solution.py:35
  153.8 8.4 %collective-permute-start.3 = (bf16[256,7168]{1,0:T(8,128)(2,1)}, bf16[256,7168]{1,0:T(8,128)(2,1)}, u32[]{:S(2)}, u32[]{:S(2)}) collective-permute-start(bf16[256,7168]{1,0:T(8,128)(2,1)} %bitcast.74), channel_id=1, source_target_pairs={{0,4},{1,5},{6,2},{7,3},{8,12},{9,13},{14,10},{15,11},{16,20},{17,... | collective-permute-start | bytes 11010056 | tf_op jit(solution)/shard_map/ppermute | solution.py:35
  162.5 3.1 convolution_convert_fusion.2
  167.1 6.8 %all-to-all-start.2 = ((bf16[16,8,7168]{2,1,0:T(8,128)(2,1)}), bf16[16,8,7168]{2,1,0:T(8,128)(2,1)S(1)}, u32[]{:S(2)}, u32[]{:S(2)}) async-start(bf16[16,8,7168]{2,1,0:T(8,128)(2,1)} %bitcast.87), calls=%async_computation.2 | async-start | bytes 3670016 | tf_op jit(solution)/shard_map/all_to_all | solution.py:219
  173.9 31.5 %collective-permute-done.8.refs_5_ = bf16[256,7168]{1,0:T(8,128)(2,1)} collective-permute-done((bf16[256,7168]{1,0:T(8,128)(2,1)}, bf16[256,7168]{1,0:T(8,128)(2,1)}, u32[]{:S(2)}, u32[]{:S(2)}) %collective-permute-start.8) | collective-permute-done | bytes 3670048 | tf_op jit(solution)/shard_map/ppermute | solution.py:35
  205.5 2.5 collective-permute-start.10
  208.0 4.2 collective-permute-done.9.refs_7_
  212.2 26.9 %shard_map.64.first = bf16[640,896]{1,0:T(8,128)(2,1)S(1)} custom-call(s32[1]{0:T(128)} %bitcast.4.flag, bf16[256,7168]{1,0:T(8,128)(2,1)} %bitcast.6.mine, bf16[256,7168]{1,0:T(8,128)(2,1)} %bitcast.14.theirs, bf16[128,7168]{1,0:T(8,128)(2,1)S(1)} %bitcast.78, bf16[256,8960]{1,0:T(8,128)(2,1)} %pad_maximum_fusion.refs_0_.own, ...), custom_call_target="tpu_custom_call" | custom-call | flops 1 | bytes 1 | tf_op jit(solution)/shard_map/pallas_call | solution.py:95
  242.2 1.8 collective-permute-start.14
  244.0 22.8 %collective-permute-done.11.refs_0_ = bf16[256,7168]{1,0:T(8,128)(2,1)S(1)} collective-permute-done((bf16[256,7168]{1,0:T(8,128)(2,1)}, bf16[256,7168]{1,0:T(8,128)(2,1)S(1)}, u32[]{:S(2)}, u32[]{:S(2)}) %collective-permute-start.11) | collective-permute-done | bytes 3670048 | tf_op jit(solution)/shard_map/ppermute | solution.py:35
  266.8 1.8 copy-done.12
  268.6 7.0 %shard_map.65.last = bf16[640,128]{1,0:T(8,128)(2,1)S(1)} custom-call(s32[1]{0:T(128)} %bitcast.4.flag, bf16[256,7168]{1,0:T(8,128)(2,1)} %bitcast.6.mine, bf16[256,7168]{1,0:T(8,128)(2,1)} %bitcast.14.theirs, bf16[128,7168]{1,0:T(8,128)(2,1)S(1)} %bitcast.79, bf16[256,7168]{1,0:T(8,128)(2,1)} %copy-done.12, bf16[256,7168]{1,0:T(8,128)(2,1)} %collective-permute-done.10.refs_1_), custom_call_target="tpu_custom_call" | custom-call | flops 1 | bytes 1 | tf_op jit(solution)/shard_map/pallas_call | solution.py:95
  275.6 5.9 %shard_map.66 = (bf16[32,16,1792]{2,1,0:T(8,128)(2,1)}, bf16[128,1792]{1,0:T(8,128)(2,1)S(1)}) custom-call(s32[1]{0:T(128)} %bitcast.4.flag, bf16[640,896]{1,0:T(8,128)(2,1)S(1)} %shard_map.64.first, bf16[640,128]{1,0:T(8,128)(2,1)S(1)} %shard_map.65.last, bf16[256,8960]{1,0:T(8,128)(2,1)} %pad_maximum_fusion.refs_0_.own, ...), custom_call_target="tpu_custom_call" | custom-call | flops 2348810240 | bytes 7274496 | tf_op jit(solution)/shard_map/pallas_call | solution.py:140
  281.5 7.4 %all-to-all-start.3 = ((bf16[32,16,1792]{2,1,0:T(8,128)(2,1)}), bf16[32,16,1792]{2,1,0:T(8,128)(2,1)}, u32[]{:S(2)}, u32[]{:S(2)}) async-start(bf16[32,16,1792]{2,1,0:T(8,128)(2,1)} %get-tuple-element.44), calls=%async_computation.3 | async-start | bytes 3670016 | tf_op jit(solution)/shard_map/all_to_all | solution.py:215
  288.9 8.1 %collective-permute-start.13 = (bf16[256,2688]{1,0:T(8,128)(2,1)}, bf16[256,2688]{1,0:T(8,128)(2,1)S(1)}, u32[]{:S(2)}, u32[]{:S(2)}) collective-permute-start(bf16[256,2688]{1,0:T(8,128)(2,1)} %collective-permute-done.12.near), channel_id=1, source_target_pairs={{0,4},{4,0},{1,5},{5,1},{2,6},{6,2},{3,7},{7,3},{8,12},{12,8},{9,1... | collective-permute-start | bytes 4128776 | tf_op jit(solution)/shard_map/ppermute | solution.py:35
  300.1 2.1 collective-permute-done.15.brought
  302.2 2.0 copy-done.1
  304.3 6.5 %shard_map.67 = (bf16[32,16,2688]{2,1,0:T(8,128)(2,1)S(1)}, bf16[128,2688]{1,0:T(8,128)(2,1)S(1)}) custom-call(s32[1]{0:T(128)} %bitcast.4.flag, bf16[640,896]{1,0:T(8,128)(2,1)S(1)} %shard_map.64.first, bf16[640,128]{1,0:T(8,128)(2,1)S(1)} %shard_map.65.last, bf16[256,7168]{1,0:T(8,128)(2,1)S(1)} %bitcast.76, ...), custom_call_target="tpu_custom_call" | custom-call | flops 3523215360 | bytes 10256384 | tf_op jit(solution)/shard_map/pallas_call | solution.py:140
  313.2 2.7 all-to-all-done.3
  315.8 4.8 %all-to-all-start.4 = ((bf16[32,16,2688]{2,1,0:T(8,128)(2,1)}), bf16[32,16,2688]{2,1,0:T(8,128)(2,1)}, u32[]{:S(2)}, u32[]{:S(2)}) async-start(bf16[32,16,2688]{2,1,0:T(8,128)(2,1)} %copy-done.3), calls=%async_computation.4 | async-start | bytes 5505024 | tf_op jit(solution)/shard_map/all_to_all | solution.py:215
  320.7 6.7 %collective-permute-done.16.near = bf16[256,2688]{1,0:T(8,128)(2,1)S(1)} collective-permute-done((bf16[256,2688]{1,0:T(8,128)(2,1)}, bf16[256,2688]{1,0:T(8,128)(2,1)S(1)}, u32[]{:S(2)}, u32[]{:S(2)}) %collective-permute-start.16) | collective-permute-done | bytes 1376288 | tf_op jit(solution)/shard_map/ppermute | solution.py:35
  327.4 6.5 %collective-permute-start.17 = (bf16[256,2688]{1,0:T(8,128)(2,1)S(1)}, bf16[256,2688]{1,0:T(8,128)(2,1)S(1)}, u32[]{:S(2)}, u32[]{:S(2)}) collective-permute-start(bf16[256,2688]{1,0:T(8,128)(2,1)S(1)} %collective-permute-done.16.near), channel_id=1, source_target_pairs={{0,4},{4,0},{1,5},{5,1},{2,6},{6,2},{3,7},{7,3},{8,12},{12,8},{9,1... | collective-permute-start | bytes 4128776 | tf_op jit(solution)/shard_map/ppermute | solution.py:35
  336.6 2.5 collective-permute-done.19.brought
  339.1 2.0 copy-done.2
  341.2 7.1 %shard_map.68 = (bf16[32,16,2688]{2,1,0:T(8,128)(2,1)}, bf16[128,2688]{1,0:T(8,128)(2,1)S(1)}) custom-call(s32[1]{0:T(128)} %bitcast.4.flag, bf16[640,896]{1,0:T(8,128)(2,1)S(1)} %shard_map.64.first, bf16[640,128]{1,0:T(8,128)(2,1)S(1)} %shard_map.65.last, bf16[256,7168]{1,0:T(8,128)(2,1)S(1)} %bitcast.77, bf16[256,7168]{1,0:T(8,128)(2,1)} %collective-permute-done.3.copied, ...), custom_call_target="tpu_custom_call" | custom-call | flops 3523215360 | bytes 10256384 | tf_op jit(solution)/shard_map/pallas_call | solution.py:140
  349.7 8.4 %all-to-all-done.4 = bf16[32,16,2688]{2,1,0:T(8,128)(2,1)} async-done(((bf16[32,16,2688]{2,1,0:T(8,128)(2,1)}), bf16[32,16,2688]{2,1,0:T(8,128)(2,1)}, u32[]{:S(2)}, u32[]{:S(2)}) %all-to-all-start.4) | async-done | bytes 2752544 | tf_op jit(solution)/shard_map/all_to_all | solution.py:215
  358.1 3.7 all-to-all-start.5
  362.4 4.3 fusion.16
  366.7 21.7 %all-to-all-done.5 = bf16[16,8,7168]{2,1,0:T(8,128)(2,1)S(1)} async-done(((bf16[16,8,7168]{2,1,0:T(8,128)(2,1)}), bf16[16,8,7168]{2,1,0:T(8,128)(2,1)S(1)}, u32[]{:S(2)}, u32[]{:S(2)}) %all-to-all-start.5) | async-done | bytes 1835040 | tf_op jit(solution)/shard_map/all_to_all | solution.py:219
  389.6 4.1 all-to-all-start.6
  395.1 2.2 convolution_add_fusion.2
  397.4 2.2 collective-permute-start.20
  403.8 2.7 collective-permute-done.20
  406.6 24.5 %all-to-all-done.6 = bf16[32,16,2688]{2,1,0:T(8,128)(2,1)S(1)} async-done(((bf16[32,16,2688]{2,1,0:T(8,128)(2,1)}), bf16[32,16,2688]{2,1,0:T(8,128)(2,1)S(1)}, u32[]{:S(2)}, u32[]{:S(2)}) %all-to-all-start.6) | async-done | bytes 2752544 | tf_op jit(solution)/shard_map/all_to_all | solution.py:215
  434.0 2.2 collective-permute-start.22
  437.2 5.8 %collective-permute-done.22 = bf16[64,2688]{1,0:T(8,128)(2,1)S(1)} collective-permute-done((bf16[64,2688]{1,0:T(8,128)(2,1)S(1)}, bf16[64,2688]{1,0:T(8,128)(2,1)S(1)}, u32[]{:S(2)}, u32[]{:S(2)}) %collective-permute-start.22) | collective-permute-done | bytes 344096 | tf_op jit(solution)/shard_map/ppermute | solution.py:170
  (109 shorter events, 34.8 us)
Async XLA Ops:
  6.0 7.7 %copy-start.15 = (f32[64,8]{0,1:T(8,128)S(1)}, f32[64,8]{0,1:T(8,128)}, u32[]{:S(2)}) copy-start(f32[64,8]{0,1:T(8,128)} %param.8) | copy-start | bytes 6148
  6.0 7.8 %copy-start.7 = (bf16[64,7168]{1,0:T(8,128)(2,1)S(1)}, bf16[64,7168]{1,0:T(8,128)(2,1)}, u32[]{:S(2)}) copy-start(bf16[64,7168]{1,0:T(8,128)(2,1)} %param.6) | copy-start | bytes 2752516
  6.0 55.3 %all-to-all-start = ((bf16[32,8,7168]{2,1,0:T(8,128)(2,1)}), bf16[32,8,7168]{2,1,0:T(8,128)(2,1)}, u32[]{:S(2)}, u32[]{:S(2)}) async-start(bf16[32,8,7168]{2,1,0:T(8,128)(2,1)} %bitcast.80), calls=%async_computation | async-start | bytes 7340032 | tf_op jit(solution)/shard_map/all_to_all | solution.py:215
  13.8 5.4 %copy-start.13 = (bf16[1,256,7168]{2,1,0:T(8,128)(2,1)S(1)}, bf16[1,256,7168]{2,1,0:T(8,128)(2,1)}, u32[]{:S(2)}) copy-start(bf16[1,256,7168]{2,1,0:T(8,128)(2,1)} %param.10) | copy-start | bytes 11010052
  13.8 25.2 %collective-permute-start = (bf16[64,7296]{1,0:T(8,128)(2,1)S(1)}, bf16[64,7296]{1,0:T(8,128)(2,1)S(1)}, u32[]{:S(2)}, u32[]{:S(2)}) collective-permute-start(bf16[64,7296]{1,0:T(8,128)(2,1)S(1)} %fusion.6), channel_id=1, source_target_pairs={{0,3},{3,0},{1,2},{2,1},{4,7},{7,4},{5,6},{6,5},{8,11},{11,8},{9,1... | collective-permute-start | bytes 2801672 | tf_op jit(solution)/shard_map/ppermute | solution.py:170
  19.2 20.9 %copy-start.14 = (bf16[1,256,7168]{2,1,0:T(8,128)(2,1)S(1)}, bf16[1,256,7168]{2,1,0:T(8,128)(2,1)}, u32[]{:S(2)}) copy-start(bf16[1,256,7168]{2,1,0:T(8,128)(2,1)} %param.9) | copy-start | bytes 11010052
  39.0 14.6 %copy-start.11 = (bf16[64,7296]{1,0:T(8,128)(2,1)}, bf16[64,7296]{1,0:T(8,128)(2,1)S(1)}, u32[]{:S(2)}) copy-start(bf16[64,7296]{1,0:T(8,128)(2,1)S(1)} %collective-permute-done) | copy-start | bytes 2801668
  47.0 106.8 %collective-permute-start.1 = (bf16[256,8960]{1,0:T(8,128)(2,1)}, bf16[256,8960]{1,0:T(8,128)(2,1)}, u32[]{:S(2)}, u32[]{:S(2)}) collective-permute-start(bf16[256,8960]{1,0:T(8,128)(2,1)} %pad_maximum_fusion.refs_0_.own), channel_id=1, source_target_pairs={{0,4},{1,5},{6,2},{7,3},{8,12},{9,13},{14,10},{15,11},{16,20},{17,... | collective-permute-start | bytes 13762568 | tf_op jit(solution)/shard_map/ppermute | solution.py:35
  50.9 101.6 %collective-permute-start.4 = (bf16[256,8960]{1,0:T(8,128)(2,1)}, bf16[256,8960]{1,0:T(8,128)(2,1)}, u32[]{:S(2)}, u32[]{:S(2)}) collective-permute-start(bf16[256,8960]{1,0:T(8,128)(2,1)} %pad_maximum_fusion.refs_0_.own), channel_id=1, source_target_pairs={{0,1},{1,0},{6,7},{7,6},{4,3},{3,4},{5,2},{2,5},{8,9},{9,8},{14,15... | collective-permute-start | bytes 13762568 | tf_op jit(solution)/shard_map/ppermute | solution.py:35
  50.9 101.6 %collective-permute-start.6 = (bf16[256,8960]{1,0:T(8,128)(2,1)}, bf16[256,8960]{1,0:T(8,128)(2,1)}, u32[]{:S(2)}, u32[]{:S(2)}) collective-permute-start(bf16[256,8960]{1,0:T(8,128)(2,1)} %pad_maximum_fusion.refs_0_.own), channel_id=1, source_target_pairs={{5,3},{3,5},{4,2},{2,4},{13,11},{11,13},{12,10},{10,12},{21,19},{1... | collective-permute-start | bytes 13762568 | tf_op jit(solution)/shard_map/ppermute | solution.py:35
  61.3 91.2 %all-to-all-start.1 = ((bf16[32,8,7168]{2,1,0:T(8,128)(2,1)}), bf16[32,8,7168]{2,1,0:T(8,128)(2,1)}, u32[]{:S(2)}, u32[]{:S(2)}) async-start(bf16[32,8,7168]{2,1,0:T(8,128)(2,1)} %bitcast.81), calls=%async_computation.1 | async-start | bytes 7340032 | tf_op jit(solution)/shard_map/all_to_all | solution.py:215
  69.7 84.1 %collective-permute-start.2 = (bf16[256,7168]{1,0:T(8,128)(2,1)}, bf16[256,7168]{1,0:T(8,128)(2,1)}, u32[]{:S(2)}, u32[]{:S(2)}) collective-permute-start(bf16[256,7168]{1,0:T(8,128)(2,1)} %pad_maximum_fusion.1.refs_2_), channel_id=1, source_target_pairs={{0,4},{1,5},{6,2},{7,3},{8,12},{9,13},{14,10},{15,11},{16,20},{17,... | collective-permute-start | bytes 11010056 | tf_op jit(solution)/shard_map/ppermute | solution.py:35
  152.5 14.3 %collective-permute-start.5 = (bf16[256,8960]{1,0:T(8,128)(2,1)}, bf16[256,8960]{1,0:T(8,128)(2,1)}, u32[]{:S(2)}, u32[]{:S(2)}) collective-permute-start(bf16[256,8960]{1,0:T(8,128)(2,1)} %collective-permute-done.4.refs_4_.near), channel_id=1, source_target_pairs={{0,4},{4,0},{1,5},{5,1},{2,6},{6,2},{3,7},{7,3},{8,12},{12,8},{9,1... | collective-permute-start | bytes 13762568 | tf_op jit(solution)/shard_map/ppermute | solution.py:35
  152.5 14.6 %collective-permute-start.7 = (bf16[256,8960]{1,0:T(8,128)(2,1)}, bf16[256,8960]{1,0:T(8,128)(2,1)}, u32[]{:S(2)}, u32[]{:S(2)}) collective-permute-start(bf16[256,8960]{1,0:T(8,128)(2,1)} %collective-permute-done.6.refs_9_.far), channel_id=1, source_target_pairs={{4,0},{5,1},{2,6},{3,7},{12,8},{13,9},{10,14},{11,15},{20,16},{21,... | collective-permute-start | bytes 13762568 | tf_op jit(solution)/shard_map/ppermute | solution.py:35
  153.8 12.9 %collective-permute-start.3 = (bf16[256,7168]{1,0:T(8,128)(2,1)}, bf16[256,7168]{1,0:T(8,128)(2,1)}, u32[]{:S(2)}, u32[]{:S(2)}) collective-permute-start(bf16[256,7168]{1,0:T(8,128)(2,1)} %bitcast.74), channel_id=1, source_target_pairs={{0,4},{1,5},{6,2},{7,3},{8,12},{9,13},{14,10},{15,11},{16,20},{17,... | collective-permute-start | bytes 11010056 | tf_op jit(solution)/shard_map/ppermute | solution.py:35
  162.3 43.2 %collective-permute-start.8 = (bf16[256,7168]{1,0:T(8,128)(2,1)}, bf16[256,7168]{1,0:T(8,128)(2,1)}, u32[]{:S(2)}, u32[]{:S(2)}) collective-permute-start(bf16[256,7168]{1,0:T(8,128)(2,1)} %pad_maximum_fusion.1.refs_2_), channel_id=1, source_target_pairs={{0,1},{1,0},{6,7},{7,6},{4,3},{3,4},{5,2},{2,5},{8,9},{9,8},{14,15... | collective-permute-start | bytes 11010056 | tf_op jit(solution)/shard_map/ppermute | solution.py:35
  167.1 38.4 %all-to-all-start.2 = ((bf16[16,8,7168]{2,1,0:T(8,128)(2,1)}), bf16[16,8,7168]{2,1,0:T(8,128)(2,1)S(1)}, u32[]{:S(2)}, u32[]{:S(2)}) async-start(bf16[16,8,7168]{2,1,0:T(8,128)(2,1)} %bitcast.87), calls=%async_computation.2 | async-start | bytes 3670016 | tf_op jit(solution)/shard_map/all_to_all | solution.py:219
  205.5 6.8 %collective-permute-start.9 = (bf16[256,7168]{1,0:T(8,128)(2,1)}, bf16[256,7168]{1,0:T(8,128)(2,1)}, u32[]{:S(2)}, u32[]{:S(2)}) collective-permute-start(bf16[256,7168]{1,0:T(8,128)(2,1)} %collective-permute-done.8.refs_5_), channel_id=1, source_target_pairs={{0,4},{4,0},{1,5},{5,1},{2,6},{6,2},{3,7},{7,3},{8,12},{12,8},{9,1... | collective-permute-start | bytes 11010056 | tf_op jit(solution)/shard_map/ppermute | solution.py:35
  205.5 33.7 %collective-permute-start.10 = (bf16[256,7168]{1,0:T(8,128)(2,1)}, bf16[256,7168]{1,0:T(8,128)(2,1)}, u32[]{:S(2)}, u32[]{:S(2)}) collective-permute-start(bf16[256,7168]{1,0:T(8,128)(2,1)} %pad_maximum_fusion.1.refs_2_), channel_id=1, source_target_pairs={{5,3},{3,5},{4,2},{2,4},{13,11},{11,13},{12,10},{10,12},{21,19},{1... | collective-permute-start | bytes 11010056 | tf_op jit(solution)/shard_map/ppermute | solution.py:35
  212.2 28.3 %copy-start = (bf16[1,256,7168]{2,1,0:T(8,128)(2,1)S(1)}, bf16[1,256,7168]{2,1,0:T(8,128)(2,1)}, u32[]{:S(2)}) copy-start(bf16[1,256,7168]{2,1,0:T(8,128)(2,1)} %param.11) | copy-start | bytes 11010052
  239.2 27.6 %collective-permute-start.11 = (bf16[256,7168]{1,0:T(8,128)(2,1)}, bf16[256,7168]{1,0:T(8,128)(2,1)S(1)}, u32[]{:S(2)}, u32[]{:S(2)}) collective-permute-start(bf16[256,7168]{1,0:T(8,128)(2,1)} %collective-permute-done.10.refs_1_), channel_id=1, source_target_pairs={{4,0},{5,1},{2,6},{3,7},{12,8},{13,9},{10,14},{11,15},{20,16},{21,... | collective-permute-start | bytes 11010056 | tf_op jit(solution)/shard_map/ppermute | solution.py:35
  242.2 46.7 %collective-permute-start.12 = (bf16[256,2688]{1,0:T(8,128)(2,1)}, bf16[256,2688]{1,0:T(8,128)(2,1)}, u32[]{:S(2)}, u32[]{:S(2)}) collective-permute-start(bf16[256,2688]{1,0:T(8,128)(2,1)} %get-tuple-element.46), channel_id=1, source_target_pairs={{0,1},{1,0},{6,7},{7,6},{4,3},{3,4},{5,2},{2,5},{8,9},{9,8},{14,15... | collective-permute-start | bytes 4128776 | tf_op jit(solution)/shard_map/ppermute | solution.py:35
  242.2 54.8 %collective-permute-start.14 = (bf16[256,2688]{1,0:T(8,128)(2,1)}, bf16[256,2688]{1,0:T(8,128)(2,1)}, u32[]{:S(2)}, u32[]{:S(2)}) collective-permute-start(bf16[256,2688]{1,0:T(8,128)(2,1)} %get-tuple-element.46), channel_id=1, source_target_pairs={{5,3},{3,5},{4,2},{2,4},{13,11},{11,13},{12,10},{10,12},{21,19},{1... | collective-permute-start | bytes 4128776 | tf_op jit(solution)/shard_map/ppermute | solution.py:35
  266.8 1.8 copy-start.12
  281.5 34.4 %all-to-all-start.3 = ((bf16[32,16,1792]{2,1,0:T(8,128)(2,1)}), bf16[32,16,1792]{2,1,0:T(8,128)(2,1)}, u32[]{:S(2)}, u32[]{:S(2)}) async-start(bf16[32,16,1792]{2,1,0:T(8,128)(2,1)} %get-tuple-element.44), calls=%async_computation.3 | async-start | bytes 3670016 | tf_op jit(solution)/shard_map/all_to_all | solution.py:215
  288.9 11.2 %collective-permute-start.13 = (bf16[256,2688]{1,0:T(8,128)(2,1)}, bf16[256,2688]{1,0:T(8,128)(2,1)S(1)}, u32[]{:S(2)}, u32[]{:S(2)}) collective-permute-start(bf16[256,2688]{1,0:T(8,128)(2,1)} %collective-permute-done.12.near), channel_id=1, source_target_pairs={{0,4},{4,0},{1,5},{5,1},{2,6},{6,2},{3,7},{7,3},{8,12},{12,8},{9,1... | collective-permute-start | bytes 4128776 | tf_op jit(solution)/shard_map/ppermute | solution.py:35
  297.0 5.2 %collective-permute-start.15 = (bf16[256,2688]{1,0:T(8,128)(2,1)}, bf16[256,2688]{1,0:T(8,128)(2,1)S(1)}, u32[]{:S(2)}, u32[]{:S(2)}) collective-permute-start(bf16[256,2688]{1,0:T(8,128)(2,1)} %collective-permute-done.14.far), channel_id=1, source_target_pairs={{4,0},{5,1},{2,6},{3,7},{12,8},{13,9},{10,14},{11,15},{20,16},{21,... | collective-permute-start | bytes 4128776 | tf_op jit(solution)/shard_map/ppermute | solution.py:35
  298.3 29.1 %collective-permute-start.16 = (bf16[256,2688]{1,0:T(8,128)(2,1)}, bf16[256,2688]{1,0:T(8,128)(2,1)S(1)}, u32[]{:S(2)}, u32[]{:S(2)}) collective-permute-start(bf16[256,2688]{1,0:T(8,128)(2,1)} %get-tuple-element.50), channel_id=1, source_target_pairs={{0,1},{1,0},{6,7},{7,6},{4,3},{3,4},{5,2},{2,5},{8,9},{9,8},{14,15... | collective-permute-start | bytes 4128776 | tf_op jit(solution)/shard_map/ppermute | solution.py:35
  298.4 35.5 %collective-permute-start.18 = (bf16[256,2688]{1,0:T(8,128)(2,1)}, bf16[256,2688]{1,0:T(8,128)(2,1)}, u32[]{:S(2)}, u32[]{:S(2)}) collective-permute-start(bf16[256,2688]{1,0:T(8,128)(2,1)} %get-tuple-element.50), channel_id=1, source_target_pairs={{5,3},{3,5},{4,2},{2,4},{13,11},{11,13},{12,10},{10,12},{21,19},{1... | collective-permute-start | bytes 4128776 | tf_op jit(solution)/shard_map/ppermute | solution.py:35
  302.2 2.0 copy-start.1
  310.7 1.6 copy-start.3
  312.3 0.8 copy-start.4
  315.8 42.3 %all-to-all-start.4 = ((bf16[32,16,2688]{2,1,0:T(8,128)(2,1)}), bf16[32,16,2688]{2,1,0:T(8,128)(2,1)}, u32[]{:S(2)}, u32[]{:S(2)}) async-start(bf16[32,16,2688]{2,1,0:T(8,128)(2,1)} %copy-done.3), calls=%async_computation.4 | async-start | bytes 5505024 | tf_op jit(solution)/shard_map/all_to_all | solution.py:215
  327.4 9.3 %collective-permute-start.17 = (bf16[256,2688]{1,0:T(8,128)(2,1)S(1)}, bf16[256,2688]{1,0:T(8,128)(2,1)S(1)}, u32[]{:S(2)}, u32[]{:S(2)}) collective-permute-start(bf16[256,2688]{1,0:T(8,128)(2,1)S(1)} %collective-permute-done.16.near), channel_id=1, source_target_pairs={{0,4},{4,0},{1,5},{5,1},{2,6},{6,2},{3,7},{7,3},{8,12},{12,8},{9,1... | collective-permute-start | bytes 4128776 | tf_op jit(solution)/shard_map/ppermute | solution.py:35
  333.9 5.2 %collective-permute-start.19 = (bf16[256,2688]{1,0:T(8,128)(2,1)}, bf16[256,2688]{1,0:T(8,128)(2,1)S(1)}, u32[]{:S(2)}, u32[]{:S(2)}) collective-permute-start(bf16[256,2688]{1,0:T(8,128)(2,1)} %collective-permute-done.18.far), channel_id=1, source_target_pairs={{4,0},{5,1},{2,6},{3,7},{12,8},{13,9},{10,14},{11,15},{20,16},{21,... | collective-permute-start | bytes 4128776 | tf_op jit(solution)/shard_map/ppermute | solution.py:35
  339.1 2.0 copy-start.2
  341.1 7.1 %copy-start.5 = (bf16[128,2688]{1,0:T(8,128)(2,1)S(1)}, bf16[128,2688]{1,0:T(8,128)(2,1)}, u32[]{:S(2)}) copy-start(bf16[128,2688]{1,0:T(8,128)(2,1)} %copy-done.4) | copy-start | bytes 2064388
  358.1 30.2 %all-to-all-start.5 = ((bf16[16,8,7168]{2,1,0:T(8,128)(2,1)}), bf16[16,8,7168]{2,1,0:T(8,128)(2,1)S(1)}, u32[]{:S(2)}, u32[]{:S(2)}) async-start(bf16[16,8,7168]{2,1,0:T(8,128)(2,1)} %bitcast.86), calls=%async_computation.5 | async-start | bytes 3670016 | tf_op jit(solution)/shard_map/all_to_all | solution.py:219
  388.3 1.2 copy-start.8
  389.6 41.6 %all-to-all-start.6 = ((bf16[32,16,2688]{2,1,0:T(8,128)(2,1)}), bf16[32,16,2688]{2,1,0:T(8,128)(2,1)S(1)}, u32[]{:S(2)}, u32[]{:S(2)}) async-start(bf16[32,16,2688]{2,1,0:T(8,128)(2,1)} %bitcast.35), calls=%async_computation.6 | async-start | bytes 5505024 | tf_op jit(solution)/shard_map/all_to_all | solution.py:215
  397.3 2.3 copy-start.6
  397.4 9.1 %collective-permute-start.20 = (bf16[64,1792]{1,0:T(8,128)(2,1)S(1)}, bf16[64,1792]{1,0:T(8,128)(2,1)S(1)}, u32[]{:S(2)}, u32[]{:S(2)}) collective-permute-start(bf16[64,1792]{1,0:T(8,128)(2,1)S(1)} %slice.193), channel_id=1, source_target_pairs={{0,3},{3,0},{1,2},{2,1},{4,7},{7,4},{5,6},{6,5},{8,11},{11,8},{9,1... | collective-permute-start | bytes 688136 | tf_op jit(solution)/shard_map/ppermute | solution.py:170
  401.4 5.1 %copy-start.9 = (f32[128,2688]{1,0:T(8,128)}, f32[128,2688]{1,0:T(8,128)S(1)}, u32[]{:S(2)}) copy-start(f32[128,2688]{1,0:T(8,128)S(1)} %slice_add_fusion.1) | copy-start | bytes 4128772
  402.3 33.9 %collective-permute-start.21 = (bf16[64,2688]{1,0:T(8,128)(2,1)}, bf16[64,2688]{1,0:T(8,128)(2,1)}, u32[]{:S(2)}, u32[]{:S(2)}) collective-permute-start(bf16[64,2688]{1,0:T(8,128)(2,1)} %slice.192), channel_id=1, source_target_pairs={{0,3},{3,0},{1,2},{2,1},{4,7},{7,4},{5,6},{6,5},{8,11},{11,8},{9,1... | collective-permute-start | bytes 1032200 | tf_op jit(solution)/shard_map/ppermute | solution.py:170
  433.8 2.4 copy-start.10
  434.0 9.0 %collective-permute-start.22 = (bf16[64,2688]{1,0:T(8,128)(2,1)S(1)}, bf16[64,2688]{1,0:T(8,128)(2,1)S(1)}, u32[]{:S(2)}, u32[]{:S(2)}) collective-permute-start(bf16[64,2688]{1,0:T(8,128)(2,1)S(1)} %slice.191), channel_id=1, source_target_pairs={{0,3},{3,0},{1,2},{2,1},{4,7},{7,4},{5,6},{6,5},{8,11},{11,8},{9,1... | collective-permute-start | bytes 1032200 | tf_op jit(solution)/shard_map/ppermute | solution.py:170

commit v6 on v4

--- a/solution.py
+++ b/solution.py
@@ -240,9 +240,10 @@
         jnp.concatenate([pick_rest, other_rest], axis=2), jnp.concatenate([tokens, other], axis=0)
     )
     theirs = exchange_main(after(rows_of(pick, other), mine, nears[0]))
-    rest = exchange_rest(after(rest, theirs))
+    copied = [along(own, FROM_HOME) for own in owns]
+    whole = down_weight[0], along(after(down_weight[0], copied[0]), FROM_HOME)
+    rest = exchange_rest(after(rest, theirs, whole[1], copied[1]))
     fars = [along(owns[0], FAR), along(after(owns[1], nears[0], theirs), FAR)]
-    copied = [along(own, FROM_HOME) for own in owns]
     across = [
         along(after(near, got), SIBLING) for near, got in zip(nears, (theirs, rest), strict=True)
     ]
@@ -260,7 +261,6 @@
         own = after(down_weight[0][:, at : at + step], *earlier)
         return along(own, NEXT), along(own, FAR)
 
-    whole = down_weight[0], along(after(down_weight[0], *copied), FROM_HOME)
     units = [*zip(owns, copied, strict=True), *zip(nears), *zip(across), (brought_0, fars[0])]
     first = hidden_units(flag, after(mine, whole[1]), theirs, rest, units)
     brought_1 = along(after(fars[1], first), TO_HOME)

time: 439 us -> 434 us (0.989)
    unnamed x31 -> x25, local copies, waits for them, and re-layouts: 10.4 us -> 5.05 us
    all_to_all x5, waiting for transfers between devices: 108 us -> 112 us  [exchange_main(): return lax.all_to_all(parts, EXP, 0, 0, tiled=True).reshape(rows.shape)]
where the time goes in v6:
time: 434 us; the launch traced here: 433 us
  waiting for transfers between devices  215 us (50%)
  starting transfers between devices  106 us (24%)
  Pallas kernels  53.5 us (12%)
  matrix products  21.4 us (5%)
  other arithmetic  18.3 us (4%)
  local copies, waits for them, and re-layouts  18.3 us (4%)
    all_to_all x5, waiting for transfers between devices, exchange_main(): return lax.all_to_all(parts, EXP, 0, 0, tiled=True).reshape(rows.shape)  112 us
    ppermute x19, starting transfers between devices, along(): return lax.ppermute(value, COL, pairs)  56.3 us
    all_to_all x2, waiting for transfers between devices, exchange_rest(): lax.all_to_all(parts, ('y', 'x'), 0, 0, tiled=True).reshape(rows.shape)  46.6 us
    ppermute x19, waiting for transfers between devices, along(): return lax.ppermute(value, COL, pairs)  35.7 us
    pallas_call x2, Pallas kernels, hidden_units(): pl.pallas_call(functools.partial(hidden_kernel, kinds=kinds), grid_spec=p...  33.9 us
    all_to_all x5, starting transfers between devices, exchange_main(): return lax.all_to_all(parts, EXP, 0, 0, tiled=True).reshape(rows.shape)  30.8 us
    ppermute x4, waiting for transfers between devices, pair_exchange(): return lax.ppermute(value, ('zh', 'zl'), PAIR)  20.9 us
    pallas_call x3, Pallas kernels, down_rows(): pl.pallas_call(down_kernel, grid_spec=pltpu.PrefetchScalarGridSpec(num_sc...  19.5 us
  transfers between devices with their start and end apart: 30, of which 17 were waited for; matrix products, arithmetic and copies ran while one was open for 9% of the time, Pallas kernels for 12%

profile of v6, /device:TPU:0, one launch (start us, length us, event | category | flops | bytes accessed | tf_op | source)
XLA Modules:
  0.0 432.7 jit_solution(15674272300566878935)
XLA Ops:
  1.5 2.2 fusion.6
  3.7 4.1 collective-permute-start
  7.8 3.6 slice_bitcast_fusion
  13.2 2.9 convolution_convert_fusion.1
  16.1 12.8 %collective-permute-done = bf16[64,7296]{1,0:T(8,128)(2,1)} collective-permute-done((bf16[64,7296]{1,0:T(8,128)(2,1)}, bf16[64,7296]{1,0:T(8,128)(2,1)}, u32[]{:S(2)}, u32[]{:S(2)}) %collective-permute-start) | collective-permute-done | bytes 933920 | tf_op jit(solution)/shard_map/ppermute | solution.py:170
  28.8 2.2 slice.110
  33.1 5.5 %pad_maximum_fusion.refs_0_.own = bf16[256,8960]{1,0:T(8,128)(2,1)} fusion(bf16[256,1792]{1,0:T(8,128)(2,1)S(1)} %slice.142, bf16[128,7168]{1,0:T(8,128)(2,1)S(1)} %copy-done.5, bf16[128,7168]{1,0:T(8,128)(2,1)S(1)} %get-tuple-element.66), kind=kLoop, calls=%fused_computation.3 | loop fusion | flops 13762560 | bytes 9175040 | tf_op jit(solution)/shard_map/concatenate | solution.py:235
  38.6 3.4 collective-permute-start.1
  42.0 8.1 %all-to-all-start = ((bf16[32,8,7168]{2,1,0:T(8,128)(2,1)}), bf16[32,8,7168]{2,1,0:T(8,128)(2,1)}, u32[]{:S(2)}, u32[]{:S(2)}) async-start(bf16[32,8,7168]{2,1,0:T(8,128)(2,1)} %bitcast.75), calls=%async_computation | async-start | bytes 7340032 | tf_op jit(solution)/shard_map/all_to_all | solution.py:215
  51.4 3.5 pad_maximum_fusion.1.refs_2_
  55.0 3.9 collective-permute-start.4
  58.9 3.2 collective-permute-start.2
  62.1 4.0 convolution_convert_fusion
  66.1 31.7 %all-to-all-done = bf16[32,8,7168]{2,1,0:T(8,128)(2,1)} async-done(((bf16[32,8,7168]{2,1,0:T(8,128)(2,1)}), bf16[32,8,7168]{2,1,0:T(8,128)(2,1)}, u32[]{:S(2)}, u32[]{:S(2)}) %all-to-all-start) | async-done | bytes 3670048 | tf_op jit(solution)/shard_map/all_to_all | solution.py:215
  97.8 5.0 %all-to-all-start.1 = ((bf16[32,8,7168]{2,1,0:T(8,128)(2,1)}), bf16[32,8,7168]{2,1,0:T(8,128)(2,1)}, u32[]{:S(2)}, u32[]{:S(2)}) async-start(bf16[32,8,7168]{2,1,0:T(8,128)(2,1)} %bitcast.76), calls=%async_computation.1 | async-start | bytes 7340032 | tf_op jit(solution)/shard_map/all_to_all | solution.py:215
  102.8 2.7 collective-permute-start.8
  109.1 41.3 %all-to-all-done.1 = bf16[32,8,7168]{2,1,0:T(8,128)(2,1)} async-done(((bf16[32,8,7168]{2,1,0:T(8,128)(2,1)}), bf16[32,8,7168]{2,1,0:T(8,128)(2,1)}, u32[]{:S(2)}, u32[]{:S(2)}) %all-to-all-start.1) | async-done | bytes 3670048 | tf_op jit(solution)/shard_map/all_to_all | solution.py:215
  150.4 3.7 all-to-all-start.2
  154.3 26.3 %all-to-all-done.2 = bf16[16,8,7168]{2,1,0:T(8,128)(2,1)S(1)} async-done(((bf16[16,8,7168]{2,1,0:T(8,128)(2,1)}), bf16[16,8,7168]{2,1,0:T(8,128)(2,1)S(1)}, u32[]{:S(2)}, u32[]{:S(2)}) %all-to-all-start.2) | async-done | bytes 1835040 | tf_op jit(solution)/shard_map/all_to_all | solution.py:219
  181.9 5.8 %collective-permute-done.5.refs_5_ = bf16[256,7168]{1,0:T(8,128)(2,1)} collective-permute-done((bf16[256,7168]{1,0:T(8,128)(2,1)}, bf16[256,7168]{1,0:T(8,128)(2,1)}, u32[]{:S(2)}, u32[]{:S(2)}) %collective-permute-start.5) | collective-permute-done | bytes 3670048 | tf_op jit(solution)/shard_map/ppermute | solution.py:35
  187.6 15.0 %collective-permute-start.7 = (bf16[256,7168]{1,0:T(8,128)(2,1)}, bf16[256,7168]{1,0:T(8,128)(2,1)}, u32[]{:S(2)}, u32[]{:S(2)}) collective-permute-start(bf16[256,7168]{1,0:T(8,128)(2,1)} %collective-permute-done.5.refs_5_), channel_id=1, source_target_pairs={{0,4},{4,0},{1,5},{5,1},{2,6},{6,2},{3,7},{7,3},{8,12},{12,8},{9,1... | collective-permute-start | bytes 11010056 | tf_op jit(solution)/shard_map/ppermute | solution.py:35
  202.6 2.4 collective-permute-start.10
  205.1 8.2 %collective-permute-done.7.refs_7_ = bf16[256,7168]{1,0:T(8,128)(2,1)} collective-permute-done((bf16[256,7168]{1,0:T(8,128)(2,1)}, bf16[256,7168]{1,0:T(8,128)(2,1)}, u32[]{:S(2)}, u32[]{:S(2)}) %collective-permute-start.7) | collective-permute-done | bytes 3670048 | tf_op jit(solution)/shard_map/ppermute | solution.py:35
  213.2 27.0 %shard_map.64.first = bf16[640,896]{1,0:T(8,128)(2,1)S(1)} custom-call(s32[1]{0:T(128)} %bitcast.4.flag, bf16[256,7168]{1,0:T(8,128)(2,1)} %bitcast.6.mine, bf16[256,7168]{1,0:T(8,128)(2,1)} %bitcast.13.theirs, bf16[128,7168]{1,0:T(8,128)(2,1)S(1)} %bitcast.73, bf16[256,8960]{1,0:T(8,128)(2,1)} %pad_maximum_fusion.refs_0_.own, ...), custom_call_target="tpu_custom_call" | custom-call | flops 1 | bytes 1 | tf_op jit(solution)/shard_map/pallas_call | solution.py:95
  241.5 3.5 fusion.41
  247.1 9.0 %collective-permute-done.11.refs_0_ = bf16[256,7168]{1,0:T(8,128)(2,1)S(1)} collective-permute-done((bf16[256,7168]{1,0:T(8,128)(2,1)}, bf16[256,7168]{1,0:T(8,128)(2,1)S(1)}, u32[]{:S(2)}, u32[]{:S(2)}) %collective-permute-start.11) | collective-permute-done | bytes 3670048 | tf_op jit(solution)/shard_map/ppermute | solution.py:35
  257.9 7.0 %shard_map.65.last = bf16[640,128]{1,0:T(8,128)(2,1)S(1)} custom-call(s32[1]{0:T(128)} %bitcast.4.flag, bf16[256,7168]{1,0:T(8,128)(2,1)} %bitcast.6.mine, bf16[256,7168]{1,0:T(8,128)(2,1)} %bitcast.13.theirs, bf16[128,7168]{1,0:T(8,128)(2,1)S(1)} %bitcast.74, bf16[256,7168]{1,0:T(8,128)(2,1)} %copy-done.8, bf16[256,7168]{1,0:T(8,128)(2,1)} %collective-permute-done.10.refs_1_), custom_call_target="tpu_custom_call" | custom-call | flops 1 | bytes 1 | tf_op jit(solution)/shard_map/pallas_call | solution.py:95
  264.8 5.8 %shard_map.66 = (bf16[32,16,1792]{2,1,0:T(8,128)(2,1)}, bf16[128,1792]{1,0:T(8,128)(2,1)S(1)}) custom-call(s32[1]{0:T(128)} %bitcast.4.flag, bf16[640,896]{1,0:T(8,128)(2,1)S(1)} %shard_map.64.first, bf16[640,128]{1,0:T(8,128)(2,1)S(1)} %shard_map.65.last, bf16[256,8960]{1,0:T(8,128)(2,1)} %pad_maximum_fusion.refs_0_.own, ...), custom_call_target="tpu_custom_call" | custom-call | flops 2348810240 | bytes 7274496 | tf_op jit(solution)/shard_map/pallas_call | solution.py:140
  270.7 8.9 %all-to-all-start.3 = ((bf16[32,16,1792]{2,1,0:T(8,128)(2,1)}), bf16[32,16,1792]{2,1,0:T(8,128)(2,1)}, u32[]{:S(2)}, u32[]{:S(2)}) async-start(bf16[32,16,1792]{2,1,0:T(8,128)(2,1)} %get-tuple-element.44), calls=%async_computation.3 | async-start | bytes 3670016 | tf_op jit(solution)/shard_map/all_to_all | solution.py:215
  279.6 8.4 %collective-permute-start.13 = (bf16[256,2688]{1,0:T(8,128)(2,1)}, bf16[256,2688]{1,0:T(8,128)(2,1)S(1)}, u32[]{:S(2)}, u32[]{:S(2)}) collective-permute-start(bf16[256,2688]{1,0:T(8,128)(2,1)} %collective-permute-done.12.near), channel_id=1, source_target_pairs={{0,4},{4,0},{1,5},{5,1},{2,6},{6,2},{3,7},{7,3},{8,12},{12,8},{9,1... | collective-permute-start | bytes 4128776 | tf_op jit(solution)/shard_map/ppermute | solution.py:35
  293.2 6.6 %shard_map.67 = (bf16[32,16,2688]{2,1,0:T(8,128)(2,1)S(1)}, bf16[128,2688]{1,0:T(8,128)(2,1)S(1)}) custom-call(s32[1]{0:T(128)} %bitcast.4.flag, bf16[640,896]{1,0:T(8,128)(2,1)S(1)} %shard_map.64.first, bf16[640,128]{1,0:T(8,128)(2,1)S(1)} %shard_map.65.last, bf16[256,7168]{1,0:T(8,128)(2,1)} %bitcast.7.own, ...), custom_call_target="tpu_custom_call" | custom-call | flops 3523215360 | bytes 10256384 | tf_op jit(solution)/shard_map/pallas_call | solution.py:140
  302.2 4.3 all-to-all-done.3
  306.5 4.8 %all-to-all-start.4 = ((bf16[32,16,2688]{2,1,0:T(8,128)(2,1)}), bf16[32,16,2688]{2,1,0:T(8,128)(2,1)}, u32[]{:S(2)}, u32[]{:S(2)}) async-start(bf16[32,16,2688]{2,1,0:T(8,128)(2,1)} %copy-done), calls=%async_computation.4 | async-start | bytes 5505024 | tf_op jit(solution)/shard_map/all_to_all | solution.py:215
  311.3 7.1 %collective-permute-done.16.near = bf16[256,2688]{1,0:T(8,128)(2,1)S(1)} collective-permute-done((bf16[256,2688]{1,0:T(8,128)(2,1)}, bf16[256,2688]{1,0:T(8,128)(2,1)S(1)}, u32[]{:S(2)}, u32[]{:S(2)}) %collective-permute-start.16) | collective-permute-done | bytes 1376288 | tf_op jit(solution)/shard_map/ppermute | solution.py:35
  318.4 6.5 %collective-permute-start.17 = (bf16[256,2688]{1,0:T(8,128)(2,1)S(1)}, bf16[256,2688]{1,0:T(8,128)(2,1)S(1)}, u32[]{:S(2)}, u32[]{:S(2)}) collective-permute-start(bf16[256,2688]{1,0:T(8,128)(2,1)S(1)} %collective-permute-done.16.near), channel_id=1, source_target_pairs={{0,4},{4,0},{1,5},{5,1},{2,6},{6,2},{3,7},{7,3},{8,12},{12,8},{9,1... | collective-permute-start | bytes 4128776 | tf_op jit(solution)/shard_map/ppermute | solution.py:35
  327.6 2.5 collective-permute-done.19.brought
  330.1 7.1 %shard_map.68 = (bf16[32,16,2688]{2,1,0:T(8,128)(2,1)}, bf16[128,2688]{1,0:T(8,128)(2,1)S(1)}) custom-call(s32[1]{0:T(128)} %bitcast.4.flag, bf16[640,896]{1,0:T(8,128)(2,1)S(1)} %shard_map.64.first, bf16[640,128]{1,0:T(8,128)(2,1)S(1)} %shard_map.65.last, bf16[256,7168]{1,0:T(8,128)(2,1)} %bitcast.7.own, bf16[256,7168]{1,0:T(8,128)(2,1)} %collective-permute-done.2.copied, ...), custom_call_target="tpu_custom_call" | custom-call | flops 3523215360 | bytes 10256384 | tf_op jit(solution)/shard_map/pallas_call | solution.py:140
  338.7 10.1 %all-to-all-done.4 = bf16[32,16,2688]{2,1,0:T(8,128)(2,1)} async-done(((bf16[32,16,2688]{2,1,0:T(8,128)(2,1)}), bf16[32,16,2688]{2,1,0:T(8,128)(2,1)}, u32[]{:S(2)}, u32[]{:S(2)}) %all-to-all-start.4) | async-done | bytes 2752544 | tf_op jit(solution)/shard_map/all_to_all | solution.py:215
  348.8 4.4 %all-to-all-start.5 = ((bf16[16,8,7168]{2,1,0:T(8,128)(2,1)}), bf16[16,8,7168]{2,1,0:T(8,128)(2,1)}, u32[]{:S(2)}, u32[]{:S(2)}) async-start(bf16[16,8,7168]{2,1,0:T(8,128)(2,1)} %bitcast.32), calls=%async_computation.5 | async-start | bytes 3670016 | tf_op jit(solution)/shard_map/all_to_all | solution.py:219
  353.7 4.3 fusion.16
  358.0 20.2 %all-to-all-done.5 = bf16[16,8,7168]{2,1,0:T(8,128)(2,1)} async-done(((bf16[16,8,7168]{2,1,0:T(8,128)(2,1)}), bf16[16,8,7168]{2,1,0:T(8,128)(2,1)}, u32[]{:S(2)}, u32[]{:S(2)}) %all-to-all-start.5) | async-done | bytes 1835040 | tf_op jit(solution)/shard_map/all_to_all | solution.py:219
  378.3 4.1 all-to-all-start.6
  383.8 2.2 convolution_add_fusion.2
  386.1 2.3 collective-permute-start.20
  392.6 2.5 collective-permute-done.20
  395.2 24.6 %all-to-all-done.6 = bf16[32,16,2688]{2,1,0:T(8,128)(2,1)S(1)} async-done(((bf16[32,16,2688]{2,1,0:T(8,128)(2,1)}), bf16[32,16,2688]{2,1,0:T(8,128)(2,1)S(1)}, u32[]{:S(2)}, u32[]{:S(2)}) %all-to-all-start.6) | async-done | bytes 2752544 | tf_op jit(solution)/shard_map/all_to_all | solution.py:215
  422.6 2.3 collective-permute-start.22
  426.0 5.6 %collective-permute-done.22 = bf16[64,2688]{1,0:T(8,128)(2,1)S(1)} collective-permute-done((bf16[64,2688]{1,0:T(8,128)(2,1)S(1)}, bf16[64,2688]{1,0:T(8,128)(2,1)S(1)}, u32[]{:S(2)}, u32[]{:S(2)}) %collective-permute-start.22) | collective-permute-done | bytes 344096 | tf_op jit(solution)/shard_map/ppermute | solution.py:170
  (101 shorter events, 39.7 us)
Async XLA Ops:
  3.7 25.1 %collective-permute-start = (bf16[64,7296]{1,0:T(8,128)(2,1)}, bf16[64,7296]{1,0:T(8,128)(2,1)}, u32[]{:S(2)}, u32[]{:S(2)}) collective-permute-start(bf16[64,7296]{1,0:T(8,128)(2,1)} %fusion.6), channel_id=1, source_target_pairs={{0,3},{3,0},{1,2},{2,1},{4,7},{7,4},{5,6},{6,5},{8,11},{11,8},{9,1... | collective-permute-start | bytes 2801672 | tf_op jit(solution)/shard_map/ppermute | solution.py:170
  11.4 1.4 copy-start.11
  11.4 1.8 copy-start.4
  13.2 17.8 %copy-start.10 = (bf16[1,256,7168]{2,1,0:T(8,128)(2,1)S(1)}, bf16[1,256,7168]{2,1,0:T(8,128)(2,1)}, u32[]{:S(2)}) copy-start(bf16[1,256,7168]{2,1,0:T(8,128)(2,1)} %param.9) | copy-start | bytes 11010052
  31.0 2.2 copy-start.5
  38.6 20.3 %collective-permute-start.1 = (bf16[256,8960]{1,0:T(8,128)(2,1)}, bf16[256,8960]{1,0:T(8,128)(2,1)}, u32[]{:S(2)}, u32[]{:S(2)}) collective-permute-start(bf16[256,8960]{1,0:T(8,128)(2,1)} %pad_maximum_fusion.refs_0_.own), channel_id=1, source_target_pairs={{0,4},{1,5},{6,2},{7,3},{8,12},{9,13},{14,10},{15,11},{16,20},{17,... | collective-permute-start | bytes 13762568 | tf_op jit(solution)/shard_map/ppermute | solution.py:35
  42.0 55.8 %collective-permute-start.3 = (bf16[256,8960]{1,0:T(8,128)(2,1)}, bf16[256,8960]{1,0:T(8,128)(2,1)}, u32[]{:S(2)}, u32[]{:S(2)}) collective-permute-start(bf16[256,8960]{1,0:T(8,128)(2,1)} %pad_maximum_fusion.refs_0_.own), channel_id=1, source_target_pairs={{0,1},{1,0},{6,7},{7,6},{4,3},{3,4},{5,2},{2,5},{8,9},{9,8},{14,15... | collective-permute-start | bytes 13762568 | tf_op jit(solution)/shard_map/ppermute | solution.py:35
  42.0 55.7 %all-to-all-start = ((bf16[32,8,7168]{2,1,0:T(8,128)(2,1)}), bf16[32,8,7168]{2,1,0:T(8,128)(2,1)}, u32[]{:S(2)}, u32[]{:S(2)}) async-start(bf16[32,8,7168]{2,1,0:T(8,128)(2,1)} %bitcast.75), calls=%async_computation | async-start | bytes 7340032 | tf_op jit(solution)/shard_map/all_to_all | solution.py:215
  55.0 54.2 %collective-permute-start.4 = (bf16[256,7168]{1,0:T(8,128)(2,1)}, bf16[256,7168]{1,0:T(8,128)(2,1)}, u32[]{:S(2)}, u32[]{:S(2)}) collective-permute-start(bf16[256,7168]{1,0:T(8,128)(2,1)} %pad_maximum_fusion.1.refs_2_), channel_id=1, source_target_pairs={{0,4},{1,5},{6,2},{7,3},{8,12},{9,13},{14,10},{15,11},{16,20},{17,... | collective-permute-start | bytes 11010056 | tf_op jit(solution)/shard_map/ppermute | solution.py:35
  58.9 91.5 %collective-permute-start.2 = (bf16[256,7168]{1,0:T(8,128)(2,1)}, bf16[256,7168]{1,0:T(8,128)(2,1)}, u32[]{:S(2)}, u32[]{:S(2)}) collective-permute-start(bf16[256,7168]{1,0:T(8,128)(2,1)} %bitcast.7.own), channel_id=1, source_target_pairs={{0,4},{1,5},{6,2},{7,3},{8,12},{9,13},{14,10},{15,11},{16,20},{17,... | collective-permute-start | bytes 11010056 | tf_op jit(solution)/shard_map/ppermute | solution.py:35
  97.8 9.3 %copy-start.9 = (bf16[64,7168]{1,0:T(8,128)(2,1)S(1)}, bf16[64,7168]{1,0:T(8,128)(2,1)}, u32[]{:S(2)}) copy-start(bf16[64,7168]{1,0:T(8,128)(2,1)} %slice.110) | copy-start | bytes 2752516
  97.8 52.6 %all-to-all-start.1 = ((bf16[32,8,7168]{2,1,0:T(8,128)(2,1)}), bf16[32,8,7168]{2,1,0:T(8,128)(2,1)}, u32[]{:S(2)}, u32[]{:S(2)}) async-start(bf16[32,8,7168]{2,1,0:T(8,128)(2,1)} %bitcast.76), calls=%async_computation.1 | async-start | bytes 7340032 | tf_op jit(solution)/shard_map/all_to_all | solution.py:215
  102.8 51.5 %collective-permute-start.8 = (bf16[256,8960]{1,0:T(8,128)(2,1)}, bf16[256,8960]{1,0:T(8,128)(2,1)}, u32[]{:S(2)}, u32[]{:S(2)}) collective-permute-start(bf16[256,8960]{1,0:T(8,128)(2,1)} %pad_maximum_fusion.refs_0_.own), channel_id=1, source_target_pairs={{5,3},{3,5},{4,2},{2,4},{13,11},{11,13},{12,10},{10,12},{21,19},{1... | collective-permute-start | bytes 13762568 | tf_op jit(solution)/shard_map/ppermute | solution.py:35
  105.5 82.1 %collective-permute-start.5 = (bf16[256,7168]{1,0:T(8,128)(2,1)}, bf16[256,7168]{1,0:T(8,128)(2,1)}, u32[]{:S(2)}, u32[]{:S(2)}) collective-permute-start(bf16[256,7168]{1,0:T(8,128)(2,1)} %pad_maximum_fusion.1.refs_2_), channel_id=1, source_target_pairs={{0,1},{1,0},{6,7},{7,6},{4,3},{3,4},{5,2},{2,5},{8,9},{9,8},{14,15... | collective-permute-start | bytes 11010056 | tf_op jit(solution)/shard_map/ppermute | solution.py:35
  150.4 30.2 %all-to-all-start.2 = ((bf16[16,8,7168]{2,1,0:T(8,128)(2,1)}), bf16[16,8,7168]{2,1,0:T(8,128)(2,1)S(1)}, u32[]{:S(2)}, u32[]{:S(2)}) async-start(bf16[16,8,7168]{2,1,0:T(8,128)(2,1)} %bitcast.78), calls=%async_computation.2 | async-start | bytes 3670016 | tf_op jit(solution)/shard_map/all_to_all | solution.py:219
  154.2 50.9 %collective-permute-start.6 = (bf16[256,8960]{1,0:T(8,128)(2,1)}, bf16[256,8960]{1,0:T(8,128)(2,1)}, u32[]{:S(2)}, u32[]{:S(2)}) collective-permute-start(bf16[256,8960]{1,0:T(8,128)(2,1)} %collective-permute-done.3.refs_4_.near), channel_id=1, source_target_pairs={{0,4},{4,0},{1,5},{5,1},{2,6},{6,2},{3,7},{7,3},{8,12},{12,8},{9,1... | collective-permute-start | bytes 13762568 | tf_op jit(solution)/shard_map/ppermute | solution.py:35
  180.6 32.6 %collective-permute-start.9 = (bf16[256,8960]{1,0:T(8,128)(2,1)}, bf16[256,8960]{1,0:T(8,128)(2,1)}, u32[]{:S(2)}, u32[]{:S(2)}) collective-permute-start(bf16[256,8960]{1,0:T(8,128)(2,1)} %collective-permute-done.8.refs_9_.far), channel_id=1, source_target_pairs={{4,0},{5,1},{2,6},{3,7},{12,8},{13,9},{10,14},{11,15},{20,16},{21,... | collective-permute-start | bytes 13762568 | tf_op jit(solution)/shard_map/ppermute | solution.py:35
  187.6 25.6 %collective-permute-start.7 = (bf16[256,7168]{1,0:T(8,128)(2,1)}, bf16[256,7168]{1,0:T(8,128)(2,1)}, u32[]{:S(2)}, u32[]{:S(2)}) collective-permute-start(bf16[256,7168]{1,0:T(8,128)(2,1)} %collective-permute-done.5.refs_5_), channel_id=1, source_target_pairs={{0,4},{4,0},{1,5},{5,1},{2,6},{6,2},{3,7},{7,3},{8,12},{12,8},{9,1... | collective-permute-start | bytes 11010056 | tf_op jit(solution)/shard_map/ppermute | solution.py:35
  202.6 37.6 %collective-permute-start.10 = (bf16[256,7168]{1,0:T(8,128)(2,1)}, bf16[256,7168]{1,0:T(8,128)(2,1)}, u32[]{:S(2)}, u32[]{:S(2)}) collective-permute-start(bf16[256,7168]{1,0:T(8,128)(2,1)} %pad_maximum_fusion.1.refs_2_), channel_id=1, source_target_pairs={{5,3},{3,5},{4,2},{2,4},{13,11},{11,13},{12,10},{10,12},{21,19},{1... | collective-permute-start | bytes 11010056 | tf_op jit(solution)/shard_map/ppermute | solution.py:35
  240.2 15.8 %collective-permute-start.11 = (bf16[256,7168]{1,0:T(8,128)(2,1)}, bf16[256,7168]{1,0:T(8,128)(2,1)S(1)}, u32[]{:S(2)}, u32[]{:S(2)}) collective-permute-start(bf16[256,7168]{1,0:T(8,128)(2,1)} %collective-permute-done.10.refs_1_), channel_id=1, source_target_pairs={{4,0},{5,1},{2,6},{3,7},{12,8},{13,9},{10,14},{11,15},{20,16},{21,... | collective-permute-start | bytes 11010056 | tf_op jit(solution)/shard_map/ppermute | solution.py:35
  245.0 34.5 %collective-permute-start.12 = (bf16[256,2688]{1,0:T(8,128)(2,1)}, bf16[256,2688]{1,0:T(8,128)(2,1)}, u32[]{:S(2)}, u32[]{:S(2)}) collective-permute-start(bf16[256,2688]{1,0:T(8,128)(2,1)} %get-tuple-element.46), channel_id=1, source_target_pairs={{0,1},{1,0},{6,7},{7,6},{4,3},{3,4},{5,2},{2,5},{8,9},{9,8},{14,15... | collective-permute-start | bytes 4128776 | tf_op jit(solution)/shard_map/ppermute | solution.py:35
  245.3 42.6 %collective-permute-start.14 = (bf16[256,2688]{1,0:T(8,128)(2,1)}, bf16[256,2688]{1,0:T(8,128)(2,1)}, u32[]{:S(2)}, u32[]{:S(2)}) collective-permute-start(bf16[256,2688]{1,0:T(8,128)(2,1)} %get-tuple-element.46), channel_id=1, source_target_pairs={{5,3},{3,5},{4,2},{2,4},{13,11},{11,13},{12,10},{10,12},{21,19},{1... | collective-permute-start | bytes 4128776 | tf_op jit(solution)/shard_map/ppermute | solution.py:35
  256.0 1.8 copy-start.8
  270.7 35.8 %all-to-all-start.3 = ((bf16[32,16,1792]{2,1,0:T(8,128)(2,1)}), bf16[32,16,1792]{2,1,0:T(8,128)(2,1)}, u32[]{:S(2)}, u32[]{:S(2)}) async-start(bf16[32,16,1792]{2,1,0:T(8,128)(2,1)} %get-tuple-element.44), calls=%async_computation.3 | async-start | bytes 3670016 | tf_op jit(solution)/shard_map/all_to_all | solution.py:215
  279.6 11.6 %collective-permute-start.13 = (bf16[256,2688]{1,0:T(8,128)(2,1)}, bf16[256,2688]{1,0:T(8,128)(2,1)S(1)}, u32[]{:S(2)}, u32[]{:S(2)}) collective-permute-start(bf16[256,2688]{1,0:T(8,128)(2,1)} %collective-permute-done.12.near), channel_id=1, source_target_pairs={{0,4},{4,0},{1,5},{5,1},{2,6},{6,2},{3,7},{7,3},{8,12},{12,8},{9,1... | collective-permute-start | bytes 4128776 | tf_op jit(solution)/shard_map/ppermute | solution.py:35
  288.0 5.2 %collective-permute-start.15 = (bf16[256,2688]{1,0:T(8,128)(2,1)}, bf16[256,2688]{1,0:T(8,128)(2,1)S(1)}, u32[]{:S(2)}, u32[]{:S(2)}) collective-permute-start(bf16[256,2688]{1,0:T(8,128)(2,1)} %collective-permute-done.14.far), channel_id=1, source_target_pairs={{4,0},{5,1},{2,6},{3,7},{12,8},{13,9},{10,14},{11,15},{20,16},{21,... | collective-permute-start | bytes 4128776 | tf_op jit(solution)/shard_map/ppermute | solution.py:35
  289.3 29.1 %collective-permute-start.16 = (bf16[256,2688]{1,0:T(8,128)(2,1)}, bf16[256,2688]{1,0:T(8,128)(2,1)S(1)}, u32[]{:S(2)}, u32[]{:S(2)}) collective-permute-start(bf16[256,2688]{1,0:T(8,128)(2,1)} %get-tuple-element.50), channel_id=1, source_target_pairs={{0,1},{1,0},{6,7},{7,6},{4,3},{3,4},{5,2},{2,5},{8,9},{9,8},{14,15... | collective-permute-start | bytes 4128776 | tf_op jit(solution)/shard_map/ppermute | solution.py:35
  289.4 35.5 %collective-permute-start.18 = (bf16[256,2688]{1,0:T(8,128)(2,1)}, bf16[256,2688]{1,0:T(8,128)(2,1)}, u32[]{:S(2)}, u32[]{:S(2)}) collective-permute-start(bf16[256,2688]{1,0:T(8,128)(2,1)} %get-tuple-element.50), channel_id=1, source_target_pairs={{5,3},{3,5},{4,2},{2,4},{13,11},{11,13},{12,10},{10,12},{21,19},{1... | collective-permute-start | bytes 4128776 | tf_op jit(solution)/shard_map/ppermute | solution.py:35
  299.8 1.6 copy-start
  301.3 0.8 copy-start.1
  306.5 42.3 %all-to-all-start.4 = ((bf16[32,16,2688]{2,1,0:T(8,128)(2,1)}), bf16[32,16,2688]{2,1,0:T(8,128)(2,1)}, u32[]{:S(2)}, u32[]{:S(2)}) async-start(bf16[32,16,2688]{2,1,0:T(8,128)(2,1)} %copy-done), calls=%async_computation.4 | async-start | bytes 5505024 | tf_op jit(solution)/shard_map/all_to_all | solution.py:215
  318.4 9.3 %collective-permute-start.17 = (bf16[256,2688]{1,0:T(8,128)(2,1)S(1)}, bf16[256,2688]{1,0:T(8,128)(2,1)S(1)}, u32[]{:S(2)}, u32[]{:S(2)}) collective-permute-start(bf16[256,2688]{1,0:T(8,128)(2,1)S(1)} %collective-permute-done.16.near), channel_id=1, source_target_pairs={{0,4},{4,0},{1,5},{5,1},{2,6},{6,2},{3,7},{7,3},{8,12},{12,8},{9,1... | collective-permute-start | bytes 4128776 | tf_op jit(solution)/shard_map/ppermute | solution.py:35
  324.9 5.2 %collective-permute-start.19 = (bf16[256,2688]{1,0:T(8,128)(2,1)}, bf16[256,2688]{1,0:T(8,128)(2,1)S(1)}, u32[]{:S(2)}, u32[]{:S(2)}) collective-permute-start(bf16[256,2688]{1,0:T(8,128)(2,1)} %collective-permute-done.18.far), channel_id=1, source_target_pairs={{4,0},{5,1},{2,6},{3,7},{12,8},{13,9},{10,14},{11,15},{20,16},{21,... | collective-permute-start | bytes 4128776 | tf_op jit(solution)/shard_map/ppermute | solution.py:35
  326.4 10.8 %copy-start.2 = (bf16[128,2688]{1,0:T(8,128)(2,1)S(1)}, bf16[128,2688]{1,0:T(8,128)(2,1)}, u32[]{:S(2)}) copy-start(bf16[128,2688]{1,0:T(8,128)(2,1)} %copy-done.1) | copy-start | bytes 2064388
  348.8 29.5 %all-to-all-start.5 = ((bf16[16,8,7168]{2,1,0:T(8,128)(2,1)}), bf16[16,8,7168]{2,1,0:T(8,128)(2,1)}, u32[]{:S(2)}, u32[]{:S(2)}) async-start(bf16[16,8,7168]{2,1,0:T(8,128)(2,1)} %bitcast.32), calls=%async_computation.5 | async-start | bytes 3670016 | tf_op jit(solution)/shard_map/all_to_all | solution.py:219
  378.3 41.6 %all-to-all-start.6 = ((bf16[32,16,2688]{2,1,0:T(8,128)(2,1)}), bf16[32,16,2688]{2,1,0:T(8,128)(2,1)S(1)}, u32[]{:S(2)}, u32[]{:S(2)}) async-start(bf16[32,16,2688]{2,1,0:T(8,128)(2,1)} %bitcast.35), calls=%async_computation.6 | async-start | bytes 5505024 | tf_op jit(solution)/shard_map/all_to_all | solution.py:215
  385.9 2.4 copy-start.3
  386.1 9.0 %collective-permute-start.20 = (bf16[64,1792]{1,0:T(8,128)(2,1)S(1)}, bf16[64,1792]{1,0:T(8,128)(2,1)S(1)}, u32[]{:S(2)}, u32[]{:S(2)}) collective-permute-start(bf16[64,1792]{1,0:T(8,128)(2,1)S(1)} %slice.193), channel_id=1, source_target_pairs={{0,3},{3,0},{1,2},{2,1},{4,7},{7,4},{5,6},{6,5},{8,11},{11,8},{9,1... | collective-permute-start | bytes 688136 | tf_op jit(solution)/shard_map/ppermute | solution.py:170
  390.2 4.9 %copy-start.6 = (f32[128,2688]{1,0:T(8,128)}, f32[128,2688]{1,0:T(8,128)S(1)}, u32[]{:S(2)}) copy-start(f32[128,2688]{1,0:T(8,128)S(1)} %slice_add_fusion.1) | copy-start | bytes 4128772
  391.0 33.9 %collective-permute-start.21 = (bf16[64,2688]{1,0:T(8,128)(2,1)}, bf16[64,2688]{1,0:T(8,128)(2,1)}, u32[]{:S(2)}, u32[]{:S(2)}) collective-permute-start(bf16[64,2688]{1,0:T(8,128)(2,1)} %slice.192), channel_id=1, source_target_pairs={{0,3},{3,0},{1,2},{2,1},{4,7},{7,4},{5,6},{6,5},{8,11},{11,8},{9,1... | collective-permute-start | bytes 1032200 | tf_op jit(solution)/shard_map/ppermute | solution.py:170
  422.4 2.5 copy-start.7
  422.6 9.0 %collective-permute-start.22 = (bf16[64,2688]{1,0:T(8,128)(2,1)S(1)}, bf16[64,2688]{1,0:T(8,128)(2,1)S(1)}, u32[]{:S(2)}, u32[]{:S(2)}) collective-permute-start(bf16[64,2688]{1,0:T(8,128)(2,1)S(1)} %slice.191), channel_id=1, source_target_pairs={{0,3},{3,0},{1,2},{2,1},{4,7},{7,4},{5,6},{6,5},{8,11},{11,8},{9,1... | collective-permute-start | bytes 1032200 | tf_op jit(solution)/shard_map/ppermute | solution.py:170

commit v7 on v6

--- a/solution.py
+++ b/solution.py
@@ -230,9 +230,10 @@
         jnp.concatenate(
             [after(gate_weight[0], got)[at : at + HALF], up_weight[0][at : at + HALF]], axis=0
         )
-        for at, got in ((0, other), (HALF, other))
+        for at, got in ((0, sent), (HALF, other))
     ]
     owns[0] = jnp.concatenate([owns[0], down_weight[0][:, : STEPS[0]]], axis=1)
+    owns[0] = after(owns[0], other)
     nears = [along(own, NEXT) for own in owns]
 
     pick, other_rest, mix_other, mix_other_rest = slots(other_routes, 1)

time: 434 us -> 424 us (0.977)
    ppermute x4, waiting for transfers between devices: 20.9 us -> 14.7 us  [pair_exchange(): return lax.ppermute(value, ('zh', 'zl'), PAIR)]
  transfers between devices with their start and end apart: 30 -> 30, of which waited for: 17 -> 17; matrix products, arithmetic and copies ran while one was open for 9% -> 10% of each run, Pallas kernels for 12% -> 13%
where the time goes in v7:
time: 424 us; the launch traced here: 423 us
  waiting for transfers between devices  211 us (50%)
  starting transfers between devices  106 us (25%)
  Pallas kernels  53.5 us (13%)
  matrix products  21.5 us (5%)
  other arithmetic  16.9 us (4%)
  local copies, waits for them, and re-layouts  14.1 us (3%)
    all_to_all x5, waiting for transfers between devices, exchange_main(): return lax.all_to_all(parts, EXP, 0, 0, tiled=True).reshape(rows.shape)  114 us
    ppermute x19, starting transfers between devices, along(): return lax.ppermute(value, COL, pairs)  56.4 us
    all_to_all x2, waiting for transfers between devices, exchange_rest(): lax.all_to_all(parts, ('y', 'x'), 0, 0, tiled=True).reshape(rows.shape)  46.6 us
    ppermute x19, waiting for transfers between devices, along(): return lax.ppermute(value, COL, pairs)  35.7 us
    pallas_call x2, Pallas kernels, hidden_units(): pl.pallas_call(functools.partial(hidden_kernel, kinds=kinds), grid_spec=p...  33.9 us
    all_to_all x5, starting transfers between devices, exchange_main(): return lax.all_to_all(parts, EXP, 0, 0, tiled=True).reshape(rows.shape)  30.8 us
    pallas_call x3, Pallas kernels, down_rows(): pl.pallas_call(down_kernel, grid_spec=pltpu.PrefetchScalarGridSpec(num_sc...  19.5 us
    ppermute x4, waiting for transfers between devices, pair_exchange(): return lax.ppermute(value, ('zh', 'zl'), PAIR)  14.7 us
  transfers between devices with their start and end apart: 30, of which 17 were waited for; matrix products, arithmetic and copies ran while one was open for 10% of the time, Pallas kernels for 13%

profile of v7, /device:TPU:0, one launch (start us, length us, event | category | flops | bytes accessed | tf_op | source)
XLA Modules:
  0.0 422.8 jit_solution(3867716245606139682)
XLA Ops:
  1.5 2.2 fusion.6
  3.7 4.1 collective-permute-start
  9.0 4.2 convolution_convert_fusion.1
  16.6 5.5 %pad_maximum_fusion.refs_0_.own = bf16[256,8960]{1,0:T(8,128)(2,1)} fusion(bf16[256,1792]{1,0:T(8,128)(2,1)S(1)} %slice.142, bf16[128,7168]{1,0:T(8,128)(2,1)S(1)} %get-tuple-element.70, bf16[128,7168]{1,0:T(8,128)(2,1)S(1)} %slice.110), kind=kLoop, calls=%fused_computation.3 | loop fusion | flops 13762560 | bytes 9175040 | tf_op jit(solution)/shard_map/concatenate | solution.py:235
  22.1 6.6 %collective-permute-done = bf16[64,7296]{1,0:T(8,128)(2,1)S(1)} collective-permute-done((bf16[64,7296]{1,0:T(8,128)(2,1)}, bf16[64,7296]{1,0:T(8,128)(2,1)S(1)}, u32[]{:S(2)}, u32[]{:S(2)}) %collective-permute-start) | collective-permute-done | bytes 933920 | tf_op jit(solution)/shard_map/ppermute | solution.py:170
  28.7 3.4 collective-permute-start.1
  32.1 8.1 %all-to-all-start = ((bf16[32,8,7168]{2,1,0:T(8,128)(2,1)}), bf16[32,8,7168]{2,1,0:T(8,128)(2,1)}, u32[]{:S(2)}, u32[]{:S(2)}) async-start(bf16[32,8,7168]{2,1,0:T(8,128)(2,1)} %bitcast.75), calls=%async_computation | async-start | bytes 7340032 | tf_op jit(solution)/shard_map/all_to_all | solution.py:215
  42.4 2.1 pad_maximum_fusion.1.refs_2_
  44.5 3.9 collective-permute-start.4
  48.4 3.2 collective-permute-start.2
  51.6 2.8 convolution_convert_fusion
  54.5 33.4 %all-to-all-done = bf16[32,8,7168]{2,1,0:T(8,128)(2,1)} async-done(((bf16[32,8,7168]{2,1,0:T(8,128)(2,1)}), bf16[32,8,7168]{2,1,0:T(8,128)(2,1)}, u32[]{:S(2)}, u32[]{:S(2)}) %all-to-all-start) | async-done | bytes 3670048 | tf_op jit(solution)/shard_map/all_to_all | solution.py:215
  87.9 5.0 %all-to-all-start.1 = ((bf16[32,8,7168]{2,1,0:T(8,128)(2,1)}), bf16[32,8,7168]{2,1,0:T(8,128)(2,1)}, u32[]{:S(2)}, u32[]{:S(2)}) async-start(bf16[32,8,7168]{2,1,0:T(8,128)(2,1)} %bitcast.76), calls=%async_computation.1 | async-start | bytes 7340032 | tf_op jit(solution)/shard_map/all_to_all | solution.py:215
  92.9 2.7 collective-permute-start.8
  97.2 2.0 convolution_convert_fusion.2
  99.2 41.3 %all-to-all-done.1 = bf16[32,8,7168]{2,1,0:T(8,128)(2,1)} async-done(((bf16[32,8,7168]{2,1,0:T(8,128)(2,1)}), bf16[32,8,7168]{2,1,0:T(8,128)(2,1)}, u32[]{:S(2)}, u32[]{:S(2)}) %all-to-all-start.1) | async-done | bytes 3670048 | tf_op jit(solution)/shard_map/all_to_all | solution.py:215
  140.5 3.7 all-to-all-start.2
  144.4 26.3 %all-to-all-done.2 = bf16[16,8,7168]{2,1,0:T(8,128)(2,1)S(1)} async-done(((bf16[16,8,7168]{2,1,0:T(8,128)(2,1)}), bf16[16,8,7168]{2,1,0:T(8,128)(2,1)S(1)}, u32[]{:S(2)}, u32[]{:S(2)}) %all-to-all-start.2) | async-done | bytes 1835040 | tf_op jit(solution)/shard_map/all_to_all | solution.py:219
  172.0 5.8 %collective-permute-done.5.refs_5_ = bf16[256,7168]{1,0:T(8,128)(2,1)} collective-permute-done((bf16[256,7168]{1,0:T(8,128)(2,1)}, bf16[256,7168]{1,0:T(8,128)(2,1)}, u32[]{:S(2)}, u32[]{:S(2)}) %collective-permute-start.5) | collective-permute-done | bytes 3670048 | tf_op jit(solution)/shard_map/ppermute | solution.py:35
  177.7 15.0 %collective-permute-start.7 = (bf16[256,7168]{1,0:T(8,128)(2,1)}, bf16[256,7168]{1,0:T(8,128)(2,1)}, u32[]{:S(2)}, u32[]{:S(2)}) collective-permute-start(bf16[256,7168]{1,0:T(8,128)(2,1)} %collective-permute-done.5.refs_5_), channel_id=1, source_target_pairs={{0,4},{4,0},{1,5},{5,1},{2,6},{6,2},{3,7},{7,3},{8,12},{12,8},{9,1... | collective-permute-start | bytes 11010056 | tf_op jit(solution)/shard_map/ppermute | solution.py:35
  192.7 2.4 collective-permute-start.10
  195.2 8.2 %collective-permute-done.7.refs_7_ = bf16[256,7168]{1,0:T(8,128)(2,1)} collective-permute-done((bf16[256,7168]{1,0:T(8,128)(2,1)}, bf16[256,7168]{1,0:T(8,128)(2,1)}, u32[]{:S(2)}, u32[]{:S(2)}) %collective-permute-start.7) | collective-permute-done | bytes 3670048 | tf_op jit(solution)/shard_map/ppermute | solution.py:35
  203.3 27.0 %shard_map.64.first = bf16[640,896]{1,0:T(8,128)(2,1)S(1)} custom-call(s32[1]{0:T(128)} %bitcast.4.flag, bf16[256,7168]{1,0:T(8,128)(2,1)} %bitcast.6.mine, bf16[256,7168]{1,0:T(8,128)(2,1)} %bitcast.13.theirs, bf16[128,7168]{1,0:T(8,128)(2,1)S(1)} %bitcast.73, bf16[256,8960]{1,0:T(8,128)(2,1)} %pad_maximum_fusion.refs_0_.own, ...), custom_call_target="tpu_custom_call" | custom-call | flops 1 | bytes 1 | tf_op jit(solution)/shard_map/pallas_call | solution.py:95
  231.6 3.5 fusion.41
  237.2 9.0 %collective-permute-done.11.refs_0_ = bf16[256,7168]{1,0:T(8,128)(2,1)S(1)} collective-permute-done((bf16[256,7168]{1,0:T(8,128)(2,1)}, bf16[256,7168]{1,0:T(8,128)(2,1)S(1)}, u32[]{:S(2)}, u32[]{:S(2)}) %collective-permute-start.11) | collective-permute-done | bytes 3670048 | tf_op jit(solution)/shard_map/ppermute | solution.py:35
  248.0 7.0 %shard_map.65.last = bf16[640,128]{1,0:T(8,128)(2,1)S(1)} custom-call(s32[1]{0:T(128)} %bitcast.4.flag, bf16[256,7168]{1,0:T(8,128)(2,1)} %bitcast.6.mine, bf16[256,7168]{1,0:T(8,128)(2,1)} %bitcast.13.theirs, bf16[128,7168]{1,0:T(8,128)(2,1)S(1)} %bitcast.74, bf16[256,7168]{1,0:T(8,128)(2,1)} %copy-done.8, bf16[256,7168]{1,0:T(8,128)(2,1)} %collective-permute-done.10.refs_1_), custom_call_target="tpu_custom_call" | custom-call | flops 1 | bytes 1 | tf_op jit(solution)/shard_map/pallas_call | solution.py:95
  254.9 5.8 %shard_map.66 = (bf16[32,16,1792]{2,1,0:T(8,128)(2,1)}, bf16[128,1792]{1,0:T(8,128)(2,1)S(1)}) custom-call(s32[1]{0:T(128)} %bitcast.4.flag, bf16[640,896]{1,0:T(8,128)(2,1)S(1)} %shard_map.64.first, bf16[640,128]{1,0:T(8,128)(2,1)S(1)} %shard_map.65.last, bf16[256,8960]{1,0:T(8,128)(2,1)} %pad_maximum_fusion.refs_0_.own, ...), custom_call_target="tpu_custom_call" | custom-call | flops 2348810240 | bytes 7274496 | tf_op jit(solution)/shard_map/pallas_call | solution.py:140
  260.8 8.9 %all-to-all-start.3 = ((bf16[32,16,1792]{2,1,0:T(8,128)(2,1)}), bf16[32,16,1792]{2,1,0:T(8,128)(2,1)}, u32[]{:S(2)}, u32[]{:S(2)}) async-start(bf16[32,16,1792]{2,1,0:T(8,128)(2,1)} %get-tuple-element.48), calls=%async_computation.3 | async-start | bytes 3670016 | tf_op jit(solution)/shard_map/all_to_all | solution.py:215
  269.7 8.4 %collective-permute-start.13 = (bf16[256,2688]{1,0:T(8,128)(2,1)}, bf16[256,2688]{1,0:T(8,128)(2,1)S(1)}, u32[]{:S(2)}, u32[]{:S(2)}) collective-permute-start(bf16[256,2688]{1,0:T(8,128)(2,1)} %collective-permute-done.12.near), channel_id=1, source_target_pairs={{0,4},{4,0},{1,5},{5,1},{2,6},{6,2},{3,7},{7,3},{8,12},{12,8},{9,1... | collective-permute-start | bytes 4128776 | tf_op jit(solution)/shard_map/ppermute | solution.py:35
  281.2 2.1 collective-permute-done.15.brought
  283.3 6.6 %shard_map.67 = (bf16[32,16,2688]{2,1,0:T(8,128)(2,1)S(1)}, bf16[128,2688]{1,0:T(8,128)(2,1)S(1)}) custom-call(s32[1]{0:T(128)} %bitcast.4.flag, bf16[640,896]{1,0:T(8,128)(2,1)S(1)} %shard_map.64.first, bf16[640,128]{1,0:T(8,128)(2,1)S(1)} %shard_map.65.last, bf16[256,7168]{1,0:T(8,128)(2,1)} %bitcast.7.own, ...), custom_call_target="tpu_custom_call" | custom-call | flops 3523215360 | bytes 10256384 | tf_op jit(solution)/shard_map/pallas_call | solution.py:140
  292.3 4.3 %all-to-all-done.3 = bf16[32,16,1792]{2,1,0:T(8,128)(2,1)} async-done(((bf16[32,16,1792]{2,1,0:T(8,128)(2,1)}), bf16[32,16,1792]{2,1,0:T(8,128)(2,1)}, u32[]{:S(2)}, u32[]{:S(2)}) %all-to-all-start.3) | async-done | bytes 1835040 | tf_op jit(solution)/shard_map/all_to_all | solution.py:215
  296.6 4.8 %all-to-all-start.4 = ((bf16[32,16,2688]{2,1,0:T(8,128)(2,1)}), bf16[32,16,2688]{2,1,0:T(8,128)(2,1)}, u32[]{:S(2)}, u32[]{:S(2)}) async-start(bf16[32,16,2688]{2,1,0:T(8,128)(2,1)} %copy-done), calls=%async_computation.4 | async-start | bytes 5505024 | tf_op jit(solution)/shard_map/all_to_all | solution.py:215
  301.4 7.1 %collective-permute-done.16.near = bf16[256,2688]{1,0:T(8,128)(2,1)S(1)} collective-permute-done((bf16[256,2688]{1,0:T(8,128)(2,1)}, bf16[256,2688]{1,0:T(8,128)(2,1)S(1)}, u32[]{:S(2)}, u32[]{:S(2)}) %collective-permute-start.16) | collective-permute-done | bytes 1376288 | tf_op jit(solution)/shard_map/ppermute | solution.py:35
  308.5 6.5 %collective-permute-start.17 = (bf16[256,2688]{1,0:T(8,128)(2,1)S(1)}, bf16[256,2688]{1,0:T(8,128)(2,1)S(1)}, u32[]{:S(2)}, u32[]{:S(2)}) collective-permute-start(bf16[256,2688]{1,0:T(8,128)(2,1)S(1)} %collective-permute-done.16.near), channel_id=1, source_target_pairs={{0,4},{4,0},{1,5},{5,1},{2,6},{6,2},{3,7},{7,3},{8,12},{12,8},{9,1... | collective-permute-start | bytes 4128776 | tf_op jit(solution)/shard_map/ppermute | solution.py:35
  317.7 2.5 collective-permute-done.19.brought
  320.2 7.1 %shard_map.68 = (bf16[32,16,2688]{2,1,0:T(8,128)(2,1)}, bf16[128,2688]{1,0:T(8,128)(2,1)S(1)}) custom-call(s32[1]{0:T(128)} %bitcast.4.flag, bf16[640,896]{1,0:T(8,128)(2,1)S(1)} %shard_map.64.first, bf16[640,128]{1,0:T(8,128)(2,1)S(1)} %shard_map.65.last, bf16[256,7168]{1,0:T(8,128)(2,1)} %bitcast.7.own, bf16[256,7168]{1,0:T(8,128)(2,1)} %collective-permute-done.2.copied, ...), custom_call_target="tpu_custom_call" | custom-call | flops 3523215360 | bytes 10256384 | tf_op jit(solution)/shard_map/pallas_call | solution.py:140
  328.8 10.1 %all-to-all-done.4 = bf16[32,16,2688]{2,1,0:T(8,128)(2,1)} async-done(((bf16[32,16,2688]{2,1,0:T(8,128)(2,1)}), bf16[32,16,2688]{2,1,0:T(8,128)(2,1)}, u32[]{:S(2)}, u32[]{:S(2)}) %all-to-all-start.4) | async-done | bytes 2752544 | tf_op jit(solution)/shard_map/all_to_all | solution.py:215
  338.9 4.4 %all-to-all-start.5 = ((bf16[16,8,7168]{2,1,0:T(8,128)(2,1)}), bf16[16,8,7168]{2,1,0:T(8,128)(2,1)}, u32[]{:S(2)}, u32[]{:S(2)}) async-start(bf16[16,8,7168]{2,1,0:T(8,128)(2,1)} %bitcast.32), calls=%async_computation.5 | async-start | bytes 3670016 | tf_op jit(solution)/shard_map/all_to_all | solution.py:219
  343.8 4.3 %fusion.16 = f32[256,2688]{1,0:T(8,128)} fusion(bf16[512,2688]{1,0:T(8,128)(2,1)} %bitcast.31, bf16[128,512]{0,1:T(8,128)(2,1)S(1)} %get-tuple-element.72, bf16[128,512]{0,1:T(8,128)(2,1)S(1)} %get-tuple-element.71), kind=kOutput, calls=%fused_computation.56 | convolution fusion | flops 705167360 | bytes 5767168 | tf_op jit(solution)/shard_map/dot_general | solution.py:287
  348.1 20.2 %all-to-all-done.5 = bf16[16,8,7168]{2,1,0:T(8,128)(2,1)} async-done(((bf16[16,8,7168]{2,1,0:T(8,128)(2,1)}), bf16[16,8,7168]{2,1,0:T(8,128)(2,1)}, u32[]{:S(2)}, u32[]{:S(2)}) %all-to-all-start.5) | async-done | bytes 1835040 | tf_op jit(solution)/shard_map/all_to_all | solution.py:219
  368.4 4.1 all-to-all-start.6
  373.9 2.2 convolution_add_fusion.2
  376.2 2.3 collective-permute-start.20
  382.7 2.5 collective-permute-done.20
  385.2 24.7 %all-to-all-done.6 = bf16[32,16,2688]{2,1,0:T(8,128)(2,1)S(1)} async-done(((bf16[32,16,2688]{2,1,0:T(8,128)(2,1)}), bf16[32,16,2688]{2,1,0:T(8,128)(2,1)S(1)}, u32[]{:S(2)}, u32[]{:S(2)}) %all-to-all-start.6) | async-done | bytes 2752544 | tf_op jit(solution)/shard_map/all_to_all | solution.py:215
  412.7 2.3 collective-permute-start.22
  416.1 5.6 %collective-permute-done.22 = bf16[64,2688]{1,0:T(8,128)(2,1)S(1)} collective-permute-done((bf16[64,2688]{1,0:T(8,128)(2,1)S(1)}, bf16[64,2688]{1,0:T(8,128)(2,1)S(1)}, u32[]{:S(2)}, u32[]{:S(2)}) %collective-permute-start.22) | collective-permute-done | bytes 344096 | tf_op jit(solution)/shard_map/ppermute | solution.py:170
  (101 shorter events, 37.2 us)
Async XLA Ops:
  3.7 25.0 %collective-permute-start = (bf16[64,7296]{1,0:T(8,128)(2,1)}, bf16[64,7296]{1,0:T(8,128)(2,1)S(1)}, u32[]{:S(2)}, u32[]{:S(2)}) collective-permute-start(bf16[64,7296]{1,0:T(8,128)(2,1)} %fusion.6), channel_id=1, source_target_pairs={{0,3},{3,0},{1,2},{2,1},{4,7},{7,4},{5,6},{6,5},{8,11},{11,8},{9,1... | collective-permute-start | bytes 2801672 | tf_op jit(solution)/shard_map/ppermute | solution.py:170
  8.9 5.5 %copy-start.9 = (bf16[1,256,7168]{2,1,0:T(8,128)(2,1)S(1)}, bf16[1,256,7168]{2,1,0:T(8,128)(2,1)}, u32[]{:S(2)}) copy-start(bf16[1,256,7168]{2,1,0:T(8,128)(2,1)} %param.10) | copy-start | bytes 11010052
  14.4 2.0 copy-start.10
  28.7 22.9 %copy-start.7 = (bf16[64,7296]{1,0:T(8,128)(2,1)}, bf16[64,7296]{1,0:T(8,128)(2,1)S(1)}, u32[]{:S(2)}) copy-start(bf16[64,7296]{1,0:T(8,128)(2,1)S(1)} %collective-permute-done) | copy-start | bytes 2801668
  28.7 19.7 %collective-permute-start.1 = (bf16[256,8960]{1,0:T(8,128)(2,1)}, bf16[256,8960]{1,0:T(8,128)(2,1)}, u32[]{:S(2)}, u32[]{:S(2)}) collective-permute-start(bf16[256,8960]{1,0:T(8,128)(2,1)} %pad_maximum_fusion.refs_0_.own), channel_id=1, source_target_pairs={{0,4},{1,5},{6,2},{7,3},{8,12},{9,13},{14,10},{15,11},{16,20},{17,... | collective-permute-start | bytes 13762568 | tf_op jit(solution)/shard_map/ppermute | solution.py:35
  32.1 55.8 %collective-permute-start.3 = (bf16[256,8960]{1,0:T(8,128)(2,1)}, bf16[256,8960]{1,0:T(8,128)(2,1)}, u32[]{:S(2)}, u32[]{:S(2)}) collective-permute-start(bf16[256,8960]{1,0:T(8,128)(2,1)} %pad_maximum_fusion.refs_0_.own), channel_id=1, source_target_pairs={{0,1},{1,0},{6,7},{7,6},{4,3},{3,4},{5,2},{2,5},{8,9},{9,8},{14,15... | collective-permute-start | bytes 13762568 | tf_op jit(solution)/shard_map/ppermute | solution.py:35
  32.1 55.7 %all-to-all-start = ((bf16[32,8,7168]{2,1,0:T(8,128)(2,1)}), bf16[32,8,7168]{2,1,0:T(8,128)(2,1)}, u32[]{:S(2)}, u32[]{:S(2)}) async-start(bf16[32,8,7168]{2,1,0:T(8,128)(2,1)} %bitcast.75), calls=%async_computation | async-start | bytes 7340032 | tf_op jit(solution)/shard_map/all_to_all | solution.py:215
  44.5 54.8 %collective-permute-start.4 = (bf16[256,7168]{1,0:T(8,128)(2,1)}, bf16[256,7168]{1,0:T(8,128)(2,1)}, u32[]{:S(2)}, u32[]{:S(2)}) collective-permute-start(bf16[256,7168]{1,0:T(8,128)(2,1)} %pad_maximum_fusion.1.refs_2_), channel_id=1, source_target_pairs={{0,4},{1,5},{6,2},{7,3},{8,12},{9,13},{14,10},{15,11},{16,20},{17,... | collective-permute-start | bytes 11010056 | tf_op jit(solution)/shard_map/ppermute | solution.py:35
  48.4 92.1 %collective-permute-start.2 = (bf16[256,7168]{1,0:T(8,128)(2,1)}, bf16[256,7168]{1,0:T(8,128)(2,1)}, u32[]{:S(2)}, u32[]{:S(2)}) collective-permute-start(bf16[256,7168]{1,0:T(8,128)(2,1)} %bitcast.7.own), channel_id=1, source_target_pairs={{0,4},{1,5},{6,2},{7,3},{8,12},{9,13},{14,10},{15,11},{16,20},{17,... | collective-permute-start | bytes 11010056 | tf_op jit(solution)/shard_map/ppermute | solution.py:35
  87.9 9.3 %copy-start.4 = (bf16[64,7168]{1,0:T(8,128)(2,1)S(1)}, bf16[64,7168]{1,0:T(8,128)(2,1)}, u32[]{:S(2)}) copy-start(bf16[64,7168]{1,0:T(8,128)(2,1)} %param.6) | copy-start | bytes 2752516
  87.9 9.3 %slice-start = ((bf16[64,7296]{1,0:T(8,128)(2,1)}), bf16[64,7168]{1,0:T(8,128)(2,1)S(1)}, s32[]{:S(2)}) async-start(bf16[64,7296]{1,0:T(8,128)(2,1)} %copy-done.7), calls=%async_computation.7 | async-start | bytes 1835008 | tf_op jit(solution)/shard_map/slice | solution.py:225
  87.9 52.6 %all-to-all-start.1 = ((bf16[32,8,7168]{2,1,0:T(8,128)(2,1)}), bf16[32,8,7168]{2,1,0:T(8,128)(2,1)}, u32[]{:S(2)}, u32[]{:S(2)}) async-start(bf16[32,8,7168]{2,1,0:T(8,128)(2,1)} %bitcast.76), calls=%async_computation.1 | async-start | bytes 7340032 | tf_op jit(solution)/shard_map/all_to_all | solution.py:215
  92.9 51.5 %collective-permute-start.8 = (bf16[256,8960]{1,0:T(8,128)(2,1)}, bf16[256,8960]{1,0:T(8,128)(2,1)}, u32[]{:S(2)}, u32[]{:S(2)}) collective-permute-start(bf16[256,8960]{1,0:T(8,128)(2,1)} %pad_maximum_fusion.refs_0_.own), channel_id=1, source_target_pairs={{5,3},{3,5},{4,2},{2,4},{13,11},{11,13},{12,10},{10,12},{21,19},{1... | collective-permute-start | bytes 13762568 | tf_op jit(solution)/shard_map/ppermute | solution.py:35
  95.6 82.1 %collective-permute-start.5 = (bf16[256,7168]{1,0:T(8,128)(2,1)}, bf16[256,7168]{1,0:T(8,128)(2,1)}, u32[]{:S(2)}, u32[]{:S(2)}) collective-permute-start(bf16[256,7168]{1,0:T(8,128)(2,1)} %pad_maximum_fusion.1.refs_2_), channel_id=1, source_target_pairs={{0,1},{1,0},{6,7},{7,6},{4,3},{3,4},{5,2},{2,5},{8,9},{9,8},{14,15... | collective-permute-start | bytes 11010056 | tf_op jit(solution)/shard_map/ppermute | solution.py:35
  140.5 30.2 %all-to-all-start.2 = ((bf16[16,8,7168]{2,1,0:T(8,128)(2,1)}), bf16[16,8,7168]{2,1,0:T(8,128)(2,1)S(1)}, u32[]{:S(2)}, u32[]{:S(2)}) async-start(bf16[16,8,7168]{2,1,0:T(8,128)(2,1)} %bitcast.78), calls=%async_computation.2 | async-start | bytes 3670016 | tf_op jit(solution)/shard_map/all_to_all | solution.py:219
  144.3 50.9 %collective-permute-start.6 = (bf16[256,8960]{1,0:T(8,128)(2,1)}, bf16[256,8960]{1,0:T(8,128)(2,1)}, u32[]{:S(2)}, u32[]{:S(2)}) collective-permute-start(bf16[256,8960]{1,0:T(8,128)(2,1)} %collective-permute-done.3.refs_4_.near), channel_id=1, source_target_pairs={{0,4},{4,0},{1,5},{5,1},{2,6},{6,2},{3,7},{7,3},{8,12},{12,8},{9,1... | collective-permute-start | bytes 13762568 | tf_op jit(solution)/shard_map/ppermute | solution.py:35
  170.7 32.6 %collective-permute-start.9 = (bf16[256,8960]{1,0:T(8,128)(2,1)}, bf16[256,8960]{1,0:T(8,128)(2,1)}, u32[]{:S(2)}, u32[]{:S(2)}) collective-permute-start(bf16[256,8960]{1,0:T(8,128)(2,1)} %collective-permute-done.8.refs_9_.far), channel_id=1, source_target_pairs={{4,0},{5,1},{2,6},{3,7},{12,8},{13,9},{10,14},{11,15},{20,16},{21,... | collective-permute-start | bytes 13762568 | tf_op jit(solution)/shard_map/ppermute | solution.py:35
  177.7 25.6 %collective-permute-start.7 = (bf16[256,7168]{1,0:T(8,128)(2,1)}, bf16[256,7168]{1,0:T(8,128)(2,1)}, u32[]{:S(2)}, u32[]{:S(2)}) collective-permute-start(bf16[256,7168]{1,0:T(8,128)(2,1)} %collective-permute-done.5.refs_5_), channel_id=1, source_target_pairs={{0,4},{4,0},{1,5},{5,1},{2,6},{6,2},{3,7},{7,3},{8,12},{12,8},{9,1... | collective-permute-start | bytes 11010056 | tf_op jit(solution)/shard_map/ppermute | solution.py:35
  192.7 37.6 %collective-permute-start.10 = (bf16[256,7168]{1,0:T(8,128)(2,1)}, bf16[256,7168]{1,0:T(8,128)(2,1)}, u32[]{:S(2)}, u32[]{:S(2)}) collective-permute-start(bf16[256,7168]{1,0:T(8,128)(2,1)} %pad_maximum_fusion.1.refs_2_), channel_id=1, source_target_pairs={{5,3},{3,5},{4,2},{2,4},{13,11},{11,13},{12,10},{10,12},{21,19},{1... | collective-permute-start | bytes 11010056 | tf_op jit(solution)/shard_map/ppermute | solution.py:35
  230.3 15.8 %collective-permute-start.11 = (bf16[256,7168]{1,0:T(8,128)(2,1)}, bf16[256,7168]{1,0:T(8,128)(2,1)S(1)}, u32[]{:S(2)}, u32[]{:S(2)}) collective-permute-start(bf16[256,7168]{1,0:T(8,128)(2,1)} %collective-permute-done.10.refs_1_), channel_id=1, source_target_pairs={{4,0},{5,1},{2,6},{3,7},{12,8},{13,9},{10,14},{11,15},{20,16},{21,... | collective-permute-start | bytes 11010056 | tf_op jit(solution)/shard_map/ppermute | solution.py:35
  235.1 34.5 %collective-permute-start.12 = (bf16[256,2688]{1,0:T(8,128)(2,1)}, bf16[256,2688]{1,0:T(8,128)(2,1)}, u32[]{:S(2)}, u32[]{:S(2)}) collective-permute-start(bf16[256,2688]{1,0:T(8,128)(2,1)} %get-tuple-element.50), channel_id=1, source_target_pairs={{0,1},{1,0},{6,7},{7,6},{4,3},{3,4},{5,2},{2,5},{8,9},{9,8},{14,15... | collective-permute-start | bytes 4128776 | tf_op jit(solution)/shard_map/ppermute | solution.py:35
  235.4 42.6 %collective-permute-start.14 = (bf16[256,2688]{1,0:T(8,128)(2,1)}, bf16[256,2688]{1,0:T(8,128)(2,1)}, u32[]{:S(2)}, u32[]{:S(2)}) collective-permute-start(bf16[256,2688]{1,0:T(8,128)(2,1)} %get-tuple-element.50), channel_id=1, source_target_pairs={{5,3},{3,5},{4,2},{2,4},{13,11},{11,13},{12,10},{10,12},{21,19},{1... | collective-permute-start | bytes 4128776 | tf_op jit(solution)/shard_map/ppermute | solution.py:35
  246.1 1.8 copy-start.8
  260.8 35.8 %all-to-all-start.3 = ((bf16[32,16,1792]{2,1,0:T(8,128)(2,1)}), bf16[32,16,1792]{2,1,0:T(8,128)(2,1)}, u32[]{:S(2)}, u32[]{:S(2)}) async-start(bf16[32,16,1792]{2,1,0:T(8,128)(2,1)} %get-tuple-element.48), calls=%async_computation.3 | async-start | bytes 3670016 | tf_op jit(solution)/shard_map/all_to_all | solution.py:215
  269.7 11.6 %collective-permute-start.13 = (bf16[256,2688]{1,0:T(8,128)(2,1)}, bf16[256,2688]{1,0:T(8,128)(2,1)S(1)}, u32[]{:S(2)}, u32[]{:S(2)}) collective-permute-start(bf16[256,2688]{1,0:T(8,128)(2,1)} %collective-permute-done.12.near), channel_id=1, source_target_pairs={{0,4},{4,0},{1,5},{5,1},{2,6},{6,2},{3,7},{7,3},{8,12},{12,8},{9,1... | collective-permute-start | bytes 4128776 | tf_op jit(solution)/shard_map/ppermute | solution.py:35
  278.1 5.2 %collective-permute-start.15 = (bf16[256,2688]{1,0:T(8,128)(2,1)}, bf16[256,2688]{1,0:T(8,128)(2,1)S(1)}, u32[]{:S(2)}, u32[]{:S(2)}) collective-permute-start(bf16[256,2688]{1,0:T(8,128)(2,1)} %collective-permute-done.14.far), channel_id=1, source_target_pairs={{4,0},{5,1},{2,6},{3,7},{12,8},{13,9},{10,14},{11,15},{20,16},{21,... | collective-permute-start | bytes 4128776 | tf_op jit(solution)/shard_map/ppermute | solution.py:35
  279.4 29.1 %collective-permute-start.16 = (bf16[256,2688]{1,0:T(8,128)(2,1)}, bf16[256,2688]{1,0:T(8,128)(2,1)S(1)}, u32[]{:S(2)}, u32[]{:S(2)}) collective-permute-start(bf16[256,2688]{1,0:T(8,128)(2,1)} %get-tuple-element.54), channel_id=1, source_target_pairs={{0,1},{1,0},{6,7},{7,6},{4,3},{3,4},{5,2},{2,5},{8,9},{9,8},{14,15... | collective-permute-start | bytes 4128776 | tf_op jit(solution)/shard_map/ppermute | solution.py:35
  279.5 35.5 %collective-permute-start.18 = (bf16[256,2688]{1,0:T(8,128)(2,1)}, bf16[256,2688]{1,0:T(8,128)(2,1)}, u32[]{:S(2)}, u32[]{:S(2)}) collective-permute-start(bf16[256,2688]{1,0:T(8,128)(2,1)} %get-tuple-element.54), channel_id=1, source_target_pairs={{5,3},{3,5},{4,2},{2,4},{13,11},{11,13},{12,10},{10,12},{21,19},{1... | collective-permute-start | bytes 4128776 | tf_op jit(solution)/shard_map/ppermute | solution.py:35
  289.9 1.6 copy-start
  291.5 0.8 copy-start.1
  296.6 42.3 %all-to-all-start.4 = ((bf16[32,16,2688]{2,1,0:T(8,128)(2,1)}), bf16[32,16,2688]{2,1,0:T(8,128)(2,1)}, u32[]{:S(2)}, u32[]{:S(2)}) async-start(bf16[32,16,2688]{2,1,0:T(8,128)(2,1)} %copy-done), calls=%async_computation.4 | async-start | bytes 5505024 | tf_op jit(solution)/shard_map/all_to_all | solution.py:215
  308.5 9.3 %collective-permute-start.17 = (bf16[256,2688]{1,0:T(8,128)(2,1)S(1)}, bf16[256,2688]{1,0:T(8,128)(2,1)S(1)}, u32[]{:S(2)}, u32[]{:S(2)}) collective-permute-start(bf16[256,2688]{1,0:T(8,128)(2,1)S(1)} %collective-permute-done.16.near), channel_id=1, source_target_pairs={{0,4},{4,0},{1,5},{5,1},{2,6},{6,2},{3,7},{7,3},{8,12},{12,8},{9,1... | collective-permute-start | bytes 4128776 | tf_op jit(solution)/shard_map/ppermute | solution.py:35
  315.0 5.2 %collective-permute-start.19 = (bf16[256,2688]{1,0:T(8,128)(2,1)}, bf16[256,2688]{1,0:T(8,128)(2,1)S(1)}, u32[]{:S(2)}, u32[]{:S(2)}) collective-permute-start(bf16[256,2688]{1,0:T(8,128)(2,1)} %collective-permute-done.18.far), channel_id=1, source_target_pairs={{4,0},{5,1},{2,6},{3,7},{12,8},{13,9},{10,14},{11,15},{20,16},{21,... | collective-permute-start | bytes 4128776 | tf_op jit(solution)/shard_map/ppermute | solution.py:35
  316.5 10.8 %copy-start.2 = (bf16[128,2688]{1,0:T(8,128)(2,1)S(1)}, bf16[128,2688]{1,0:T(8,128)(2,1)}, u32[]{:S(2)}) copy-start(bf16[128,2688]{1,0:T(8,128)(2,1)} %copy-done.1) | copy-start | bytes 2064388
  338.9 29.5 %all-to-all-start.5 = ((bf16[16,8,7168]{2,1,0:T(8,128)(2,1)}), bf16[16,8,7168]{2,1,0:T(8,128)(2,1)}, u32[]{:S(2)}, u32[]{:S(2)}) async-start(bf16[16,8,7168]{2,1,0:T(8,128)(2,1)} %bitcast.32), calls=%async_computation.5 | async-start | bytes 3670016 | tf_op jit(solution)/shard_map/all_to_all | solution.py:219
  368.4 41.6 %all-to-all-start.6 = ((bf16[32,16,2688]{2,1,0:T(8,128)(2,1)}), bf16[32,16,2688]{2,1,0:T(8,128)(2,1)S(1)}, u32[]{:S(2)}, u32[]{:S(2)}) async-start(bf16[32,16,2688]{2,1,0:T(8,128)(2,1)} %bitcast.35), calls=%async_computation.6 | async-start | bytes 5505024 | tf_op jit(solution)/shard_map/all_to_all | solution.py:215
  376.1 2.4 copy-start.3
  376.2 9.0 %collective-permute-start.20 = (bf16[64,1792]{1,0:T(8,128)(2,1)S(1)}, bf16[64,1792]{1,0:T(8,128)(2,1)S(1)}, u32[]{:S(2)}, u32[]{:S(2)}) collective-permute-start(bf16[64,1792]{1,0:T(8,128)(2,1)S(1)} %slice.193), channel_id=1, source_target_pairs={{0,3},{3,0},{1,2},{2,1},{4,7},{7,4},{5,6},{6,5},{8,11},{11,8},{9,1... | collective-permute-start | bytes 688136 | tf_op jit(solution)/shard_map/ppermute | solution.py:170
  380.3 4.9 %copy-start.5 = (f32[128,2688]{1,0:T(8,128)}, f32[128,2688]{1,0:T(8,128)S(1)}, u32[]{:S(2)}) copy-start(f32[128,2688]{1,0:T(8,128)S(1)} %slice_add_fusion.1) | copy-start | bytes 4128772
  381.2 33.9 %collective-permute-start.21 = (bf16[64,2688]{1,0:T(8,128)(2,1)}, bf16[64,2688]{1,0:T(8,128)(2,1)}, u32[]{:S(2)}, u32[]{:S(2)}) collective-permute-start(bf16[64,2688]{1,0:T(8,128)(2,1)} %slice.192), channel_id=1, source_target_pairs={{0,3},{3,0},{1,2},{2,1},{4,7},{7,4},{5,6},{6,5},{8,11},{11,8},{9,1... | collective-permute-start | bytes 1032200 | tf_op jit(solution)/shard_map/ppermute | solution.py:170
  412.5 2.5 copy-start.6
  412.7 9.0 %collective-permute-start.22 = (bf16[64,2688]{1,0:T(8,128)(2,1)S(1)}, bf16[64,2688]{1,0:T(8,128)(2,1)S(1)}, u32[]{:S(2)}, u32[]{:S(2)}) collective-permute-start(bf16[64,2688]{1,0:T(8,128)(2,1)S(1)} %slice.191), channel_id=1, source_target_pairs={{0,3},{3,0},{1,2},{2,1},{4,7},{7,4},{5,6},{6,5},{8,11},{11,8},{9,1... | collective-permute-start | bytes 1032200 | tf_op jit(solution)/shard_map/ppermute | solution.py:170
